TPU v7x, 512 devices: a whole 4x8x8 slice. The times are simulated.
512 devices in a mesh: rep: 8 (over z), ep: 64 (over y, x, core).
Axes of the slice: x: 4, y: 8, z: 8, core: 2. Of those that a mesh axis runs over, the one named last changes fastest.
Arguments:
- train_acts: bfloat16 [8, 64, 320, 2048], P('rep', 'ep'), may hold values from -6 to 6
- train_cotan: bfloat16 [8, 64, 320, 384], P('rep', 'ep'), may hold values from -0.59765625 to 0.59765625
- weight: bfloat16 [8, 64, 256, 768], P('rep', 'ep'), may hold values from -3 to 3
- moment_one: float32 [8, 64, 256, 768], P('rep', 'ep'), may hold values from -0.006 to 0.006
- moment_two: float32 [8, 64, 256, 768], P('rep', 'ep'), may hold values from 1e-06 to 1e-05
- tokens: bfloat16 [4096, 2, 2048], P('ep', None, 'rep'), may hold values from -6 to 6
- routes: int32 [4096, 8], P('ep'), may hold values from 0 to 31, all different within a row; in each aligned block of 64 rows (0 to 63, 64 to 127, ...) at most 20 rows name the same one
- gate_weights: bfloat16 [4096, 8], P('ep'), may hold values from 0.099609375 to 1
- train_place: int32 [32], replicated, may hold values from 0 to 31, each once
- serve_place: int32 [64], replicated, may hold values from 0 to 31, as said below
Outputs:
- serve_weight: bfloat16 [8, 64, 2, 256, 768], P('rep', 'ep')
- expert_act: bfloat16 [64, 1280, 768], P('ep', None, 'rep')
Inputs may be any that keep to these rules, and one draw needn't show every extreme that they name: `routes`: in each aligned block of 64 rows (the rows of one device) no expert is named by more than 20 rows, a bound that some block reaches. `train_place`: each expert is trained by exactly one pair. `serve_place`: every expert is served by at least one device.
All inputs are finite; a program needn't handle non-finite values.
Results may differ from a plain program's by a relative error of at most 0.024.
Values may be sent and summed in bfloat16 or wider, within the bound.
No kernel may reach another device: no remote copies, remote signals or barrier semaphores. Data moves between devices by JAX's collectives and lax.ppermute only.
A program may use at most 64 MiB of HBM per device.

v0:
```python
import math

import jax
import jax.numpy as jnp
from jax import lax
from jax.sharding import PartitionSpec as P

beta_one = 0.9
beta_two = 0.999
bias_one = 1.0 - math.exp(100.0 * math.log(0.9))
bias_two = 1.0 - math.exp(100.0 * math.log(0.999))
learn_rate = 0.5
decay_rate = 0.1
adam_eps = 1e-08


def swapped(x, axis, apart):
    return lax.ppermute(x, axis, [(i, i ^ 1 << apart) for i in range(lax.axis_size(axis))])


def body(
    train_acts,
    train_cotan,
    weight,
    moment_one,
    moment_two,
    tokens,
    routes,
    gate_weights,
    train_place,
    serve_place,
):
    ep_count = lax.axis_size("ep")
    rep_count = lax.axis_size("rep")
    acts_local = train_acts[0, 0]
    half_width = acts_local.shape[1]
    width_scale = float(2 * half_width) ** (-0.5)
    piece_rows = weight.shape[2]
    hidden_width = weight.shape[3]
    group_rows = piece_rows // ep_count
    row_count, top_count = routes.shape
    expert_count = train_place.shape[0]
    capacity = min(row_count, row_count * top_count // expert_count + max(1, row_count // 16))
    pair_count = row_count * top_count
    slot_count = ep_count * capacity
    expert_ids = jnp.arange(expert_count, dtype=jnp.int32)
    device_ids = jnp.arange(ep_count, dtype=jnp.int32)
    chosen = routes.reshape(pair_count)
    picked = (chosen[:, None] == expert_ids[None, :]).astype(jnp.int32)
    position = jnp.sum((jnp.cumsum(picked, axis=0) - 1) * picked, axis=1)
    serving_match = serve_place[None, :] == expert_ids[:, None]
    first_device = jnp.min(jnp.where(serving_match, device_ids[None, :], ep_count), axis=1)
    target = jnp.sum(picked * first_device[None, :], axis=1)
    slot_of_pair = target * capacity + position
    placing = jnp.arange(slot_count, dtype=jnp.int32)[:, None] == slot_of_pair[None, :]
    place_rows = jnp.sum(
        placing.reshape(slot_count, row_count, top_count).astype(jnp.int32), axis=2
    ).astype(jnp.bfloat16)
    send_tokens = jnp.dot(
        place_rows, tokens.reshape(row_count, -1), preferred_element_type=jnp.float32
    )
    send_tokens = send_tokens.astype(jnp.bfloat16).reshape(ep_count, capacity, -1)
    gate_row = gate_weights.reshape(1, pair_count).astype(jnp.float32)
    send_gates = (
        jnp.sum(jnp.where(placing, gate_row, 0.0), axis=1)
        .astype(jnp.bfloat16)
        .reshape(ep_count, capacity)
    )
    own_cotan = train_cotan[0, 0]
    partner_cotan = swapped(own_cotan, "ep", 0)
    is_upper = lax.axis_index("ep") % 2 == 1
    full_cotan = jnp.where(
        is_upper,
        jnp.concatenate([partner_cotan, own_cotan], axis=1),
        jnp.concatenate([own_cotan, partner_cotan], axis=1),
    )
    product = lax.dot_general(
        acts_local, full_cotan, (((0,), (0,)), ((), ())), preferred_element_type=jnp.float32
    )
    summed = lax.psum((product * width_scale).astype(jnp.bfloat16), "rep").astype(jnp.float32)
    gradient = lax.dynamic_slice_in_dim(summed, lax.axis_index("rep") * piece_rows, piece_rows, 0)
    first = beta_one * moment_one[0, 0] + (1.0 - beta_one) * gradient
    second = beta_two * moment_two[0, 0] + (1.0 - beta_two) * gradient * gradient
    weight_now = weight[0, 0].astype(jnp.float32)
    update = first / bias_one / (jnp.sqrt(second / bias_two) + adam_eps)
    new_weight = (weight_now - learn_rate * (update + decay_rate * weight_now)).astype(jnp.bfloat16)
    spread = lax.all_to_all(
        new_weight.reshape(ep_count, group_rows, hidden_width),
        "ep",
        split_axis=0,
        concat_axis=0,
        tiled=True,
    )
    block_of = 2 * jnp.sum(jnp.where(serving_match.T, train_place[None, :], 0), axis=1)
    block_order = jnp.stack([block_of, block_of + 1], axis=1).reshape(2 * ep_count)
    payload = jnp.take(spread, block_order, axis=0).reshape(ep_count, 2, group_rows, hidden_width)
    arrived, recv_tokens, recv_gates = (
        lax.all_to_all(payload, "ep", split_axis=0, concat_axis=0, tiled=True),
        lax.all_to_all(send_tokens, "ep", split_axis=0, concat_axis=0, tiled=True),
        lax.all_to_all(send_gates, "ep", split_axis=0, concat_axis=0, tiled=True),
    )
    serving = jnp.transpose(arrived, (1, 0, 2, 3)).reshape(2 * piece_rows, hidden_width)
    partial_value = (
        jnp.dot(recv_tokens.reshape(slot_count, -1), serving, preferred_element_type=jnp.float32)
        * width_scale
    )
    share_width = hidden_width // rep_count
    summed_pre = lax.psum(partial_value.astype(jnp.bfloat16), "rep").astype(jnp.float32)
    preact = lax.dynamic_slice_in_dim(
        summed_pre, lax.axis_index("rep") * share_width, share_width, 1
    )
    activation = (
        recv_gates.reshape(slot_count, 1).astype(jnp.float32) * jax.nn.silu(preact)
    ).astype(jnp.bfloat16)
    return (
        serving.reshape(1, 1, 2, piece_rows, hidden_width),
        activation.reshape(1, slot_count, share_width),
    )


def solution(mesh):
    return jax.shard_map(
        body,
        mesh=mesh,
        in_specs=(
            P("rep", "ep", None, None),
            P("rep", "ep", None, None),
            P("rep", "ep", None, None),
            P("rep", "ep", None, None),
            P("rep", "ep", None, None),
            P("ep", None, "rep"),
            P("ep", None),
            P("ep", None),
            P(),
            P(),
        ),
        out_specs=(P("rep", "ep", None, None, None), P("ep", None, "rep")),
        check_vma=False,
    )
```

profile of v0, /device:TPU:1, one launch (start us, length us, event | category | flops | bytes accessed | tf_op | source)
XLA Modules:
  0.0 315.6 jit_solution(13957998124281017588)
XLA Ops:
  7.2 0.0 copy-start
  7.2 0.0 all-reduce.3.cloned.1.call-start
  7.2 8.9 %collective-permute-start = (bf16[320,384]{1,0:T(8,128)(2,1)}, bf16[320,384]{1,0:T(8,128)(2,1)S(1)}, u32[]{:S(2)}, u32[]{:S(2)}) collective-permute-start(bf16[320,384]{1,0:T(8,128)(2,1)} %bitcast.54), channel_id=1, source_target_pairs={{0,1},{1,0},{2,3},{3,2},{4,5},{5,4},{6,7},{7,6},{8,9},{9,8},{10,11... | collective-permute-start | bytes 737288 | tf_op jit(solution)/shard_map/ppermute | solution.py:18
  16.2 1.3 collective-permute-done
  17.5 0.0 copy-done
  17.5 4.6 %fusion.1 = bf16[2048,768]{0,1:T(8,128)(2,1)} fusion(bf16[1,1,320,2048]{3,2,1,0:T(8,128)(2,1)S(1)} %copy-done, bf16[320,384]{1,0:T(8,128)(2,1)} %bitcast.55, bf16[320,384]{1,0:T(8,128)(2,1)S(1)} %collective-permute-done, pred[]{:T(512)S(6)} %eq.73), kind=kOutput, calls=%fused_computation.4 | convolution fusion | flops 1011990528 | bytes 4947969 | tf_op jit(solution)/shard_map/dot_general | solution.py:77
  22.1 0.0 all-reduce.3.cloned.1.call-update
  22.1 0.0 copy-start.4
  22.1 1.1 copy-done.2
  23.2 0.3 copy.66
  23.5 1.4 copy.67
  24.9 1.2 copy.65
  26.1 0.0 copy-done.4
  26.1 0.1 copy.71
  26.2 0.1 eq.82
  26.3 1.2 reduce-window.6
  27.4 0.2 slice_reduce_fusion
  27.7 0.0 copy-start.3
  27.7 90.8 %all-reduce.3.cloned.1.call-done = bf16[2048,768]{0,1:T(8,128)(2,1)} async-done(((bf16[2048,768]{0,1:T(8,128)(2,1)}), bf16[2048,768]{0,1:T(8,128)(2,1)}) %all-reduce.3.cloned.1.call-update) | async-done | bytes 3145744 | tf_op jit(solution)/shard_map/psum | solution.py:80
  118.5 2.4 fusion.12
  121.0 1.2 copy.68
  122.1 0.8 reshape.162
  123.0 10.5 %all-to-all-start = ((bf16[64,4,768]{2,1,0:T(4,128)(2,1)}), bf16[64,4,768]{2,1,0:T(4,128)(2,1)S(1)}, u32[]{:S(2)}, u32[]{:S(2)}) async-start(bf16[64,4,768]{2,1,0:T(4,128)(2,1)} %reshape.162), calls=%async_computation | async-start | bytes 786432 | tf_op jit(solution)/shard_map/all_to_all | solution.py:87
  133.5 0.0 copy-done.7
  133.5 0.1 select_reduce_fusion.2
  133.6 0.1 eq.75
  133.8 0.1 select_reduce_fusion.1
  133.9 0.1 add.96
  134.0 0.0 copy-done.3
  134.0 0.8 convert_reduce_fusion
  134.8 0.5 convolution_convert_fusion
  135.4 0.0 copy-start.6
  135.4 1.3 reshape.166
  136.7 11.9 %all-to-all-done = bf16[64,4,768]{2,1,0:T(4,128)(2,1)S(1)} async-done(((bf16[64,4,768]{2,1,0:T(4,128)(2,1)}), bf16[64,4,768]{2,1,0:T(4,128)(2,1)S(1)}, u32[]{:S(2)}, u32[]{:S(2)}) %all-to-all-start) | async-done | bytes 393248 | tf_op jit(solution)/shard_map/all_to_all | solution.py:87
  148.6 5.6 %all-to-all-start.3 = ((bf16[64,20,512]{2,1,0:T(8,128)(2,1)}), bf16[64,20,512]{2,1,0:T(8,128)(2,1)S(1)}, u32[]{:S(2)}, u32[]{:S(2)}) async-start(bf16[64,20,512]{2,1,0:T(8,128)(2,1)} %reshape.166), calls=%async_computation.3 | async-start | bytes 3145728 | tf_op jit(solution)/shard_map/all_to_all | solution.py:99
  154.2 0.0 copy-done.6
  154.2 0.1 select_reduce_fusion.3
  154.3 0.1 copy.69
  154.4 0.1 reshape.163
  154.6 0.1 copy.64
  154.7 2.1 gather_fusion
  156.8 2.5 broadcast_select_fusion
  159.3 33.9 %all-to-all-done.3 = bf16[64,20,512]{2,1,0:T(8,128)(2,1)S(1)} async-done(((bf16[64,20,512]{2,1,0:T(8,128)(2,1)}), bf16[64,20,512]{2,1,0:T(8,128)(2,1)S(1)}, u32[]{:S(2)}, u32[]{:S(2)}) %all-to-all-start.3) | async-done | bytes 1310752 | tf_op jit(solution)/shard_map/all_to_all | solution.py:99
  193.2 1.2 copy-done.1
  194.3 6.5 %all-to-all-start.1 = ((bf16[64,2,4,768]{3,2,1,0:T(4,128)(2,1)}), bf16[64,2,4,768]{3,2,1,0:T(4,128)(2,1)S(1)}, u32[]{:S(2)}, u32[]{:S(2)}) async-start(bf16[64,2,4,768]{3,2,1,0:T(4,128)(2,1)} %broadcast_select_fusion), calls=%async_computation.1 | async-start | bytes 1572864 | tf_op jit(solution)/shard_map/all_to_all | solution.py:98
  200.8 0.2 all-reduce.5.cloned.1.call-start
  201.0 3.3 %reshape.167 = bf16[1280,512]{1,0:T(8,128)(2,1)} reshape(bf16[64,20,512]{2,1,0:T(8,128)(2,1)} %copy-done.1) | data formatting | bytes 2621440 | tf_op jit(solution)/shard_map/reshape | solution.py:104
  204.3 19.2 %all-to-all-done.1 = bf16[64,2,4,768]{3,2,1,0:T(4,128)(2,1)S(1)} async-done(((bf16[64,2,4,768]{3,2,1,0:T(4,128)(2,1)}), bf16[64,2,4,768]{3,2,1,0:T(4,128)(2,1)S(1)}, u32[]{:S(2)}, u32[]{:S(2)}) %all-to-all-start.1) | async-done | bytes 786464 | tf_op jit(solution)/shard_map/all_to_all | solution.py:98
  223.5 0.3 copy.76
  223.8 1.1 reshape.168
  224.9 4.1 %fusion = bf16[1280,768]{0,1:T(8,128)(2,1)} fusion(bf16[1280,512]{1,0:T(8,128)(2,1)} %reshape.167, bf16[512,768]{1,0:T(8,128)(2,1)} %reshape.168), kind=kOutput, calls=%fused_computation.3 | convolution fusion | flops 1008599040 | bytes 4063232 | tf_op jit(solution)/shard_map/dot_general | solution.py:104
  228.9 0.0 all-reduce.5.cloned.1.call-update
  229.0 0.1 copy.74
  229.1 0.1 reshape.171
  229.2 0.4 select_reduce_fusion
  229.5 0.7 convert_element_type.99
  230.3 6.2 %all-to-all-start.2 = ((bf16[64,1,20]{2,1,0:T(2,128)(2,1)}), bf16[64,1,20]{2,1,0:T(2,128)(2,1)S(1)}, u32[]{:S(2)}, u32[]{:S(2)}) async-start(bf16[64,1,20]{2,1,0:T(2,128)(2,1)} %convert_element_type.99), calls=%async_computation.2 | async-start | bytes 65536 | tf_op jit(solution)/shard_map/all_to_all | solution.py:100
  236.5 9.3 %all-to-all-done.2 = bf16[64,1,20]{2,1,0:T(2,128)(2,1)S(1)} async-done(((bf16[64,1,20]{2,1,0:T(2,128)(2,1)}), bf16[64,1,20]{2,1,0:T(2,128)(2,1)S(1)}, u32[]{:S(2)}, u32[]{:S(2)}) %all-to-all-start.2) | async-done | bytes 2592 | tf_op jit(solution)/shard_map/all_to_all | solution.py:100
  245.8 0.1 convert_reduce_fusion.1
  245.9 0.1 reshape.172
  246.0 0.6 copy.70
  246.6 1.0 copy.77
  247.6 59.4 %all-reduce.5.cloned.1.call-done = bf16[1280,768]{0,1:T(8,128)(2,1)} async-done(((bf16[1280,768]{0,1:T(8,128)(2,1)}), bf16[1280,768]{0,1:T(8,128)(2,1)}) %all-reduce.5.cloned.1.call-update) | async-done | bytes 1966096 | tf_op jit(solution)/shard_map/psum | solution.py:108
  307.0 1.8 fusion.24
  (16 shorter events, 0.1 us)
Async XLA Ops:
  7.2 10.3 %copy-start = (bf16[1,1,320,2048]{3,2,1,0:T(8,128)(2,1)S(1)}, bf16[1,1,320,2048]{3,2,1,0:T(8,128)(2,1)}, u32[]{:S(2)}) copy-start(bf16[1,1,320,2048]{3,2,1,0:T(8,128)(2,1)} %param.10) | copy-start | bytes 3932164
  7.2 111.3 %all-reduce.3.cloned.1.call-start = ((), (), s32[]{:S(2)}) async-start(), calls=%async_computation.4 | async-start | bytes 6291456 | tf_op jit(solution)/shard_map/psum | solution.py:80
  7.2 10.3 %collective-permute-start = (bf16[320,384]{1,0:T(8,128)(2,1)}, bf16[320,384]{1,0:T(8,128)(2,1)S(1)}, u32[]{:S(2)}, u32[]{:S(2)}) collective-permute-start(bf16[320,384]{1,0:T(8,128)(2,1)} %bitcast.54), channel_id=1, source_target_pairs={{0,1},{1,0},{2,3},{3,2},{4,5},{5,4},{6,7},{7,6},{8,9},{9,8},{10,11... | collective-permute-start | bytes 737288 | tf_op jit(solution)/shard_map/ppermute | solution.py:18
  22.1 1.1 copy-start.2
  22.1 4.0 %copy-start.4 = (s32[64,8]{0,1:T(8,128)S(1)}, s32[64,8]{0,1:T(8,128)}, u32[]{:S(2)}) copy-start(s32[64,8]{0,1:T(8,128)} %param.16) | copy-start | bytes 6148
  27.4 106.1 %copy-start.7 = (s32[64]{0:T(128)S(1)}, s32[64]{0:T(128)}, u32[]{:S(2)}) copy-start(s32[64]{0:T(128)} %param.19) | copy-start | bytes 772
  27.7 106.3 %copy-start.3 = (bf16[64,2,256]{2,1,0:T(2,128)(2,1)S(1)}, bf16[64,2,256]{2,1,0:T(2,128)(2,1)}, u32[]{:S(2)}) copy-start(bf16[64,2,256]{2,1,0:T(2,128)(2,1)} %param.15) | copy-start | bytes 196612
  123.0 25.6 %all-to-all-start = ((bf16[64,4,768]{2,1,0:T(4,128)(2,1)}), bf16[64,4,768]{2,1,0:T(4,128)(2,1)S(1)}, u32[]{:S(2)}, u32[]{:S(2)}) async-start(bf16[64,4,768]{2,1,0:T(4,128)(2,1)} %reshape.162), calls=%async_computation | async-start | bytes 786432 | tf_op jit(solution)/shard_map/all_to_all | solution.py:87
  135.4 18.8 %copy-start.6 = (s32[32]{0:T(128)S(1)}, s32[32]{0:T(128)}, u32[]{:S(2)}) copy-start(s32[32]{0:T(128)} %param.18) | copy-start | bytes 388
  148.6 44.6 %all-to-all-start.3 = ((bf16[64,20,512]{2,1,0:T(8,128)(2,1)}), bf16[64,20,512]{2,1,0:T(8,128)(2,1)S(1)}, u32[]{:S(2)}, u32[]{:S(2)}) async-start(bf16[64,20,512]{2,1,0:T(8,128)(2,1)} %reshape.166), calls=%async_computation.3 | async-start | bytes 3145728 | tf_op jit(solution)/shard_map/all_to_all | solution.py:99
  193.2 1.2 copy-start.1
  194.3 29.2 %all-to-all-start.1 = ((bf16[64,2,4,768]{3,2,1,0:T(4,128)(2,1)}), bf16[64,2,4,768]{3,2,1,0:T(4,128)(2,1)S(1)}, u32[]{:S(2)}, u32[]{:S(2)}) async-start(bf16[64,2,4,768]{3,2,1,0:T(4,128)(2,1)} %broadcast_select_fusion), calls=%async_computation.1 | async-start | bytes 1572864 | tf_op jit(solution)/shard_map/all_to_all | solution.py:98
  200.8 106.2 %all-reduce.5.cloned.1.call-start = ((), (), s32[]{:S(2)}) async-start(), calls=%async_computation.5 | async-start | bytes 3932160 | tf_op jit(solution)/shard_map/psum | solution.py:108
  224.9 4.1 %copy-start.5 = (bf16[64,8]{0,1:T(8,128)(2,1)S(1)}, bf16[64,8]{0,1:T(8,128)(2,1)}, u32[]{:S(2)}) copy-start(bf16[64,8]{0,1:T(8,128)(2,1)} %param.17) | copy-start | bytes 3076
  230.3 15.5 %all-to-all-start.2 = ((bf16[64,1,20]{2,1,0:T(2,128)(2,1)}), bf16[64,1,20]{2,1,0:T(2,128)(2,1)S(1)}, u32[]{:S(2)}, u32[]{:S(2)}) async-start(bf16[64,1,20]{2,1,0:T(2,128)(2,1)} %convert_element_type.99), calls=%async_computation.2 | async-start | bytes 65536 | tf_op jit(solution)/shard_map/all_to_all | solution.py:100
Sparse Core Ops, SparseCore 0:
  22.2 96.2 all-reduce.2
  229.1 77.8 all-reduce.4
where the time goes:
time: 319 us; the launch traced here: 316 us
  waiting for transfers between devices  226 us (71%)
  starting transfers between devices  38 us (12%)
  local copies, waits for them, and re-layouts  18.7 us (6%)
  between operations  14.3 us (4%)
  other arithmetic  9.56 us (3%)
  matrix products  9.18 us (3%)
    psum x1, waiting for transfers between devices, body(): lax.psum((product * width_scale).astype(jnp.bfloat16), 'rep')  90.8 us
    psum x1, waiting for transfers between devices, body(): lax.psum(partial_value.astype(jnp.bfloat16), 'rep').astype(jnp.float32)  59.4 us
    all_to_all x1, waiting for transfers between devices, body(): lax.all_to_all(send_tokens, 'ep', split_axis=0, concat_axis=0, tiled=True)  33.9 us
    all_to_all x1, waiting for transfers between devices, body(): lax.all_to_all(payload, 'ep', split_axis=0, concat_axis=0, tiled=True)  19.2 us
    all_to_all x1, waiting for transfers between devices, body(): lax.all_to_all(new_weight.reshape(ep_count, group_rows, hidden_width), 'e...  11.9 us
    all_to_all x1, starting transfers between devices, body(): lax.all_to_all(new_weight.reshape(ep_count, group_rows, hidden_width), 'e...  10.5 us
    all_to_all x1, waiting for transfers between devices, body(): lax.all_to_all(send_gates, 'ep', split_axis=0, concat_axis=0, tiled=True)  9.3 us
    ppermute x1, starting transfers between devices, swapped(): lax.ppermute(x, axis, [(i, i ^ 1 << apart) for i in range(lax.axis_size(a...  8.92 us
  transfers between devices with their start and end apart: 7, of which 7 were waited for; matrix products, arithmetic and copies ran while one was open for 6% of the time, Pallas kernels for 0%

commit v1 on v0

v1 whole, which is shorter than its diff:
```python
import math

import jax
import jax.numpy as jnp
from jax import lax
from jax.sharding import PartitionSpec as P

beta_one = 0.9
beta_two = 0.999
bias_one = 1.0 - math.exp(100.0 * math.log(0.9))
bias_two = 1.0 - math.exp(100.0 * math.log(0.999))
learn_rate = 0.5
decay_rate = 0.1
adam_eps = 1e-08


def swapped(x):
    return lax.ppermute(x, "ep", [(i, i ^ 1) for i in range(lax.axis_size("ep"))])


def exchanged(x):
    return lax.all_to_all(x, "ep", split_axis=0, concat_axis=0, tiled=True)


def exchanged_chips(x):
    ep_count = lax.axis_size("ep")
    groups = [list(range(core, ep_count, 2)) for core in range(2)]
    return lax.all_to_all(
        x, "ep", split_axis=0, concat_axis=0, tiled=True, axis_index_groups=groups
    )


def body(
    train_acts,
    train_cotan,
    weight,
    moment_one,
    moment_two,
    tokens,
    routes,
    gate_weights,
    train_place,
    serve_place,
):
    ep_count = lax.axis_size("ep")
    rep_count = lax.axis_size("rep")
    chip_count = ep_count // 2
    core = lax.axis_index("ep") % 2
    is_upper = core == 1
    acts_local = train_acts[0, 0]
    half_width = acts_local.shape[1]
    width_scale = float(2 * half_width) ** (-0.5)
    piece_rows = weight.shape[2]
    hidden_width = weight.shape[3]
    share_width = hidden_width // rep_count
    row_count, top_count = routes.shape
    expert_count = train_place.shape[0]
    capacity = min(row_count, row_count * top_count // expert_count + max(1, row_count // 16))
    pair_count = row_count * top_count
    slot_count = expert_count * capacity
    expert_ids = jnp.arange(expert_count, dtype=jnp.int32)
    device_ids = jnp.arange(ep_count, dtype=jnp.int32)

    own_cotan = train_cotan[0, 0]
    partner_cotan = swapped(own_cotan)
    full_cotan = jnp.where(
        is_upper,
        jnp.concatenate([partner_cotan, own_cotan], axis=1),
        jnp.concatenate([own_cotan, partner_cotan], axis=1),
    )
    product = lax.dot_general(
        acts_local, full_cotan, (((0,), (0,)), ((), ())), preferred_element_type=jnp.float32
    )
    summed = lax.psum_scatter(
        (product * width_scale).astype(jnp.bfloat16), "rep", scatter_dimension=0, tiled=True
    )

    chosen = routes.reshape(pair_count)
    picked = (chosen[:, None] == expert_ids[None, :]).astype(jnp.int32)
    position = jnp.sum((jnp.cumsum(picked, axis=0) - 1) * picked, axis=1)
    trainer = jnp.sum(picked * train_place[None, :], axis=1)
    slot_of_pair = trainer * capacity + position
    placing = jnp.arange(slot_count, dtype=jnp.int32)[:, None] == slot_of_pair[None, :]
    place_rows = jnp.sum(
        placing.reshape(slot_count, row_count, top_count).astype(jnp.int32), axis=2
    ).astype(jnp.bfloat16)
    halves = [
        jnp.dot(place_rows, tokens[:, h, :], preferred_element_type=jnp.float32)
        .astype(jnp.bfloat16)
        .reshape(chip_count, capacity, -1)
        for h in range(2)
    ]
    send_tokens = jnp.stack(halves, axis=1).reshape(ep_count, capacity, -1)
    gate_row = gate_weights.reshape(1, pair_count).astype(jnp.float32)
    slot_gates = jnp.sum(jnp.where(placing, gate_row, 0.0), axis=1)
    recv_tokens = exchanged(send_tokens).reshape(ep_count * capacity, -1)

    weight_local, recv_tokens = lax.optimization_barrier((weight[0, 0], recv_tokens))
    gradient = summed.astype(jnp.float32)
    first = beta_one * moment_one[0, 0] + (1.0 - beta_one) * gradient
    second = beta_two * moment_two[0, 0] + (1.0 - beta_two) * gradient * gradient
    weight_now = weight_local.astype(jnp.float32)
    update = first / bias_one / (jnp.sqrt(second / bias_two) + adam_eps)
    new_weight = (weight_now - learn_rate * (update + decay_rate * weight_now)).astype(jnp.bfloat16)

    terms = (
        lax.dot_general(
            new_weight, recv_tokens, (((0,), (1,)), ((), ())), preferred_element_type=jnp.float32
        )
        * width_scale
    ).astype(jnp.bfloat16)
    preact_share = lax.psum_scatter(terms, "rep", scatter_dimension=0, tiled=True)

    group_rows = piece_rows // chip_count
    spread = exchanged_chips(new_weight.reshape(chip_count, group_rows, hidden_width))
    served_from = jnp.sum(
        jnp.where(serve_place[:, None] == expert_ids[None, :], train_place[None, :], 0), axis=1
    )
    from_pairs = served_from.reshape(chip_count, 2)
    from_order = jnp.where(is_upper, from_pairs[:, ::-1], from_pairs).reshape(ep_count)
    payload = jnp.take(spread, from_order, axis=0).reshape(
        chip_count, 2 * group_rows, hidden_width
    )
    arrived = exchanged_chips(payload)
    own_half = arrived[:, :group_rows].reshape(piece_rows, hidden_width)
    other_half = swapped(arrived[:, group_rows:].reshape(piece_rows, hidden_width))
    serving = jnp.where(
        is_upper, jnp.stack([other_half, own_half]), jnp.stack([own_half, other_half])
    )

    preact_share, arrived = lax.optimization_barrier((preact_share, arrived))
    back = exchanged(
        jnp.transpose(preact_share.reshape(share_width, ep_count, capacity), (1, 2, 0))
    )
    preact = jnp.sum(
        back.reshape(chip_count, 2, capacity, share_width).astype(jnp.float32), axis=1
    )
    activation = (
        slot_gates.reshape(chip_count, capacity, 1) * jax.nn.silu(preact)
    ).astype(jnp.bfloat16)
    first_device = jnp.min(
        jnp.where(serve_place[None, :] == expert_ids[:, None], device_ids[None, :], ep_count),
        axis=1,
    )
    is_first = (
        jnp.sum((first_device[None, :] == device_ids[:, None]).astype(jnp.int32), axis=1) > 0
    )
    choosing = (
        (served_from[:, None] == jnp.arange(chip_count, dtype=jnp.int32)[None, :])
        & is_first[:, None]
    ).astype(jnp.bfloat16)
    send_acts = (
        jnp.dot(
            choosing,
            activation.reshape(chip_count, capacity * share_width),
            preferred_element_type=jnp.float32,
        )
        .astype(jnp.bfloat16)
        .reshape(ep_count, capacity, share_width)
    )
    out_acts = exchanged(send_acts)
    return (
        serving.reshape(1, 1, 2, piece_rows, hidden_width),
        out_acts.reshape(1, ep_count * capacity, share_width),
    )


def solution(mesh):
    return jax.shard_map(
        body,
        mesh=mesh,
        in_specs=(
            P("rep", "ep", None, None),
            P("rep", "ep", None, None),
            P("rep", "ep", None, None),
            P("rep", "ep", None, None),
            P("rep", "ep", None, None),
            P("ep", None, "rep"),
            P("ep", None),
            P("ep", None),
            P(),
            P(),
        ),
        out_specs=(P("rep", "ep", None, None, None), P("ep", None, "rep")),
        check_vma=False,
    )
```

time: 319 us -> 179 us (0.56)
  waiting for transfers between devices: 226 us -> 87.5 us
  starting transfers between devices: 38 us -> 47.4 us
  local copies, waits for them, and re-layouts: 18.7 us -> 14.8 us
    psum x2 -> x0, waiting for transfers between devices: 150 us -> none  [the longest x1 90.8 us: body(): lax.psum((product * width_scale).astype(jnp.bfloat16), 'rep')]
    reduce_scatter x0 -> x2, waiting for transfers between devices: none -> 13.9 us  [the longest x1 13.9 us: body(): lax.psum_scatter((product * width_scale).astype(jnp.bfloat16), 'rep', sca...]
    all_to_all x4 -> x5, starting transfers between devices: 28.8 us -> 36 us  [the longest x3 22.4 us: exchanged(): return lax.all_to_all(x, 'ep', split_axis=0, concat_axis=0, tiled=True)]
    reshape x5 -> x8, local copies, waits for them, and re-layouts: 6.63 us -> 3.54 us  [the longest x1 1.24 us: body(): send_acts = jnp.dot(choosing, activation.reshape(chip_count, capacity * s...]
    ppermute x1 -> x2, starting transfers between devices: 8.92 us -> 11.3 us  [swapped(): lax.ppermute(x, 'ep', [(i, i ^ 1) for i in range(lax.axis_size('ep'))])]
    all_to_all x4 -> x5, waiting for transfers between devices: 74.3 us -> 72.3 us  [the longest x3 44.2 us: exchanged(): return lax.all_to_all(x, 'ep', split_axis=0, concat_axis=0, tiled=True)]
    unnamed x22 -> x19, local copies, waits for them, and re-layouts: 6.16 us -> 6.92 us
  transfers between devices with their start and end apart: 7 -> 9, of which waited for: 7 -> 7; matrix products, arithmetic and copies ran while one was open for 6% -> 9% of each run, Pallas kernels for 0% -> 0%
where the time goes in v1:
time: 179 us; the launch traced here: 178 us
  waiting for transfers between devices  87.5 us (49%)
  starting transfers between devices  47.4 us (26%)
  local copies, waits for them, and re-layouts  14.8 us (8%)
  between operations  14.4 us (8%)
  matrix products  7.4 us (4%)
  other arithmetic  6.59 us (4%)
    all_to_all x3, waiting for transfers between devices, exchanged(): return lax.all_to_all(x, 'ep', split_axis=0, concat_axis=0, tiled=True)  44.2 us
    all_to_all x2, waiting for transfers between devices, exchanged_chips(): lax.all_to_all(x, 'ep', split_axis=0, concat_axis=0, tiled=True, axis_ind...  28.1 us
    all_to_all x3, starting transfers between devices, exchanged(): return lax.all_to_all(x, 'ep', split_axis=0, concat_axis=0, tiled=True)  22.4 us
    reduce_scatter x1, waiting for transfers between devices, body(): lax.psum_scatter((product * width_scale).astype(jnp.bfloat16), 'rep', sca...  13.9 us
    all_to_all x2, starting transfers between devices, exchanged_chips(): lax.all_to_all(x, 'ep', split_axis=0, concat_axis=0, tiled=True, axis_ind...  13.7 us
    ppermute x2, starting transfers between devices, swapped(): lax.ppermute(x, 'ep', [(i, i ^ 1) for i in range(lax.axis_size('ep'))])  11.3 us
    unnamed x19, local copies, waits for them, and re-layouts  6.92 us
    dot_general x1, matrix products, body(): lax.dot_general(acts_local, full_cotan, (((0,), (0,)), ((), ())), preferr...  4.57 us
  transfers between devices with their start and end apart: 9, of which 7 were waited for; matrix products, arithmetic and copies ran while one was open for 9% of the time, Pallas kernels for 0%

profile of v1, /device:TPU:1, one launch (start us, length us, event | category | flops | bytes accessed | tf_op | source)
XLA Modules:
  0.0 178.1 jit_solution(10317346276534786673)
XLA Ops:
  7.2 8.9 %collective-permute-start = (bf16[320,384]{1,0:T(8,128)(2,1)}, bf16[320,384]{1,0:T(8,128)(2,1)S(1)}, u32[]{:S(2)}, u32[]{:S(2)}) collective-permute-start(bf16[320,384]{1,0:T(8,128)(2,1)} %bitcast.57), channel_id=1, source_target_pairs={{0,1},{1,0},{2,3},{3,2},{4,5},{5,4},{6,7},{7,6},{8,9},{9,8},{10,11... | collective-permute-start | bytes 737288 | tf_op jit(solution)/shard_map/ppermute | solution.py:18
  16.2 1.3 collective-permute-done
  17.5 4.6 %fusion.1 = bf16[2048,768]{0,1:T(8,128)(2,1)} fusion(bf16[1,1,320,2048]{3,2,1,0:T(8,128)(2,1)S(1)} %copy-done, bf16[320,384]{1,0:T(8,128)(2,1)} %bitcast.58, bf16[320,384]{1,0:T(8,128)(2,1)S(1)} %collective-permute-done, pred[]{:T(512)S(6)} %eq.102), kind=kOutput, calls=%fused_computation.4 | convolution fusion | flops 1011990528 | bytes 4947969 | tf_op jit(solution)/shard_map/dot_general | solution.py:71
  22.1 0.7 copy-done.3
  22.7 0.1 copy.52
  22.8 0.1 eq.111
  22.9 0.1 eq.107
  23.0 1.2 reduce-window.6
  24.2 0.2 slice_reduce_fusion
  24.4 0.1 select_reduce_fusion.1
  24.6 0.1 add.68
  24.7 0.4 convert_reduce_fusion
  25.1 0.1 fusion.31
  25.2 0.3 convolution_convert_fusion.2
  25.5 0.1 stack_reshape.8
  25.6 0.3 convolution_convert_fusion.1
  25.9 0.1 stack_reshape.9
  26.0 0.1 pad_maximum_fusion
  26.1 0.9 copy.65
  27.0 5.1 %all-to-all-start = ((bf16[64,20,256]{2,1,0:T(8,128)(2,1)}), bf16[64,20,256]{2,1,0:T(8,128)(2,1)S(1)}, u32[]{:S(2)}, u32[]{:S(2)}) async-start(bf16[64,20,256]{2,1,0:T(8,128)(2,1)} %bitcast.5), calls=%async_computation | async-start | bytes 1572864 | tf_op jit(solution)/shard_map/all_to_all | solution.py:22
  32.2 0.9 copy.51
  33.1 1.4 copy.59
  34.5 2.3 %copy.60 = f32[1,1,256,768]{2,3,1,0:T(8,128)} copy(f32[1,1,256,768]{3,2,1,0:T(8,128)} %param.14) | data formatting | bytes 1572864 | tf_op args[4]
  36.9 18.0 %all-to-all-done = bf16[64,20,256]{2,1,0:T(8,128)(2,1)S(1)} async-done(((bf16[64,20,256]{2,1,0:T(8,128)(2,1)}), bf16[64,20,256]{2,1,0:T(8,128)(2,1)S(1)}, u32[]{:S(2)}, u32[]{:S(2)}) %all-to-all-start) | async-done | bytes 655392 | tf_op jit(solution)/shard_map/all_to_all | solution.py:22
  54.9 0.1 reshape.202
  55.0 13.9 %reduce-scatter.3.cloned.1.call-done = bf16[256,768]{0,1:T(8,128)(2,1)} async-done(((bf16[2048,768]{0,1:T(8,128)(2,1)}), bf16[256,768]{0,1:T(8,128)(2,1)}) %reduce-scatter.3.cloned.1.call-update) | async-done | bytes 393232 | tf_op jit(solution)/shard_map/reduce_scatter | solution.py:74
  69.0 2.1 %fusion.5 = bf16[256,768]{0,1:T(8,128)(2,1)S(1)} fusion(bf16[256,768]{0,1:T(8,128)(2,1)} %bitcast.55, bf16[256,768]{0,1:T(8,128)(2,1)} %reduce-scatter.3.cloned.1.call-done, f32[1,1,256,768]{2,3,1,0:T(8,128)} %copy.60, f32[1,1,256,768]{2,3,1,0:T(8,128)S(1)} %copy.59), kind=kLoop, calls=%fused_computation.19 | loop fusion | flops 3538944 | bytes 2752512 | tf_op jit(solution)/shard_map/convert_element_type | solution.py:104
  71.0 2.0 %fusion = bf16[768,1280]{1,0:T(8,128)(2,1)} fusion(bf16[256,768]{0,1:T(8,128)(2,1)S(1)} %fusion.5, bf16[1280,256]{1,0:T(8,128)(2,1)S(1)} %reshape.202), kind=kOutput, calls=%fused_computation.3 | convolution fusion | flops 505282560 | bytes 3014656 | tf_op jit(solution)/shard_map/dot_general | solution.py:107
  73.1 0.6 copy-done.6
  73.7 0.1 select_reduce_fusion.3
  73.8 0.1 reshape.199
  73.9 0.1 rev.3
  74.0 0.9 copy.61
  74.9 9.2 %all-to-all-start.1 = ((bf16[32,8,768]{2,1,0:T(8,128)(2,1)}), bf16[32,8,768]{2,1,0:T(8,128)(2,1)S(1)}, u32[]{:S(2)}, u32[]{:S(2)}) async-start(bf16[32,8,768]{2,1,0:T(8,128)(2,1)} %bitcast.11), calls=%async_computation.2 | async-start | bytes 786432 | tf_op jit(solution)/shard_map/all_to_all | solution.py:28
  84.2 0.1 reshape.204
  84.3 0.1 copy.49
  84.4 0.1 copy.50
  84.5 11.1 %all-to-all-done.1 = bf16[32,8,768]{2,1,0:T(8,128)(2,1)S(1)} async-done(((bf16[32,8,768]{2,1,0:T(8,128)(2,1)}), bf16[32,8,768]{2,1,0:T(8,128)(2,1)S(1)}, u32[]{:S(2)}, u32[]{:S(2)}) %all-to-all-start.1) | async-done | bytes 393248 | tf_op jit(solution)/shard_map/all_to_all | solution.py:28
  95.6 0.6 gather_fusion
  96.2 1.0 bitcast_select_fusion
  97.2 4.4 %all-to-all-start.2 = ((bf16[32,16,768]{2,1,0:T(8,128)(2,1)}), bf16[32,16,768]{2,1,0:T(8,128)(2,1)S(1)}, u32[]{:S(2)}, u32[]{:S(2)}) async-start(bf16[32,16,768]{2,1,0:T(8,128)(2,1)} %bitcast_select_fusion), calls=%async_computation.3 | async-start | bytes 1572864 | tf_op jit(solution)/shard_map/all_to_all | solution.py:28
  101.7 0.1 copy.62
  101.8 0.1 reshape.209
  101.9 0.1 select_reduce_fusion.2
  102.0 0.2 select_reduce_fusion
  102.2 17.0 %all-to-all-done.2 = bf16[32,16,768]{2,1,0:T(8,128)(2,1)S(1)} async-done(((bf16[32,16,768]{2,1,0:T(8,128)(2,1)}), bf16[32,16,768]{2,1,0:T(8,128)(2,1)S(1)}, u32[]{:S(2)}, u32[]{:S(2)}) %all-to-all-start.2) | async-done | bytes 786464 | tf_op jit(solution)/shard_map/all_to_all | solution.py:28
  119.2 1.2 copy.63
  120.3 0.9 reshape.206
  121.2 11.7 %all-to-all-start.3 = ((bf16[64,20,96]{2,1,0:T(8,128)(2,1)}), bf16[64,20,96]{2,1,0:T(8,128)(2,1)S(1)}, u32[]{:S(2)}, u32[]{:S(2)}) async-start(bf16[64,20,96]{2,1,0:T(8,128)(2,1)} %bitcast.17), calls=%async_computation.5 | async-start | bytes 786432 | tf_op jit(solution)/shard_map/all_to_all | solution.py:22
  132.8 0.1 convert_reduce_fusion.2
  132.9 0.1 mul.113
  133.0 0.2 mul.114
  133.2 0.1 mul.115
  133.4 2.4 %collective-permute-start.1 = (bf16[256,768]{1,0:T(8,128)(2,1)S(1)}, bf16[256,768]{1,0:T(8,128)(2,1)S(1)}, u32[]{:S(2)}, u32[]{:S(2)}) collective-permute-start(bf16[256,768]{1,0:T(8,128)(2,1)S(1)} %get-tuple-element.18), channel_id=1, source_target_pairs={{0,1},{1,0},{2,3},{3,2},{4,5},{5,4},{6,7},{7,6},{8,9},{9,8},{10,11... | collective-permute-start | bytes 1179656 | tf_op jit(solution)/shard_map/ppermute | solution.py:18
  135.8 12.1 %all-to-all-done.3 = bf16[64,20,96]{2,1,0:T(8,128)(2,1)S(1)} async-done(((bf16[64,20,96]{2,1,0:T(8,128)(2,1)}), bf16[64,20,96]{2,1,0:T(8,128)(2,1)S(1)}, u32[]{:S(2)}, u32[]{:S(2)}) %all-to-all-start.3) | async-done | bytes 245792 | tf_op jit(solution)/shard_map/all_to_all | solution.py:22
  147.9 0.1 convert_reduce_fusion.1
  148.0 0.1 reduce_sum.72
  148.1 0.3 convolution_convert_fusion
  148.4 1.2 reshape.207
  149.6 5.6 %all-to-all-start.4 = ((bf16[64,20,96]{2,1,0:T(8,128)(2,1)}), bf16[64,20,96]{2,1,0:T(8,128)(2,1)S(1)}, u32[]{:S(2)}, u32[]{:S(2)}) async-start(bf16[64,20,96]{2,1,0:T(8,128)(2,1)} %reshape.207), calls=%async_computation.6 | async-start | bytes 786432 | tf_op jit(solution)/shard_map/all_to_all | solution.py:22
  155.2 1.0 maximum_select_fusion
  156.2 14.0 %all-to-all-done.4 = bf16[64,20,96]{2,1,0:T(8,128)(2,1)S(1)} async-done(((bf16[64,20,96]{2,1,0:T(8,128)(2,1)}), bf16[64,20,96]{2,1,0:T(8,128)(2,1)S(1)}, u32[]{:S(2)}, u32[]{:S(2)}) %all-to-all-start.4) | async-done | bytes 245792 | tf_op jit(solution)/shard_map/all_to_all | solution.py:22
  170.3 0.1 reshape.208
  170.4 0.9 copy.64
  (28 shorter events, 0.3 us)
Async XLA Ops:
  7.2 10.3 %copy-start = (bf16[1,1,320,2048]{3,2,1,0:T(8,128)(2,1)S(1)}, bf16[1,1,320,2048]{3,2,1,0:T(8,128)(2,1)}, u32[]{:S(2)}) copy-start(bf16[1,1,320,2048]{3,2,1,0:T(8,128)(2,1)} %param.10) | copy-start | bytes 3932164
  7.2 61.8 %reduce-scatter.3.cloned.1.call-start = ((), (), s32[]{:S(2)}) async-start(), calls=%async_computation.7 | async-start | bytes 3538944 | tf_op jit(solution)/shard_map/reduce_scatter | solution.py:74
  7.2 10.3 %collective-permute-start = (bf16[320,384]{1,0:T(8,128)(2,1)}, bf16[320,384]{1,0:T(8,128)(2,1)S(1)}, u32[]{:S(2)}, u32[]{:S(2)}) collective-permute-start(bf16[320,384]{1,0:T(8,128)(2,1)} %bitcast.57), channel_id=1, source_target_pairs={{0,1},{1,0},{2,3},{3,2},{4,5},{5,4},{6,7},{7,6},{8,9},{9,8},{10,11... | collective-permute-start | bytes 737288 | tf_op jit(solution)/shard_map/ppermute | solution.py:18
  22.0 0.7 copy-start.3
  22.0 2.4 %copy-start.5 = (s32[32]{0:T(128)S(1)}, s32[32]{0:T(128)}, u32[]{:S(2)}) copy-start(s32[32]{0:T(128)} %param.18) | copy-start | bytes 388
  22.1 3.1 %copy-start.2 = (bf16[64,2,256]{2,1,0:T(2,128)(2,1)S(1)}, bf16[64,2,256]{2,1,0:T(2,128)(2,1)}, u32[]{:S(2)}) copy-start(bf16[64,2,256]{2,1,0:T(2,128)(2,1)} %param.15) | copy-start | bytes 196612
  26.1 6.1 %copy-start.1 = (bf16[1,1,256,768]{3,2,1,0:T(8,128)(2,1)S(1)}, bf16[1,1,256,768]{3,2,1,0:T(8,128)(2,1)}, u32[]{:S(2)}) copy-start(bf16[1,1,256,768]{3,2,1,0:T(8,128)(2,1)} %param.12) | copy-start | bytes 1179652
  27.0 27.9 %all-to-all-start = ((bf16[64,20,256]{2,1,0:T(8,128)(2,1)}), bf16[64,20,256]{2,1,0:T(8,128)(2,1)S(1)}, u32[]{:S(2)}, u32[]{:S(2)}) async-start(bf16[64,20,256]{2,1,0:T(8,128)(2,1)} %bitcast.5), calls=%async_computation | async-start | bytes 1572864 | tf_op jit(solution)/shard_map/all_to_all | solution.py:22
  32.1 87.0 %reduce-scatter.5.cloned.1.call-start = ((), (), s32[]{:S(2)}) async-start(), calls=%async_computation.8 | async-start | bytes 2211840 | tf_op jit(solution)/shard_map/reduce_scatter | solution.py:112
  73.0 0.7 copy-start.6
  74.9 20.7 %all-to-all-start.1 = ((bf16[32,8,768]{2,1,0:T(8,128)(2,1)}), bf16[32,8,768]{2,1,0:T(8,128)(2,1)S(1)}, u32[]{:S(2)}, u32[]{:S(2)}) async-start(bf16[32,8,768]{2,1,0:T(8,128)(2,1)} %bitcast.11), calls=%async_computation.2 | async-start | bytes 786432 | tf_op jit(solution)/shard_map/all_to_all | solution.py:28
  96.2 5.5 %copy-start.4 = (bf16[64,8]{0,1:T(8,128)(2,1)S(1)}, bf16[64,8]{0,1:T(8,128)(2,1)}, u32[]{:S(2)}) copy-start(bf16[64,8]{0,1:T(8,128)(2,1)} %param.17) | copy-start | bytes 3076
  97.2 21.9 %all-to-all-start.2 = ((bf16[32,16,768]{2,1,0:T(8,128)(2,1)}), bf16[32,16,768]{2,1,0:T(8,128)(2,1)S(1)}, u32[]{:S(2)}, u32[]{:S(2)}) async-start(bf16[32,16,768]{2,1,0:T(8,128)(2,1)} %bitcast_select_fusion), calls=%async_computation.3 | async-start | bytes 1572864 | tf_op jit(solution)/shard_map/all_to_all | solution.py:28
  121.2 26.7 %all-to-all-start.3 = ((bf16[64,20,96]{2,1,0:T(8,128)(2,1)}), bf16[64,20,96]{2,1,0:T(8,128)(2,1)S(1)}, u32[]{:S(2)}, u32[]{:S(2)}) async-start(bf16[64,20,96]{2,1,0:T(8,128)(2,1)} %bitcast.17), calls=%async_computation.5 | async-start | bytes 786432 | tf_op jit(solution)/shard_map/all_to_all | solution.py:22
  133.4 21.8 %collective-permute-start.1 = (bf16[256,768]{1,0:T(8,128)(2,1)S(1)}, bf16[256,768]{1,0:T(8,128)(2,1)S(1)}, u32[]{:S(2)}, u32[]{:S(2)}) collective-permute-start(bf16[256,768]{1,0:T(8,128)(2,1)S(1)} %get-tuple-element.18), channel_id=1, source_target_pairs={{0,1},{1,0},{2,3},{3,2},{4,5},{5,4},{6,7},{7,6},{8,9},{9,8},{10,11... | collective-permute-start | bytes 1179656 | tf_op jit(solution)/shard_map/ppermute | solution.py:18
  149.6 20.7 %all-to-all-start.4 = ((bf16[64,20,96]{2,1,0:T(8,128)(2,1)}), bf16[64,20,96]{2,1,0:T(8,128)(2,1)S(1)}, u32[]{:S(2)}, u32[]{:S(2)}) async-start(bf16[64,20,96]{2,1,0:T(8,128)(2,1)} %reshape.207), calls=%async_computation.6 | async-start | bytes 786432 | tf_op jit(solution)/shard_map/all_to_all | solution.py:22
Sparse Core Ops, SparseCore 0:
  22.2 46.7 reduce-scatter.2
  73.2 42.1 reduce-scatter.4

commit v2 on v1

--- a/solution.py
+++ b/solution.py
@@ -84,18 +84,20 @@
     place_rows = jnp.sum(
         placing.reshape(slot_count, row_count, top_count).astype(jnp.int32), axis=2
     ).astype(jnp.bfloat16)
-    halves = [
-        jnp.dot(place_rows, tokens[:, h, :], preferred_element_type=jnp.float32)
-        .astype(jnp.bfloat16)
-        .reshape(chip_count, capacity, -1)
-        for h in range(2)
-    ]
-    send_tokens = jnp.stack(halves, axis=1).reshape(ep_count, capacity, -1)
+    send_tokens = jnp.dot(
+        place_rows, tokens.reshape(row_count, -1), preferred_element_type=jnp.float32
+    ).astype(jnp.bfloat16)
     gate_row = gate_weights.reshape(1, pair_count).astype(jnp.float32)
     slot_gates = jnp.sum(jnp.where(placing, gate_row, 0.0), axis=1)
-    recv_tokens = exchanged(send_tokens).reshape(ep_count * capacity, -1)
+    recv_tokens = exchanged_chips(send_tokens.reshape(chip_count, capacity, -1))
+    recv_tokens = recv_tokens.reshape(slot_count, 2 * piece_rows)
+    lower_tokens, upper_tokens = recv_tokens[:, :piece_rows], recv_tokens[:, piece_rows:]
+    own_tokens = jnp.where(is_upper, upper_tokens, lower_tokens)
+    partner_tokens = jnp.where(is_upper, lower_tokens, upper_tokens)
 
-    weight_local, recv_tokens = lax.optimization_barrier((weight[0, 0], recv_tokens))
+    weight_local, own_tokens, partner_tokens = lax.optimization_barrier(
+        (weight[0, 0], own_tokens, partner_tokens)
+    )
     gradient = summed.astype(jnp.float32)
     first = beta_one * moment_one[0, 0] + (1.0 - beta_one) * gradient
     second = beta_two * moment_two[0, 0] + (1.0 - beta_two) * gradient * gradient
@@ -103,12 +105,15 @@
     update = first / bias_one / (jnp.sqrt(second / bias_two) + adam_eps)
     new_weight = (weight_now - learn_rate * (update + decay_rate * weight_now)).astype(jnp.bfloat16)
 
-    terms = (
-        lax.dot_general(
-            new_weight, recv_tokens, (((0,), (1,)), ((), ())), preferred_element_type=jnp.float32
-        )
-        * width_scale
-    ).astype(jnp.bfloat16)
+    partner_weight = swapped(new_weight)
+    rows_last = (((0,), (1,)), ((), ()))
+    own_terms = lax.dot_general(
+        new_weight, own_tokens, rows_last, preferred_element_type=jnp.float32
+    )
+    partner_terms = lax.dot_general(
+        partner_weight, partner_tokens, rows_last, preferred_element_type=jnp.float32
+    )
+    terms = ((own_terms + partner_terms) * width_scale).astype(jnp.bfloat16)
     preact_share = lax.psum_scatter(terms, "rep", scatter_dimension=0, tiled=True)
 
     group_rows = piece_rows // chip_count
@@ -118,8 +123,10 @@
     )
     from_pairs = served_from.reshape(chip_count, 2)
     from_order = jnp.where(is_upper, from_pairs[:, ::-1], from_pairs).reshape(ep_count)
-    payload = jnp.take(spread, from_order, axis=0).reshape(
-        chip_count, 2 * group_rows, hidden_width
+    payload = (
+        spread.at[from_order]
+        .get(mode="promise_in_bounds")
+        .reshape(chip_count, 2 * group_rows, hidden_width)
     )
     arrived = exchanged_chips(payload)
     own_half = arrived[:, :group_rows].reshape(piece_rows, hidden_width)
@@ -129,14 +136,11 @@
     )
 
     preact_share, arrived = lax.optimization_barrier((preact_share, arrived))
-    back = exchanged(
-        jnp.transpose(preact_share.reshape(share_width, ep_count, capacity), (1, 2, 0))
-    )
-    preact = jnp.sum(
-        back.reshape(chip_count, 2, capacity, share_width).astype(jnp.float32), axis=1
+    back = exchanged_chips(
+        jnp.transpose(preact_share.reshape(share_width, chip_count, capacity), (1, 2, 0))
     )
     activation = (
-        slot_gates.reshape(chip_count, capacity, 1) * jax.nn.silu(preact)
+        slot_gates.reshape(chip_count, capacity, 1) * jax.nn.silu(back.astype(jnp.float32))
     ).astype(jnp.bfloat16)
     first_device = jnp.min(
         jnp.where(serve_place[None, :] == expert_ids[:, None], device_ids[None, :], ep_count),
@@ -145,18 +149,11 @@
     is_first = (
         jnp.sum((first_device[None, :] == device_ids[:, None]).astype(jnp.int32), axis=1) > 0
     )
-    choosing = (
-        (served_from[:, None] == jnp.arange(chip_count, dtype=jnp.int32)[None, :])
-        & is_first[:, None]
-    ).astype(jnp.bfloat16)
-    send_acts = (
-        jnp.dot(
-            choosing,
-            activation.reshape(chip_count, capacity * share_width),
-            preferred_element_type=jnp.float32,
-        )
-        .astype(jnp.bfloat16)
-        .reshape(ep_count, capacity, share_width)
+    padded = jnp.concatenate(
+        [activation, jnp.zeros((1, capacity, share_width), jnp.bfloat16)], axis=0
+    )
+    send_acts = padded.at[jnp.where(is_first, served_from, chip_count)].get(
+        mode="promise_in_bounds"
     )
     out_acts = exchanged(send_acts)
     return (

time: 179 us -> 183 us (1.022)
  starting transfers between devices: 47.4 us -> 57.7 us
  waiting for transfers between devices: 87.5 us -> 82.7 us
    all_to_all x3 -> x1, waiting for transfers between devices: 44.2 us -> 14.2 us  [exchanged(): return lax.all_to_all(x, 'ep', split_axis=0, concat_axis=0, tiled=True)]
    all_to_all x2 -> x4, waiting for transfers between devices: 28.1 us -> 51.3 us  [exchanged_chips(): lax.all_to_all(x, 'ep', split_axis=0, concat_axis=0, tiled=True, axis_ind...]
    all_to_all x2 -> x4, starting transfers between devices: 13.7 us -> 26.3 us  [exchanged_chips(): lax.all_to_all(x, 'ep', split_axis=0, concat_axis=0, tiled=True, axis_ind...]
    all_to_all x3 -> x1, starting transfers between devices: 22.4 us -> 10.2 us  [exchanged(): return lax.all_to_all(x, 'ep', split_axis=0, concat_axis=0, tiled=True)]
    ppermute x2 -> x3, starting transfers between devices: 11.3 us -> 21.1 us  [swapped(): lax.ppermute(x, 'ep', [(i, i ^ 1) for i in range(lax.axis_size('ep'))])]
    gather x1 -> x2, local copies, waits for them, and re-layouts: 0.6 us -> 2.84 us  [the longest x1 1.48 us: body(): payload = spread.at[from_order].get(mode='promise_in_bounds').reshape(chi...]
    reduce_scatter x1, waiting for transfers between devices: 13.9 us -> 15.8 us  [body(): lax.psum_scatter((product * width_scale).astype(jnp.bfloat16), 'rep', sca...]
    unnamed x19 -> x26, local copies, waits for them, and re-layouts: 6.92 us -> 6.66 us
  transfers between devices with their start and end apart: 9 -> 10, of which waited for: 7 -> 7; matrix products, arithmetic and copies ran while one was open for 9% -> 10% of each run, Pallas kernels for 0% -> 0%
where the time goes in v2:
time: 183 us
  waiting for transfers between devices  82.7 us (45%)
  starting transfers between devices  57.7 us (32%)
  local copies, waits for them, and re-layouts  14.6 us (8%)
  between operations  14.4 us (8%)
  matrix products  6.88 us (4%)
  other arithmetic  6.25 us (3%)
    all_to_all x4, waiting for transfers between devices, exchanged_chips(): lax.all_to_all(x, 'ep', split_axis=0, concat_axis=0, tiled=True, axis_ind...  51.3 us
    all_to_all x4, starting transfers between devices, exchanged_chips(): lax.all_to_all(x, 'ep', split_axis=0, concat_axis=0, tiled=True, axis_ind...  26.3 us
    ppermute x3, starting transfers between devices, swapped(): lax.ppermute(x, 'ep', [(i, i ^ 1) for i in range(lax.axis_size('ep'))])  21.1 us
    reduce_scatter x1, waiting for transfers between devices, body(): lax.psum_scatter((product * width_scale).astype(jnp.bfloat16), 'rep', sca...  15.8 us
    all_to_all x1, waiting for transfers between devices, exchanged(): return lax.all_to_all(x, 'ep', split_axis=0, concat_axis=0, tiled=True)  14.2 us
    all_to_all x1, starting transfers between devices, exchanged(): return lax.all_to_all(x, 'ep', split_axis=0, concat_axis=0, tiled=True)  10.2 us
    unnamed x26, local copies, waits for them, and re-layouts  6.66 us
    dot_general x1, matrix products, body(): lax.dot_general(acts_local, full_cotan, (((0,), (0,)), ((), ())), preferr...  4.57 us
  transfers between devices with their start and end apart: 10, of which 7 were waited for; matrix products, arithmetic and copies ran while one was open for 10% of the time, Pallas kernels for 0%

profile of v2, /device:TPU:1, one launch (start us, length us, event | category | flops | bytes accessed | tf_op | source)
XLA Modules:
  0.0 182.5 jit_solution(17285837471791346190)
XLA Ops:
  7.2 0.0 copy-start
  7.2 0.0 reduce-scatter.3.cloned.1.call-start
  7.2 8.9 %collective-permute-start = (bf16[320,384]{1,0:T(8,128)(2,1)}, bf16[320,384]{1,0:T(8,128)(2,1)S(1)}, u32[]{:S(2)}, u32[]{:S(2)}) collective-permute-start(bf16[320,384]{1,0:T(8,128)(2,1)} %bitcast.55), channel_id=1, source_target_pairs={{0,1},{1,0},{2,3},{3,2},{4,5},{5,4},{6,7},{7,6},{8,9},{9,8},{10,11... | collective-permute-start | bytes 737288 | tf_op jit(solution)/shard_map/ppermute | solution.py:18
  16.2 1.3 collective-permute-done
  17.5 4.6 %fusion = bf16[2048,768]{0,1:T(8,128)(2,1)} fusion(bf16[1,1,320,2048]{3,2,1,0:T(8,128)(2,1)S(1)} %copy-done, bf16[320,384]{1,0:T(8,128)(2,1)} %bitcast.56, bf16[320,384]{1,0:T(8,128)(2,1)S(1)} %collective-permute-done, pred[]{:T(512)S(6)} %eq.89), kind=kOutput, calls=%fused_computation.3 | convolution fusion | flops 1011990528 | bytes 4947969 | tf_op jit(solution)/shard_map/dot_general | solution.py:71
  22.1 0.0 reduce-scatter.3.cloned.1.call-update
  22.1 0.7 copy-done.6
  22.7 0.1 copy.27
  22.8 0.1 eq.95
  22.9 0.1 eq.91
  23.0 1.2 reduce-window.6
  24.2 0.2 slice_reduce_fusion
  24.4 0.1 select_reduce_fusion.1
  24.6 0.1 add.76
  24.7 0.4 convert_reduce_fusion
  25.2 0.3 convolution_convert_fusion
  25.5 0.0 copy-start.4
  25.5 1.0 reshape.210
  26.5 4.3 %all-to-all-start = ((bf16[32,20,512]{2,1,0:T(8,128)(2,1)}), bf16[32,20,512]{2,1,0:T(8,128)(2,1)S(1)}, u32[]{:S(2)}, u32[]{:S(2)}) async-start(bf16[32,20,512]{2,1,0:T(8,128)(2,1)} %reshape.210), calls=%async_computation | async-start | bytes 1572864 | tf_op jit(solution)/shard_map/all_to_all | solution.py:28
  30.8 0.9 copy.26
  31.8 1.4 copy.30
  33.2 2.3 %copy.31 = f32[1,1,256,768]{2,3,1,0:T(8,128)} copy(f32[1,1,256,768]{3,2,1,0:T(8,128)} %param.14) | data formatting | bytes 1572864 | tf_op args[4]
  35.5 0.1 select_reduce_fusion.2
  35.6 16.5 %all-to-all-done = bf16[32,20,512]{2,1,0:T(8,128)(2,1)S(1)} async-done(((bf16[32,20,512]{2,1,0:T(8,128)(2,1)}), bf16[32,20,512]{2,1,0:T(8,128)(2,1)S(1)}, u32[]{:S(2)}, u32[]{:S(2)}) %all-to-all-start) | async-done | bytes 655392 | tf_op jit(solution)/shard_map/all_to_all | solution.py:28
  52.1 0.1 reshape.211
  52.2 0.9 broadcast_select_fusion
  53.1 15.8 %reduce-scatter.3.cloned.1.call-done = bf16[256,768]{0,1:T(8,128)(2,1)} async-done(((bf16[2048,768]{0,1:T(8,128)(2,1)}), bf16[256,768]{0,1:T(8,128)(2,1)}) %reduce-scatter.3.cloned.1.call-update) | async-done | bytes 393232 | tf_op jit(solution)/shard_map/reduce_scatter | solution.py:74
  69.0 2.0 %fusion.4 = bf16[256,768]{0,1:T(8,128)(2,1)S(1)} fusion(bf16[256,768]{0,1:T(8,128)(2,1)S(1)} %bitcast.51, bf16[256,768]{0,1:T(8,128)(2,1)} %reduce-scatter.3.cloned.1.call-done, f32[1,1,256,768]{2,3,1,0:T(8,128)} %copy.31, f32[1,1,256,768]{2,3,1,0:T(8,128)S(1)} %copy.30), kind=kLoop, calls=%fused_computation.17 | loop fusion | flops 3538944 | bytes 2752512 | tf_op jit(solution)/shard_map/convert_element_type | solution.py:106
  70.9 5.2 %collective-permute-start.2 = (bf16[256,768]{0,1:T(8,128)(2,1)S(1)}, bf16[256,768]{0,1:T(8,128)(2,1)S(1)}, u32[]{:S(2)}, u32[]{:S(2)}) collective-permute-start(bf16[256,768]{0,1:T(8,128)(2,1)S(1)} %fusion.4), channel_id=1, source_target_pairs={{0,1},{1,0},{2,3},{3,2},{4,5},{5,4},{6,7},{7,6},{8,9},{9,8},{10,11... | collective-permute-start | bytes 1179656 | tf_op jit(solution)/shard_map/ppermute | solution.py:18
  76.2 0.1 convert_reduce_fusion.1
  76.2 0.1 reshape.213
  76.4 0.1 rev.3
  76.4 0.9 copy.32
  77.4 9.2 %all-to-all-start.1 = ((bf16[32,8,768]{2,1,0:T(8,128)(2,1)}), bf16[32,8,768]{2,1,0:T(8,128)(2,1)S(1)}, u32[]{:S(2)}, u32[]{:S(2)}) async-start(bf16[32,8,768]{2,1,0:T(8,128)(2,1)} %bitcast.7), calls=%async_computation.2 | async-start | bytes 786432 | tf_op jit(solution)/shard_map/all_to_all | solution.py:28
  86.6 0.0 reduce-scatter.5.cloned.1.call-start
  86.6 0.5 fusion.31
  87.1 0.0 collective-permute-done.2
  87.2 0.4 copy-done.2
  87.5 1.5 multiply_convert_fusion.1
  89.0 0.0 reduce-scatter.5.cloned.1.call-update
  89.0 0.1 reshape.214
  89.2 0.0 copy-start.8
  89.2 11.8 %all-to-all-done.1 = bf16[32,8,768]{2,1,0:T(8,128)(2,1)S(1)} async-done(((bf16[32,8,768]{2,1,0:T(8,128)(2,1)}), bf16[32,8,768]{2,1,0:T(8,128)(2,1)S(1)}, u32[]{:S(2)}, u32[]{:S(2)}) %all-to-all-start.1) | async-done | bytes 393248 | tf_op jit(solution)/shard_map/all_to_all | solution.py:28
  101.0 1.5 gather_fusion
  102.5 4.4 %all-to-all-start.2 = ((bf16[32,16,768]{2,1,0:T(8,128)(2,1)}), bf16[32,16,768]{2,1,0:T(8,128)(2,1)S(1)}, u32[]{:S(2)}, u32[]{:S(2)}) async-start(bf16[32,16,768]{2,1,0:T(8,128)(2,1)} %bitcast.9), calls=%async_computation.3 | async-start | bytes 1572864 | tf_op jit(solution)/shard_map/all_to_all | solution.py:28
  106.9 0.1 copy.33
  107.0 0.1 reshape.219
  107.1 0.2 select_reduce_fusion
  107.3 0.1 mul.109
  107.5 20.1 %all-to-all-done.2 = bf16[32,16,768]{2,1,0:T(8,128)(2,1)S(1)} async-done(((bf16[32,16,768]{2,1,0:T(8,128)(2,1)}), bf16[32,16,768]{2,1,0:T(8,128)(2,1)S(1)}, u32[]{:S(2)}, u32[]{:S(2)}) %all-to-all-start.2) | async-done | bytes 786464 | tf_op jit(solution)/shard_map/all_to_all | solution.py:28
  127.6 1.1 copy.34
  128.6 0.7 reshape.217
  129.4 8.4 %all-to-all-start.3 = ((bf16[32,20,96]{2,1,0:T(8,128)(2,1)}), bf16[32,20,96]{2,1,0:T(8,128)(2,1)S(1)}, u32[]{:S(2)}, u32[]{:S(2)}) async-start(bf16[32,20,96]{2,1,0:T(8,128)(2,1)} %bitcast.13), calls=%async_computation.5 | async-start | bytes 393216 | tf_op jit(solution)/shard_map/all_to_all | solution.py:28
  137.8 0.1 slice_bitcast_fusion.1
  137.8 6.9 %collective-permute-start.1 = (bf16[256,768]{1,0:T(8,128)(2,1)S(1)}, bf16[256,768]{1,0:T(8,128)(2,1)S(1)}, u32[]{:S(2)}, u32[]{:S(2)}) collective-permute-start(bf16[256,768]{1,0:T(8,128)(2,1)S(1)} %get-tuple-element.16), channel_id=1, source_target_pairs={{0,1},{1,0},{2,3},{3,2},{4,5},{5,4},{6,7},{7,6},{8,9},{9,8},{10,11... | collective-permute-start | bytes 1179656 | tf_op jit(solution)/shard_map/ppermute | solution.py:18
  144.8 2.9 %all-to-all-done.3 = bf16[32,20,96]{2,1,0:T(8,128)(2,1)S(1)} async-done(((bf16[32,20,96]{2,1,0:T(8,128)(2,1)}), bf16[32,20,96]{2,1,0:T(8,128)(2,1)S(1)}, u32[]{:S(2)}, u32[]{:S(2)}) %all-to-all-start.3) | async-done | bytes 122912 | tf_op jit(solution)/shard_map/all_to_all | solution.py:28
  147.7 0.2 fusion.22
  147.9 1.4 gather_fusion.1
  149.3 10.2 %all-to-all-start.4 = ((bf16[64,20,96]{2,1,0:T(8,128)(2,1)}), bf16[64,20,96]{2,1,0:T(8,128)(2,1)S(1)}, u32[]{:S(2)}, u32[]{:S(2)}) async-start(bf16[64,20,96]{2,1,0:T(8,128)(2,1)} %gather_fusion.1), calls=%async_computation.6 | async-start | bytes 786432 | tf_op jit(solution)/shard_map/all_to_all | solution.py:22
  159.5 0.0 collective-permute-done.1
  159.5 1.0 maximum_select_fusion
  160.5 14.2 %all-to-all-done.4 = bf16[64,20,96]{2,1,0:T(8,128)(2,1)S(1)} async-done(((bf16[64,20,96]{2,1,0:T(8,128)(2,1)}), bf16[64,20,96]{2,1,0:T(8,128)(2,1)S(1)}, u32[]{:S(2)}, u32[]{:S(2)}) %all-to-all-start.4) | async-done | bytes 245792 | tf_op jit(solution)/shard_map/all_to_all | solution.py:22
  174.7 0.1 reshape.218
  174.8 0.9 copy.35
  (27 shorter events, 0.2 us)
Async XLA Ops:
  7.2 10.3 %copy-start = (bf16[1,1,320,2048]{3,2,1,0:T(8,128)(2,1)S(1)}, bf16[1,1,320,2048]{3,2,1,0:T(8,128)(2,1)}, u32[]{:S(2)}) copy-start(bf16[1,1,320,2048]{3,2,1,0:T(8,128)(2,1)} %param.10) | copy-start | bytes 3932164
  7.2 61.8 %reduce-scatter.3.cloned.1.call-start = ((), (), s32[]{:S(2)}) async-start(), calls=%async_computation.7 | async-start | bytes 3538944 | tf_op jit(solution)/shard_map/reduce_scatter | solution.py:74
  7.2 10.3 %collective-permute-start = (bf16[320,384]{1,0:T(8,128)(2,1)}, bf16[320,384]{1,0:T(8,128)(2,1)S(1)}, u32[]{:S(2)}, u32[]{:S(2)}) collective-permute-start(bf16[320,384]{1,0:T(8,128)(2,1)} %bitcast.55), channel_id=1, source_target_pairs={{0,1},{1,0},{2,3},{3,2},{4,5},{5,4},{6,7},{7,6},{8,9},{9,8},{10,11... | collective-permute-start | bytes 737288 | tf_op jit(solution)/shard_map/ppermute | solution.py:18
  22.0 0.7 copy-start.6
  22.0 2.4 %copy-start.7 = (s32[32]{0:T(128)S(1)}, s32[32]{0:T(128)}, u32[]{:S(2)}) copy-start(s32[32]{0:T(128)} %param.18) | copy-start | bytes 388
  22.1 2.6 %copy-start.5 = (bf16[64,2,256]{2,1,0:T(2,128)(2,1)S(1)}, bf16[64,2,256]{2,1,0:T(2,128)(2,1)}, u32[]{:S(2)}) copy-start(bf16[64,2,256]{2,1,0:T(2,128)(2,1)} %param.15) | copy-start | bytes 196612
  25.5 5.3 %copy-start.4 = (bf16[1,1,256,768]{3,2,1,0:T(8,128)(2,1)S(1)}, bf16[1,1,256,768]{3,2,1,0:T(8,128)(2,1)}, u32[]{:S(2)}) copy-start(bf16[1,1,256,768]{3,2,1,0:T(8,128)(2,1)} %param.12) | copy-start | bytes 1179652
  26.5 25.6 %all-to-all-start = ((bf16[32,20,512]{2,1,0:T(8,128)(2,1)}), bf16[32,20,512]{2,1,0:T(8,128)(2,1)S(1)}, u32[]{:S(2)}, u32[]{:S(2)}) async-start(bf16[32,20,512]{2,1,0:T(8,128)(2,1)} %reshape.210), calls=%async_computation | async-start | bytes 1572864 | tf_op jit(solution)/shard_map/all_to_all | solution.py:28
  31.8 3.7 %copy-start.9 = (s32[64]{0:T(128)S(1)}, s32[64]{0:T(128)}, u32[]{:S(2)}) copy-start(s32[64]{0:T(128)} %param.19) | copy-start | bytes 772
  52.2 16.7 %copy-start.1 = (bf16[1,1,256,768]{2,3,1,0:T(8,128)(2,1)S(1)}, bf16[1,1,256,768]{2,3,1,0:T(8,128)(2,1)}, u32[]{:S(2)}) copy-start(bf16[1,1,256,768]{2,3,1,0:T(8,128)(2,1)} %copy.26) | copy-start | bytes 1179652
  70.9 15.7 %copy-start.3 = (bf16[640,256]{1,0:T(8,128)(2,1)S(1)}, bf16[640,256]{1,0:T(8,128)(2,1)}, u32[]{:S(2)}) copy-start(bf16[640,256]{1,0:T(8,128)(2,1)} %get-tuple-element.7) | copy-start | bytes 983044
  70.9 16.2 %collective-permute-start.2 = (bf16[256,768]{0,1:T(8,128)(2,1)S(1)}, bf16[256,768]{0,1:T(8,128)(2,1)S(1)}, u32[]{:S(2)}, u32[]{:S(2)}) collective-permute-start(bf16[256,768]{0,1:T(8,128)(2,1)S(1)} %fusion.4), channel_id=1, source_target_pairs={{0,1},{1,0},{2,3},{3,2},{4,5},{5,4},{6,7},{7,6},{8,9},{9,8},{10,11... | collective-permute-start | bytes 1179656 | tf_op jit(solution)/shard_map/ppermute | solution.py:18
  77.4 23.7 %all-to-all-start.1 = ((bf16[32,8,768]{2,1,0:T(8,128)(2,1)}), bf16[32,8,768]{2,1,0:T(8,128)(2,1)S(1)}, u32[]{:S(2)}, u32[]{:S(2)}) async-start(bf16[32,8,768]{2,1,0:T(8,128)(2,1)} %bitcast.7), calls=%async_computation.2 | async-start | bytes 786432 | tf_op jit(solution)/shard_map/all_to_all | solution.py:28
  86.6 1.0 copy-start.2
  86.6 41.0 %reduce-scatter.5.cloned.1.call-start = ((), (), s32[]{:S(2)}) async-start(), calls=%async_computation.8 | async-start | bytes 1105920 | tf_op jit(solution)/shard_map/reduce_scatter | solution.py:117
  89.2 17.8 %copy-start.8 = (bf16[64,8]{0,1:T(8,128)(2,1)S(1)}, bf16[64,8]{0,1:T(8,128)(2,1)}, u32[]{:S(2)}) copy-start(bf16[64,8]{0,1:T(8,128)(2,1)} %param.17) | copy-start | bytes 3076
  102.5 25.1 %all-to-all-start.2 = ((bf16[32,16,768]{2,1,0:T(8,128)(2,1)}), bf16[32,16,768]{2,1,0:T(8,128)(2,1)S(1)}, u32[]{:S(2)}, u32[]{:S(2)}) async-start(bf16[32,16,768]{2,1,0:T(8,128)(2,1)} %bitcast.9), calls=%async_computation.3 | async-start | bytes 1572864 | tf_op jit(solution)/shard_map/all_to_all | solution.py:28
  129.4 18.3 %all-to-all-start.3 = ((bf16[32,20,96]{2,1,0:T(8,128)(2,1)}), bf16[32,20,96]{2,1,0:T(8,128)(2,1)S(1)}, u32[]{:S(2)}, u32[]{:S(2)}) async-start(bf16[32,20,96]{2,1,0:T(8,128)(2,1)} %bitcast.13), calls=%async_computation.5 | async-start | bytes 393216 | tf_op jit(solution)/shard_map/all_to_all | solution.py:28
  137.8 21.7 %collective-permute-start.1 = (bf16[256,768]{1,0:T(8,128)(2,1)S(1)}, bf16[256,768]{1,0:T(8,128)(2,1)S(1)}, u32[]{:S(2)}, u32[]{:S(2)}) collective-permute-start(bf16[256,768]{1,0:T(8,128)(2,1)S(1)} %get-tuple-element.16), channel_id=1, source_target_pairs={{0,1},{1,0},{2,3},{3,2},{4,5},{5,4},{6,7},{7,6},{8,9},{9,8},{10,11... | collective-permute-start | bytes 1179656 | tf_op jit(solution)/shard_map/ppermute | solution.py:18
  149.3 25.4 %all-to-all-start.4 = ((bf16[64,20,96]{2,1,0:T(8,128)(2,1)}), bf16[64,20,96]{2,1,0:T(8,128)(2,1)S(1)}, u32[]{:S(2)}, u32[]{:S(2)}) async-start(bf16[64,20,96]{2,1,0:T(8,128)(2,1)} %gather_fusion.1), calls=%async_computation.6 | async-start | bytes 786432 | tf_op jit(solution)/shard_map/all_to_all | solution.py:22
Sparse Core Ops, SparseCore 0:
  22.2 46.7 reduce-scatter.2
  90.3 36.2 reduce-scatter.4

commit v3 on v2

--- a/solution.py
+++ b/solution.py
@@ -1,8 +1,11 @@
+import functools
 import math
 
 import jax
 import jax.numpy as jnp
 from jax import lax
+from jax.experimental import pallas as pl
+from jax.experimental.pallas import tpu as pltpu
 from jax.sharding import PartitionSpec as P
 
 beta_one = 0.9
@@ -28,6 +31,77 @@
     return lax.all_to_all(
         x, "ep", split_axis=0, concat_axis=0, tiled=True, axis_index_groups=groups
     )
+
+
+def half_kernel(scale, side_ref, acts_ref, cotan_ref, *refs):
+    product = lax.dot_general(
+        acts_ref[...], cotan_ref[...], (((0,), (0,)), ((), ())), preferred_element_type=jnp.float32
+    )
+    refs[-1][...] = (product * scale).astype(jnp.bfloat16)
+
+
+def half_partial(side, acts, cotan, scale, filled=None):
+    depth, width = acts.shape
+    columns = cotan.shape[1]
+    tile = 512
+    more = [] if filled is None else [filled]
+    return pl.pallas_call(
+        functools.partial(half_kernel, scale),
+        grid_spec=pltpu.PrefetchScalarGridSpec(
+            num_scalar_prefetch=1,
+            grid=(width // tile,),
+            in_specs=[
+                pl.BlockSpec((depth, tile), lambda i, side: (0, i)),
+                pl.BlockSpec((depth, columns), lambda i, side: (0, 0)),
+            ]
+            + [pl.BlockSpec(memory_space=pl.ANY)] * len(more),
+            out_specs=pl.BlockSpec((tile, columns), lambda i, side: (i, side[0])),
+        ),
+        out_shape=jax.ShapeDtypeStruct((width, 2 * columns), jnp.bfloat16),
+        input_output_aliases={3: 0} if more else {},
+        compiler_params=pltpu.CompilerParams(vmem_limit_bytes=24 << 20),
+        cost_estimate=pl.CostEstimate(
+            flops=2 * depth * width * columns,
+            bytes_accessed=2 * (depth * width + depth * columns + width * columns),
+            transcendentals=0,
+        ),
+    )(side, acts, cotan, *more)
+
+
+def terms_kernel(scale, core_ref, own_ref, partner_ref, tokens_ref, out_ref):
+    core = core_ref[0]
+    depth = own_ref.shape[0]
+    own_at = pl.multiple_of(core * depth, depth)
+    partner_at = pl.multiple_of((1 - core) * depth, depth)
+    total = jnp.dot(
+        tokens_ref[:, pl.ds(own_at, depth)], own_ref[...], preferred_element_type=jnp.float32
+    ) + jnp.dot(
+        tokens_ref[:, pl.ds(partner_at, depth)],
+        partner_ref[...],
+        preferred_element_type=jnp.float32,
+    )
+    total = (total * scale).astype(jnp.bfloat16)
+    share = out_ref.shape[2]
+    for r in range(out_ref.shape[0]):
+        out_ref[r] = total[:, r * share : (r + 1) * share]
+
+
+def projected(core, own_weight, partner_weight, token_rows, scale, shares):
+    rows = token_rows.shape[0]
+    depth, width = own_weight.shape
+    in_vmem = pl.BlockSpec(memory_space=pltpu.VMEM)
+    return pl.pallas_call(
+        functools.partial(terms_kernel, scale),
+        in_specs=[pl.BlockSpec(memory_space=pltpu.SMEM), in_vmem, in_vmem, in_vmem],
+        out_specs=in_vmem,
+        out_shape=jax.ShapeDtypeStruct((shares, rows, width // shares), jnp.bfloat16),
+        compiler_params=pltpu.CompilerParams(vmem_limit_bytes=32 << 20),
+        cost_estimate=pl.CostEstimate(
+            flops=4 * rows * depth * width,
+            bytes_accessed=4 * depth * width + 4 * rows * depth + 2 * rows * width,
+            transcendentals=0,
+        ),
+    )(core, own_weight, partner_weight, token_rows)
 
 
 def body(
@@ -57,29 +131,23 @@
     expert_count = train_place.shape[0]
     capacity = min(row_count, row_count * top_count // expert_count + max(1, row_count // 16))
     pair_count = row_count * top_count
-    slot_count = expert_count * capacity
+    stride = -(-capacity // 8) * 8
+    slot_count = expert_count * stride
     expert_ids = jnp.arange(expert_count, dtype=jnp.int32)
     device_ids = jnp.arange(ep_count, dtype=jnp.int32)
 
     own_cotan = train_cotan[0, 0]
     partner_cotan = swapped(own_cotan)
-    full_cotan = jnp.where(
-        is_upper,
-        jnp.concatenate([partner_cotan, own_cotan], axis=1),
-        jnp.concatenate([own_cotan, partner_cotan], axis=1),
-    )
-    product = lax.dot_general(
-        acts_local, full_cotan, (((0,), (0,)), ((), ())), preferred_element_type=jnp.float32
-    )
-    summed = lax.psum_scatter(
-        (product * width_scale).astype(jnp.bfloat16), "rep", scatter_dimension=0, tiled=True
-    )
+    sides = core.astype(jnp.int32).reshape(1)
+    own_filled = half_partial(sides, acts_local, own_cotan, width_scale)
+    partials = half_partial(1 - sides, acts_local, partner_cotan, width_scale, own_filled)
+    summed = lax.psum_scatter(partials, "rep", scatter_dimension=0, tiled=True)
 
     chosen = routes.reshape(pair_count)
     picked = (chosen[:, None] == expert_ids[None, :]).astype(jnp.int32)
     position = jnp.sum((jnp.cumsum(picked, axis=0) - 1) * picked, axis=1)
     trainer = jnp.sum(picked * train_place[None, :], axis=1)
-    slot_of_pair = trainer * capacity + position
+    slot_of_pair = trainer * stride + position
     placing = jnp.arange(slot_count, dtype=jnp.int32)[:, None] == slot_of_pair[None, :]
     place_rows = jnp.sum(
         placing.reshape(slot_count, row_count, top_count).astype(jnp.int32), axis=2
@@ -89,15 +157,10 @@
     ).astype(jnp.bfloat16)
     gate_row = gate_weights.reshape(1, pair_count).astype(jnp.float32)
     slot_gates = jnp.sum(jnp.where(placing, gate_row, 0.0), axis=1)
-    recv_tokens = exchanged_chips(send_tokens.reshape(chip_count, capacity, -1))
+    recv_tokens = exchanged_chips(send_tokens.reshape(chip_count, stride, -1))
     recv_tokens = recv_tokens.reshape(slot_count, 2 * piece_rows)
-    lower_tokens, upper_tokens = recv_tokens[:, :piece_rows], recv_tokens[:, piece_rows:]
-    own_tokens = jnp.where(is_upper, upper_tokens, lower_tokens)
-    partner_tokens = jnp.where(is_upper, lower_tokens, upper_tokens)
-
-    weight_local, own_tokens, partner_tokens = lax.optimization_barrier(
-        (weight[0, 0], own_tokens, partner_tokens)
-    )
+
+    weight_local, recv_tokens = lax.optimization_barrier((weight[0, 0], recv_tokens))
     gradient = summed.astype(jnp.float32)
     first = beta_one * moment_one[0, 0] + (1.0 - beta_one) * gradient
     second = beta_two * moment_two[0, 0] + (1.0 - beta_two) * gradient * gradient
@@ -106,15 +169,11 @@
     new_weight = (weight_now - learn_rate * (update + decay_rate * weight_now)).astype(jnp.bfloat16)
 
     partner_weight = swapped(new_weight)
-    rows_last = (((0,), (1,)), ((), ()))
-    own_terms = lax.dot_general(
-        new_weight, own_tokens, rows_last, preferred_element_type=jnp.float32
-    )
-    partner_terms = lax.dot_general(
-        partner_weight, partner_tokens, rows_last, preferred_element_type=jnp.float32
-    )
-    terms = ((own_terms + partner_terms) * width_scale).astype(jnp.bfloat16)
-    preact_share = lax.psum_scatter(terms, "rep", scatter_dimension=0, tiled=True)
+    terms = projected(
+        sides, new_weight, partner_weight, recv_tokens, width_scale, rep_count
+    )
+    terms, new_weight = lax.optimization_barrier((terms, new_weight))
+    preact_share = lax.psum_scatter(terms, "rep", scatter_dimension=0, tiled=False)
 
     group_rows = piece_rows // chip_count
     spread = exchanged_chips(new_weight.reshape(chip_count, group_rows, hidden_width))
@@ -136,11 +195,9 @@
     )
 
     preact_share, arrived = lax.optimization_barrier((preact_share, arrived))
-    back = exchanged_chips(
-        jnp.transpose(preact_share.reshape(share_width, chip_count, capacity), (1, 2, 0))
-    )
+    back = exchanged_chips(preact_share.reshape(chip_count, stride, share_width))
     activation = (
-        slot_gates.reshape(chip_count, capacity, 1) * jax.nn.silu(back.astype(jnp.float32))
+        slot_gates.reshape(chip_count, stride, 1) * jax.nn.silu(back.astype(jnp.float32))
     ).astype(jnp.bfloat16)
     first_device = jnp.min(
         jnp.where(serve_place[None, :] == expert_ids[:, None], device_ids[None, :], ep_count),
@@ -150,12 +207,12 @@
         jnp.sum((first_device[None, :] == device_ids[:, None]).astype(jnp.int32), axis=1) > 0
     )
     padded = jnp.concatenate(
-        [activation, jnp.zeros((1, capacity, share_width), jnp.bfloat16)], axis=0
+        [activation, jnp.zeros((1, stride, share_width), jnp.bfloat16)], axis=0
     )
     send_acts = padded.at[jnp.where(is_first, served_from, chip_count)].get(
         mode="promise_in_bounds"
     )
-    out_acts = exchanged(send_acts)
+    out_acts = exchanged(send_acts)[:, :capacity]
     return (
         serving.reshape(1, 1, 2, piece_rows, hidden_width),
         out_acts.reshape(1, ep_count * capacity, share_width),

time: 183 us -> 182 us (level)
  blocking collectives: 0 us -> 26.2 us
  starting transfers between devices: 57.7 us -> 44.2 us
  waiting for transfers between devices: 82.7 us -> 73.2 us
  Pallas kernels: 0 us -> 9.4 us
  local copies, waits for them, and re-layouts: 14.6 us -> 7.97 us
  matrix products: 6.88 us -> 0.38 us
    all_to_all x0 -> x1, blocking collectives: none -> 26.2 us  [exchanged_chips(): lax.all_to_all(x, 'ep', split_axis=0, concat_axis=0, tiled=True, axis_ind...]
    pallas_call x0 -> x3, Pallas kernels: none -> 9.4 us  [the longest x2 6.09 us: half_partial(): pl.pallas_call(functools.partial(half_kernel, scale), grid_spec=pltpu.Pre...]
    all_to_all x4 -> x3, waiting for transfers between devices: 51.3 us -> 43.2 us  [exchanged_chips(): lax.all_to_all(x, 'ep', split_axis=0, concat_axis=0, tiled=True, axis_ind...]
    dot_general x3 -> x0, matrix products: 6.54 us -> none  [the longest x1 4.57 us: body(): lax.dot_general(acts_local, full_cotan, (((0,), (0,)), ((), ())), preferr...]
    all_to_all x4 -> x3, starting transfers between devices: 26.3 us -> 20.3 us  [exchanged_chips(): lax.all_to_all(x, 'ep', split_axis=0, concat_axis=0, tiled=True, axis_ind...]
    ppermute x3, starting transfers between devices: 21.1 us -> 16.3 us  [swapped(): lax.ppermute(x, 'ep', [(i, i ^ 1) for i in range(lax.axis_size('ep'))])]
    all_to_all x1, waiting for transfers between devices: 14.2 us -> 10.3 us  [exchanged(): return lax.all_to_all(x, 'ep', split_axis=0, concat_axis=0, tiled=True)]
    unnamed x26 -> x25, local copies, waits for them, and re-layouts: 6.66 us -> 3.86 us
  transfers between devices with their start and end apart: 10 -> 9, of which waited for: 7 -> 7; matrix products, arithmetic and copies ran while one was open for 10% -> 4% of each run, Pallas kernels for 0% -> 2%
where the time goes in v3:
time: 182 us
  waiting for transfers between devices  73.2 us (40%)
  starting transfers between devices  44.2 us (24%)
  blocking collectives  26.2 us (14%)
  between operations  14.3 us (8%)
  Pallas kernels  9.4 us (5%)
  local copies, waits for them, and re-layouts  7.97 us (4%)
  other arithmetic  5.91 us (3%)
    all_to_all x3, waiting for transfers between devices, exchanged_chips(): lax.all_to_all(x, 'ep', split_axis=0, concat_axis=0, tiled=True, axis_ind...  43.2 us
    all_to_all x1, blocking collectives, exchanged_chips(): lax.all_to_all(x, 'ep', split_axis=0, concat_axis=0, tiled=True, axis_ind...  26.2 us
    all_to_all x3, starting transfers between devices, exchanged_chips(): lax.all_to_all(x, 'ep', split_axis=0, concat_axis=0, tiled=True, axis_ind...  20.3 us
    reduce_scatter x1, waiting for transfers between devices, body(): summed = lax.psum_scatter(partials, 'rep', scatter_dimension=0, tiled=True)  16.8 us
    ppermute x3, starting transfers between devices, swapped(): lax.ppermute(x, 'ep', [(i, i ^ 1) for i in range(lax.axis_size('ep'))])  16.3 us
    all_to_all x1, waiting for transfers between devices, exchanged(): return lax.all_to_all(x, 'ep', split_axis=0, concat_axis=0, tiled=True)  10.3 us
    all_to_all x1, starting transfers between devices, exchanged(): return lax.all_to_all(x, 'ep', split_axis=0, concat_axis=0, tiled=True)  7.55 us
    pallas_call x2, Pallas kernels, half_partial(): pl.pallas_call(functools.partial(half_kernel, scale), grid_spec=pltpu.Pre...  6.09 us
  transfers between devices with their start and end apart: 9, of which 7 were waited for; matrix products, arithmetic and copies ran while one was open for 4% of the time, Pallas kernels for 2%

profile of v3, /device:TPU:1, one launch (start us, length us, event | category | flops | bytes accessed | tf_op | source)
XLA Modules:
  0.0 181.6 jit_solution(11530968204268501606)
XLA Ops:
  7.2 0.0 reduce-scatter.3.cloned.1.call-start
  7.2 8.8 %collective-permute-start = (bf16[320,384]{1,0:T(8,128)(2,1)}, bf16[320,384]{1,0:T(8,128)(2,1)S(1)}, u32[]{:S(2)}, u32[]{:S(2)}) collective-permute-start(bf16[320,384]{1,0:T(8,128)(2,1)} %bitcast.49), channel_id=1, source_target_pairs={{0,1},{1,0},{2,3},{3,2},{4,5},{5,4},{6,7},{7,6},{8,9},{9,8},{10,11... | collective-permute-start | bytes 737288 | tf_op jit(solution)/shard_map/ppermute | solution.py:21
  16.0 0.0 copy-start
  16.0 1.3 copy-done
  17.3 0.9 copy-done.2
  18.3 3.0 %shard_map.113.refs_0_ = bf16[2048,768]{1,0:T(8,128)(2,1)} custom-call(s32[1]{0:T(128)} %bitcast.side_ref.core_ref, bf16[320,2048]{1,0:T(8,128)(2,1)S(1)} %bitcast.46, bf16[320,384]{1,0:T(8,128)(2,1)S(1)} %bitcast.50), custom_call_target="tpu_custom_call" | custom-call | flops 503316480 | bytes 3129344 | tf_op jit(solution)/shard_map/pallas_call | solution.py:48
  21.3 0.0 collective-permute-done.cotan_ref
  21.3 0.0 copy-done.1
  21.3 3.1 %shard_map.114 = bf16[2048,768]{1,0:T(8,128)(2,1)} custom-call(s32[1]{0:T(128)S(6)} %sub.17.side_ref, bf16[320,2048]{1,0:T(8,128)(2,1)S(1)} %bitcast.47, bf16[320,384]{1,0:T(8,128)(2,1)S(1)} %collective-permute-done.cotan_ref, bf16[2048,768]{1,0:T(8,128)(2,1)} %shard_map.113.refs_0_), custom_call_target="tpu_custom_call", output_to_operand_aliasing={{}: (3, {})} | custom-call | flops 503316480 | bytes 3129344 | tf_op jit(solution)/shard_map/pallas_call | solution.py:48
  24.4 0.0 reduce-scatter.3.cloned.1.call-update
  24.4 0.0 reduce-scatter.5.cloned.1.call-start
  24.5 0.6 copy-done.7
  25.1 0.1 copy.19
  25.1 0.1 eq.95
  25.2 0.1 eq.91
  25.3 1.2 reduce-window.6
  26.5 0.2 slice_reduce_fusion
  26.7 0.0 copy-start.3
  26.8 0.0 copy-start.4
  26.8 0.0 copy-start.5
  26.8 0.0 copy-done.8
  26.8 0.1 select_reduce_fusion.1
  26.9 0.1 add.73
  27.0 0.0 copy-done.6
  27.1 0.5 convert_reduce_fusion
  27.6 0.4 convolution_convert_fusion
  28.0 26.2 %all_to_all.25 = bf16[32,24,512]{2,1,0:T(8,128)(2,1)S(1)} all-to-all(bf16[32,24,512]{2,1,0:T(8,128)(2,1)S(1)} %bitcast.51), channel_id=1, replica_groups={{0,2,4,6,8,10,12,14,16,18,20,22,24,26,28,30,32,34,36,38,40,42,44,46,48,..., dimensions={0} | all-to-all | bytes 1572864 | tf_op jit(solution)/shard_map/all_to_all | solution.py:31
  54.2 16.8 %reduce-scatter.3.cloned.1.call-done = bf16[256,768]{1,0:T(8,128)(2,1)} async-done(((bf16[2048,768]{1,0:T(8,128)(2,1)}), bf16[256,768]{1,0:T(8,128)(2,1)}) %reduce-scatter.3.cloned.1.call-update) | async-done | bytes 393232 | tf_op jit(solution)/shard_map/reduce_scatter | solution.py:144
  71.0 0.0 copy-done.3
  71.0 0.0 copy-done.4
  71.0 0.0 copy-done.5
  71.0 2.4 %fusion.2.own_ref = bf16[256,768]{1,0:T(8,128)(2,1)} fusion(bf16[256,768]{1,0:T(8,128)(2,1)S(1)} %bitcast.54, bf16[256,768]{1,0:T(8,128)(2,1)} %reduce-scatter.3.cloned.1.call-done, f32[1,1,256,768]{3,2,1,0:T(8,128)S(1)} %copy-done.3, f32[1,1,256,768]{3,2,1,0:T(8,128)S(1)} %copy-done.4), kind=kLoop, calls=%fused_computation.13 | loop fusion | flops 3538944 | bytes 2752512 | tf_op jit(solution)/shard_map/convert_element_type | solution.py:169
  73.4 5.0 %collective-permute-start.1 = (bf16[256,768]{1,0:T(8,128)(2,1)}, bf16[256,768]{1,0:T(8,128)(2,1)S(1)}, u32[]{:S(2)}, u32[]{:S(2)}) collective-permute-start(bf16[256,768]{1,0:T(8,128)(2,1)} %fusion.2.own_ref), channel_id=1, source_target_pairs={{0,1},{1,0},{2,3},{3,2},{4,5},{5,4},{6,7},{7,6},{8,9},{9,8},{10,11... | collective-permute-start | bytes 1179656 | tf_op jit(solution)/shard_map/ppermute | solution.py:21
  78.4 1.5 collective-permute-done.1.partner_ref
  79.9 3.3 %shard_map.115 = bf16[8,768,96]{2,1,0:T(8,128)(2,1)} custom-call(s32[1]{0:T(128)} %bitcast.side_ref.core_ref, bf16[256,768]{1,0:T(8,128)(2,1)} %fusion.2.own_ref, bf16[256,768]{1,0:T(8,128)(2,1)S(1)} %collective-permute-done.1.partner_ref, bf16[768,512]{1,0:T(8,128)(2,1)S(1)} %bitcast.48), custom_call_target="tpu_custom_call" | custom-call | flops 603979776 | bytes 2752512 | tf_op jit(solution)/shard_map/pallas_call | solution.py:93
  83.2 0.0 reduce-scatter.5.cloned.1.call-update
  83.2 9.2 %all-to-all-start.1 = ((bf16[32,8,768]{2,1,0:T(8,128)(2,1)}), bf16[32,8,768]{2,1,0:T(8,128)(2,1)S(1)}, u32[]{:S(2)}, u32[]{:S(2)}) async-start(bf16[32,8,768]{2,1,0:T(8,128)(2,1)} %bitcast.9), calls=%async_computation.2 | async-start | bytes 786432 | tf_op jit(solution)/shard_map/all_to_all | solution.py:31
  92.5 0.1 select_reduce_fusion.2
  92.6 0.1 convert_reduce_fusion.1
  92.7 0.1 reshape.217
  92.8 0.1 rev.3
  92.9 0.1 reshape.218
  93.0 0.0 copy-start.9
  93.0 13.3 %all-to-all-done.1 = bf16[32,8,768]{2,1,0:T(8,128)(2,1)S(1)} async-done(((bf16[32,8,768]{2,1,0:T(8,128)(2,1)}), bf16[32,8,768]{2,1,0:T(8,128)(2,1)S(1)}, u32[]{:S(2)}, u32[]{:S(2)}) %all-to-all-start.1) | async-done | bytes 393248 | tf_op jit(solution)/shard_map/all_to_all | solution.py:31
  106.3 1.5 gather_fusion
  107.8 5.0 %all-to-all-start.2 = ((bf16[32,16,768]{2,1,0:T(8,128)(2,1)}), bf16[32,16,768]{2,1,0:T(8,128)(2,1)S(1)}, u32[]{:S(2)}, u32[]{:S(2)}) async-start(bf16[32,16,768]{2,1,0:T(8,128)(2,1)} %bitcast.11), calls=%async_computation.3 | async-start | bytes 1572864 | tf_op jit(solution)/shard_map/all_to_all | solution.py:31
  112.8 0.0 copy-done.9
  112.8 0.1 copy.22
  112.9 0.1 reshape.223
  113.0 0.2 select_reduce_fusion
  113.2 0.1 mul.94
  113.3 20.1 %all-to-all-done.2 = bf16[32,16,768]{2,1,0:T(8,128)(2,1)S(1)} async-done(((bf16[32,16,768]{2,1,0:T(8,128)(2,1)}), bf16[32,16,768]{2,1,0:T(8,128)(2,1)S(1)}, u32[]{:S(2)}, u32[]{:S(2)}) %all-to-all-start.2) | async-done | bytes 786464 | tf_op jit(solution)/shard_map/all_to_all | solution.py:31
  133.4 6.1 %all-to-all-start.3 = ((bf16[32,24,96]{2,1,0:T(8,128)(2,1)}), bf16[32,24,96]{2,1,0:T(8,128)(2,1)S(1)}, u32[]{:S(2)}, u32[]{:S(2)}) async-start(bf16[32,24,96]{2,1,0:T(8,128)(2,1)} %bitcast.56), calls=%async_computation.5 | async-start | bytes 393216 | tf_op jit(solution)/shard_map/all_to_all | solution.py:31
  139.6 9.8 %all-to-all-done.3 = bf16[32,24,96]{2,1,0:T(8,128)(2,1)S(1)} async-done(((bf16[32,24,96]{2,1,0:T(8,128)(2,1)}), bf16[32,24,96]{2,1,0:T(8,128)(2,1)S(1)}, u32[]{:S(2)}, u32[]{:S(2)}) %all-to-all-start.3) | async-done | bytes 147488 | tf_op jit(solution)/shard_map/all_to_all | solution.py:31
  149.4 0.2 fusion.14
  149.7 1.4 gather_fusion.1
  151.0 7.6 %all-to-all-start.4 = ((bf16[64,24,96]{2,1,0:T(8,128)(2,1)}), bf16[64,24,96]{2,1,0:T(8,128)(2,1)S(1)}, u32[]{:S(2)}, u32[]{:S(2)}) async-start(bf16[64,24,96]{2,1,0:T(8,128)(2,1)} %gather_fusion.1), calls=%async_computation.6 | async-start | bytes 786432 | tf_op jit(solution)/shard_map/all_to_all | solution.py:25
  158.6 0.1 slice_bitcast_fusion.1
  158.7 2.5 %collective-permute-start.2 = (bf16[256,768]{1,0:T(8,128)(2,1)S(1)}, bf16[256,768]{1,0:T(8,128)(2,1)S(1)}, u32[]{:S(2)}, u32[]{:S(2)}) collective-permute-start(bf16[256,768]{1,0:T(8,128)(2,1)S(1)} %get-tuple-element.18), channel_id=1, source_target_pairs={{0,1},{1,0},{2,3},{3,2},{4,5},{5,4},{6,7},{7,6},{8,9},{9,8},{10,11... | collective-permute-start | bytes 1179656 | tf_op jit(solution)/shard_map/ppermute | solution.py:21
  161.1 1.3 collective-permute-done.2
  162.5 1.0 maximum_select_fusion
  163.5 10.3 %all-to-all-done.4 = bf16[64,24,96]{2,1,0:T(8,128)(2,1)S(1)} async-done(((bf16[64,24,96]{2,1,0:T(8,128)(2,1)}), bf16[64,24,96]{2,1,0:T(8,128)(2,1)S(1)}, u32[]{:S(2)}, u32[]{:S(2)}) %all-to-all-start.4) | async-done | bytes 294944 | tf_op jit(solution)/shard_map/all_to_all | solution.py:25
  173.8 0.1 reshape.222
  173.9 0.9 copy.23
  (19 shorter events, 0.2 us)
Async XLA Ops:
  7.2 63.8 %reduce-scatter.3.cloned.1.call-start = ((), (), s32[]{:S(2)}) async-start(), calls=%async_computation.7 | async-start | bytes 3538944 | tf_op jit(solution)/shard_map/reduce_scatter | solution.py:144
  7.2 14.1 %collective-permute-start = (bf16[320,384]{1,0:T(8,128)(2,1)}, bf16[320,384]{1,0:T(8,128)(2,1)S(1)}, u32[]{:S(2)}, u32[]{:S(2)}) collective-permute-start(bf16[320,384]{1,0:T(8,128)(2,1)} %bitcast.49), channel_id=1, source_target_pairs={{0,1},{1,0},{2,3},{3,2},{4,5},{5,4},{6,7},{7,6},{8,9},{9,8},{10,11... | collective-permute-start | bytes 737288 | tf_op jit(solution)/shard_map/ppermute | solution.py:21
  16.0 1.3 copy-start
  17.3 0.9 copy-start.2
  18.3 3.0 %copy-start.1 = (bf16[1,1,320,2048]{3,2,1,0:T(8,128)(2,1)S(1)}, bf16[1,1,320,2048]{3,2,1,0:T(8,128)(2,1)}, u32[]{:S(2)}) copy-start(bf16[1,1,320,2048]{3,2,1,0:T(8,128)(2,1)} %param.10) | copy-start | bytes 3932164
  24.4 0.7 copy-start.7
  24.4 2.4 %copy-start.8 = (s32[32]{0:T(128)S(1)}, s32[32]{0:T(128)}, u32[]{:S(2)}) copy-start(s32[32]{0:T(128)} %param.18) | copy-start | bytes 388
  24.4 2.6 %copy-start.6 = (bf16[64,2,256]{2,1,0:T(2,128)(2,1)S(1)}, bf16[64,2,256]{2,1,0:T(2,128)(2,1)}, u32[]{:S(2)}) copy-start(bf16[64,2,256]{2,1,0:T(2,128)(2,1)} %param.15) | copy-start | bytes 196612
  24.4 109.0 %reduce-scatter.5.cloned.1.call-start = ((), (), s32[]{:S(2)}) async-start(), calls=%async_computation.8 | async-start | bytes 1769472 | tf_op jit(solution)/shard_map/reduce_scatter | solution.py:176
  26.7 44.2 %copy-start.3 = (f32[1,1,256,768]{3,2,1,0:T(8,128)S(1)}, f32[1,1,256,768]{3,2,1,0:T(8,128)}, u32[]{:S(2)}) copy-start(f32[1,1,256,768]{3,2,1,0:T(8,128)} %param.14) | copy-start | bytes 2359300
  26.8 44.2 %copy-start.4 = (f32[1,1,256,768]{3,2,1,0:T(8,128)S(1)}, f32[1,1,256,768]{3,2,1,0:T(8,128)}, u32[]{:S(2)}) copy-start(f32[1,1,256,768]{3,2,1,0:T(8,128)} %param.13) | copy-start | bytes 2359300
  26.8 44.2 %copy-start.5 = (bf16[1,1,256,768]{3,2,1,0:T(8,128)(2,1)S(1)}, bf16[1,1,256,768]{3,2,1,0:T(8,128)(2,1)}, u32[]{:S(2)}) copy-start(bf16[1,1,256,768]{3,2,1,0:T(8,128)(2,1)} %param.12) | copy-start | bytes 1179652
  73.4 6.5 %collective-permute-start.1 = (bf16[256,768]{1,0:T(8,128)(2,1)}, bf16[256,768]{1,0:T(8,128)(2,1)S(1)}, u32[]{:S(2)}, u32[]{:S(2)}) collective-permute-start(bf16[256,768]{1,0:T(8,128)(2,1)} %fusion.2.own_ref), channel_id=1, source_target_pairs={{0,1},{1,0},{2,3},{3,2},{4,5},{5,4},{6,7},{7,6},{8,9},{9,8},{10,11... | collective-permute-start | bytes 1179656 | tf_op jit(solution)/shard_map/ppermute | solution.py:21
  83.2 9.3 %copy-start.10 = (s32[64]{0:T(128)S(1)}, s32[64]{0:T(128)}, u32[]{:S(2)}) copy-start(s32[64]{0:T(128)} %param.19) | copy-start | bytes 772
  83.2 23.1 %all-to-all-start.1 = ((bf16[32,8,768]{2,1,0:T(8,128)(2,1)}), bf16[32,8,768]{2,1,0:T(8,128)(2,1)S(1)}, u32[]{:S(2)}, u32[]{:S(2)}) async-start(bf16[32,8,768]{2,1,0:T(8,128)(2,1)} %bitcast.9), calls=%async_computation.2 | async-start | bytes 786432 | tf_op jit(solution)/shard_map/all_to_all | solution.py:31
  93.0 19.8 %copy-start.9 = (bf16[64,8]{0,1:T(8,128)(2,1)S(1)}, bf16[64,8]{0,1:T(8,128)(2,1)}, u32[]{:S(2)}) copy-start(bf16[64,8]{0,1:T(8,128)(2,1)} %param.17) | copy-start | bytes 3076
  107.8 25.6 %all-to-all-start.2 = ((bf16[32,16,768]{2,1,0:T(8,128)(2,1)}), bf16[32,16,768]{2,1,0:T(8,128)(2,1)S(1)}, u32[]{:S(2)}, u32[]{:S(2)}) async-start(bf16[32,16,768]{2,1,0:T(8,128)(2,1)} %bitcast.11), calls=%async_computation.3 | async-start | bytes 1572864 | tf_op jit(solution)/shard_map/all_to_all | solution.py:31
  133.4 16.0 %all-to-all-start.3 = ((bf16[32,24,96]{2,1,0:T(8,128)(2,1)}), bf16[32,24,96]{2,1,0:T(8,128)(2,1)S(1)}, u32[]{:S(2)}, u32[]{:S(2)}) async-start(bf16[32,24,96]{2,1,0:T(8,128)(2,1)} %bitcast.56), calls=%async_computation.5 | async-start | bytes 393216 | tf_op jit(solution)/shard_map/all_to_all | solution.py:31
  151.0 22.7 %all-to-all-start.4 = ((bf16[64,24,96]{2,1,0:T(8,128)(2,1)}), bf16[64,24,96]{2,1,0:T(8,128)(2,1)S(1)}, u32[]{:S(2)}, u32[]{:S(2)}) async-start(bf16[64,24,96]{2,1,0:T(8,128)(2,1)} %gather_fusion.1), calls=%async_computation.6 | async-start | bytes 786432 | tf_op jit(solution)/shard_map/all_to_all | solution.py:25
  158.7 3.8 %collective-permute-start.2 = (bf16[256,768]{1,0:T(8,128)(2,1)S(1)}, bf16[256,768]{1,0:T(8,128)(2,1)S(1)}, u32[]{:S(2)}, u32[]{:S(2)}) collective-permute-start(bf16[256,768]{1,0:T(8,128)(2,1)S(1)} %get-tuple-element.18), channel_id=1, source_target_pairs={{0,1},{1,0},{2,3},{3,2},{4,5},{5,4},{6,7},{7,6},{8,9},{9,8},{10,11... | collective-permute-start | bytes 1179656 | tf_op jit(solution)/shard_map/ppermute | solution.py:21
Sparse Core Ops, SparseCore 0:
  24.5 46.3 reduce-scatter.2
  83.4 38.3 reduce-scatter.4

commit v4 on v2

--- a/solution.py
+++ b/solution.py
@@ -1,8 +1,12 @@
+import functools
 import math
 
 import jax
 import jax.numpy as jnp
 from jax import lax
+from jax.experimental import pallas as pl
+from jax.experimental.layout import Layout, with_layout_constraint
+from jax.experimental.pallas import tpu as pltpu
 from jax.sharding import PartitionSpec as P
 
 beta_one = 0.9
@@ -28,6 +32,34 @@
     return lax.all_to_all(
         x, "ep", split_axis=0, concat_axis=0, tiled=True, axis_index_groups=groups
     )
+
+
+def terms_kernel(scale, weight_ref, tokens_ref, out_ref):
+    cores = tokens_ref.shape[0]
+    share = out_ref.shape[2]
+    for core in range(cores):
+        total = jnp.dot(tokens_ref[core], weight_ref[...], preferred_element_type=jnp.float32)
+        total = (total * scale).astype(jnp.bfloat16)
+        for r in range(out_ref.shape[0] // cores):
+            out_ref[cores * r + core] = total[:, r * share : (r + 1) * share]
+
+
+def projected(weight_rows, token_rows, scale, shares):
+    cores, rows, depth = token_rows.shape
+    width = weight_rows.shape[1]
+    in_vmem = pl.BlockSpec(memory_space=pltpu.VMEM)
+    return pl.pallas_call(
+        functools.partial(terms_kernel, scale),
+        in_specs=[in_vmem, in_vmem],
+        out_specs=in_vmem,
+        out_shape=jax.ShapeDtypeStruct((cores * shares, rows, width // shares), jnp.bfloat16),
+        compiler_params=pltpu.CompilerParams(vmem_limit_bytes=60 << 20),
+        cost_estimate=pl.CostEstimate(
+            flops=2 * cores * rows * depth * width,
+            bytes_accessed=2 * (depth * width + cores * rows * (depth + width)),
+            transcendentals=0,
+        ),
+    )(weight_rows, token_rows)
 
 
 def body(
@@ -57,7 +89,8 @@
     expert_count = train_place.shape[0]
     capacity = min(row_count, row_count * top_count // expert_count + max(1, row_count // 16))
     pair_count = row_count * top_count
-    slot_count = expert_count * capacity
+    stride = -(-capacity // 8) * 8
+    slot_count = expert_count * stride
     expert_ids = jnp.arange(expert_count, dtype=jnp.int32)
     device_ids = jnp.arange(ep_count, dtype=jnp.int32)
 
@@ -71,33 +104,34 @@
     product = lax.dot_general(
         acts_local, full_cotan, (((0,), (0,)), ((), ())), preferred_element_type=jnp.float32
     )
-    summed = lax.psum_scatter(
-        (product * width_scale).astype(jnp.bfloat16), "rep", scatter_dimension=0, tiled=True
-    )
+    partials = with_layout_constraint(
+        (product * width_scale).astype(jnp.bfloat16), Layout(major_to_minor=(0, 1))
+    )
+    summed = lax.psum_scatter(partials, "rep", scatter_dimension=0, tiled=True)
 
     chosen = routes.reshape(pair_count)
     picked = (chosen[:, None] == expert_ids[None, :]).astype(jnp.int32)
     position = jnp.sum((jnp.cumsum(picked, axis=0) - 1) * picked, axis=1)
     trainer = jnp.sum(picked * train_place[None, :], axis=1)
-    slot_of_pair = trainer * capacity + position
+    slot_of_pair = trainer * stride + position
     placing = jnp.arange(slot_count, dtype=jnp.int32)[:, None] == slot_of_pair[None, :]
     place_rows = jnp.sum(
         placing.reshape(slot_count, row_count, top_count).astype(jnp.int32), axis=2
     ).astype(jnp.bfloat16)
-    send_tokens = jnp.dot(
-        place_rows, tokens.reshape(row_count, -1), preferred_element_type=jnp.float32
-    ).astype(jnp.bfloat16)
+    halves = [
+        jnp.dot(place_rows, tokens[:, h, :], preferred_element_type=jnp.float32)
+        .astype(jnp.bfloat16)
+        .reshape(chip_count, stride, piece_rows)
+        for h in range(2)
+    ]
+    send_tokens = jnp.stack(halves, axis=1).reshape(ep_count, stride, piece_rows)
     gate_row = gate_weights.reshape(1, pair_count).astype(jnp.float32)
     slot_gates = jnp.sum(jnp.where(placing, gate_row, 0.0), axis=1)
-    recv_tokens = exchanged_chips(send_tokens.reshape(chip_count, capacity, -1))
-    recv_tokens = recv_tokens.reshape(slot_count, 2 * piece_rows)
-    lower_tokens, upper_tokens = recv_tokens[:, :piece_rows], recv_tokens[:, piece_rows:]
-    own_tokens = jnp.where(is_upper, upper_tokens, lower_tokens)
-    partner_tokens = jnp.where(is_upper, lower_tokens, upper_tokens)
-
-    weight_local, own_tokens, partner_tokens = lax.optimization_barrier(
-        (weight[0, 0], own_tokens, partner_tokens)
-    )
+    recv_tokens = jnp.transpose(
+        exchanged(send_tokens).reshape(chip_count, 2, stride, piece_rows), (1, 0, 2, 3)
+    ).reshape(2, slot_count, piece_rows)
+
+    weight_local, recv_tokens = lax.optimization_barrier((weight[0, 0], recv_tokens))
     gradient = summed.astype(jnp.float32)
     first = beta_one * moment_one[0, 0] + (1.0 - beta_one) * gradient
     second = beta_two * moment_two[0, 0] + (1.0 - beta_two) * gradient * gradient
@@ -105,16 +139,15 @@
     update = first / bias_one / (jnp.sqrt(second / bias_two) + adam_eps)
     new_weight = (weight_now - learn_rate * (update + decay_rate * weight_now)).astype(jnp.bfloat16)
 
-    partner_weight = swapped(new_weight)
-    rows_last = (((0,), (1,)), ((), ()))
-    own_terms = lax.dot_general(
-        new_weight, own_tokens, rows_last, preferred_element_type=jnp.float32
-    )
-    partner_terms = lax.dot_general(
-        partner_weight, partner_tokens, rows_last, preferred_element_type=jnp.float32
-    )
-    terms = ((own_terms + partner_terms) * width_scale).astype(jnp.bfloat16)
-    preact_share = lax.psum_scatter(terms, "rep", scatter_dimension=0, tiled=True)
+    terms = projected(new_weight, recv_tokens, width_scale, rep_count)
+    terms, new_weight = lax.optimization_barrier((terms, new_weight))
+    chips = [
+        [r * ep_count + 2 * chip + c for r in range(rep_count) for c in range(2)]
+        for chip in range(chip_count)
+    ]
+    preact_share = lax.psum_scatter(
+        terms, ("rep", "ep"), scatter_dimension=0, tiled=False, axis_index_groups=chips
+    )
 
     group_rows = piece_rows // chip_count
     spread = exchanged_chips(new_weight.reshape(chip_count, group_rows, hidden_width))
@@ -136,11 +169,9 @@
     )
 
     preact_share, arrived = lax.optimization_barrier((preact_share, arrived))
-    back = exchanged_chips(
-        jnp.transpose(preact_share.reshape(share_width, chip_count, capacity), (1, 2, 0))
-    )
+    back = exchanged_chips(preact_share.reshape(chip_count, stride, share_width))
     activation = (
-        slot_gates.reshape(chip_count, capacity, 1) * jax.nn.silu(back.astype(jnp.float32))
+        slot_gates.reshape(chip_count, stride, 1) * jax.nn.silu(back.astype(jnp.float32))
     ).astype(jnp.bfloat16)
     first_device = jnp.min(
         jnp.where(serve_place[None, :] == expert_ids[:, None], device_ids[None, :], ep_count),
@@ -150,12 +181,12 @@
         jnp.sum((first_device[None, :] == device_ids[:, None]).astype(jnp.int32), axis=1) > 0
     )
     padded = jnp.concatenate(
-        [activation, jnp.zeros((1, capacity, share_width), jnp.bfloat16)], axis=0
+        [activation, jnp.zeros((1, stride, share_width), jnp.bfloat16)], axis=0
     )
     send_acts = padded.at[jnp.where(is_first, served_from, chip_count)].get(
         mode="promise_in_bounds"
     )
-    out_acts = exchanged(send_acts)
+    out_acts = exchanged(send_acts)[:, :capacity]
     return (
         serving.reshape(1, 1, 2, piece_rows, hidden_width),
         out_acts.reshape(1, ep_count * capacity, share_width),

time: 183 us -> 193 us (1.055)
  blocking collectives: 0 us -> 27.8 us
  starting transfers between devices: 57.7 us -> 43.2 us
  local copies, waits for them, and re-layouts: 14.6 us -> 6.74 us
  Pallas kernels: 0 us -> 4.44 us
    all_to_all x0 -> x1, blocking collectives: none -> 27.8 us  [exchanged(): return lax.all_to_all(x, 'ep', split_axis=0, concat_axis=0, tiled=True)]
    reduce_scatter x2, waiting for transfers between devices: 15.8 us -> 33.6 us  [the longest x1 19.5 us: body(): lax.psum_scatter(terms, ('rep', 'ep'), scatter_dimension=0, tiled=False,...]
    all_to_all x4 -> x3, waiting for transfers between devices: 51.3 us -> 37.7 us  [exchanged_chips(): lax.all_to_all(x, 'ep', split_axis=0, concat_axis=0, tiled=True, axis_ind...]
    ppermute x3 -> x2, starting transfers between devices: 21.1 us -> 11.4 us  [swapped(): lax.ppermute(x, 'ep', [(i, i ^ 1) for i in range(lax.axis_size('ep'))])]
    unnamed x26 -> x20, local copies, waits for them, and re-layouts: 6.66 us -> 1.6 us
    pallas_call x0 -> x1, Pallas kernels: none -> 4.44 us  [projected(): pl.pallas_call(functools.partial(terms_kernel, scale), in_specs=[in_vmem,...]
    all_to_all x1, waiting for transfers between devices: 14.2 us -> 10.3 us  [exchanged(): return lax.all_to_all(x, 'ep', split_axis=0, concat_axis=0, tiled=True)]
    all_to_all x4 -> x3, starting transfers between devices: 26.3 us -> 22.7 us  [exchanged_chips(): lax.all_to_all(x, 'ep', split_axis=0, concat_axis=0, tiled=True, axis_ind...]
  transfers between devices with their start and end apart: 10 -> 8, of which waited for: 7 -> 8; matrix products, arithmetic and copies ran while one was open for 10% -> 4% of each run, Pallas kernels for 0% -> 0%
where the time goes in v4:
time: 193 us; the launch traced here: 192 us
  waiting for transfers between devices  84.2 us (44%)
  starting transfers between devices  43.2 us (22%)
  blocking collectives  27.8 us (14%)
  between operations  14.3 us (7%)
  local copies, waits for them, and re-layouts  6.74 us (3%)
  other arithmetic  5.99 us (3%)
  matrix products  5.16 us (3%)
  Pallas kernels  4.44 us (2%)
    all_to_all x3, waiting for transfers between devices, exchanged_chips(): lax.all_to_all(x, 'ep', split_axis=0, concat_axis=0, tiled=True, axis_ind...  37.7 us
    all_to_all x1, blocking collectives, exchanged(): return lax.all_to_all(x, 'ep', split_axis=0, concat_axis=0, tiled=True)  27.8 us
    all_to_all x3, starting transfers between devices, exchanged_chips(): lax.all_to_all(x, 'ep', split_axis=0, concat_axis=0, tiled=True, axis_ind...  22.7 us
    reduce_scatter x1, waiting for transfers between devices, body(): lax.psum_scatter(terms, ('rep', 'ep'), scatter_dimension=0, tiled=False,...  19.5 us
    reduce_scatter x1, waiting for transfers between devices, body(): summed = lax.psum_scatter(partials, 'rep', scatter_dimension=0, tiled=True)  14.1 us
    ppermute x2, starting transfers between devices, swapped(): lax.ppermute(x, 'ep', [(i, i ^ 1) for i in range(lax.axis_size('ep'))])  11.4 us
    all_to_all x1, waiting for transfers between devices, exchanged(): return lax.all_to_all(x, 'ep', split_axis=0, concat_axis=0, tiled=True)  10.3 us
    all_to_all x1, starting transfers between devices, exchanged(): return lax.all_to_all(x, 'ep', split_axis=0, concat_axis=0, tiled=True)  9.08 us
  transfers between devices with their start and end apart: 8, of which 8 were waited for; matrix products, arithmetic and copies ran while one was open for 4% of the time, Pallas kernels for 0%

profile of v4, /device:TPU:1, one launch (start us, length us, event | category | flops | bytes accessed | tf_op | source)
XLA Modules:
  0.0 191.9 jit_solution(9193438453188300438)
XLA Ops:
  7.2 0.0 copy-start
  7.2 0.0 reduce-scatter.3.cloned.1.call-start
  7.2 8.9 %collective-permute-start = (bf16[320,384]{1,0:T(8,128)(2,1)}, bf16[320,384]{1,0:T(8,128)(2,1)S(1)}, u32[]{:S(2)}, u32[]{:S(2)}) collective-permute-start(bf16[320,384]{1,0:T(8,128)(2,1)} %bitcast.70), channel_id=1, source_target_pairs={{0,1},{1,0},{2,3},{3,2},{4,5},{5,4},{6,7},{7,6},{8,9},{9,8},{10,11... | collective-permute-start | bytes 737288 | tf_op jit(solution)/shard_map/ppermute | solution.py:22
  16.2 1.3 collective-permute-done
  17.5 0.0 copy-done
  17.5 4.6 %fusion = bf16[2048,768]{1,0:T(8,128)(2,1)} fusion(bf16[1,1,320,2048]{3,2,1,0:T(8,128)(2,1)S(1)} %copy-done, bf16[320,384]{1,0:T(8,128)(2,1)} %bitcast.71, bf16[320,384]{1,0:T(8,128)(2,1)S(1)} %collective-permute-done, pred[]{:T(512)S(6)} %eq.89), kind=kOutput, calls=%fused_computation.3 | convolution fusion | flops 1011990528 | bytes 4947969 | tf_op jit(solution)/shard_map/dot_general | solution.py:104
  22.1 0.0 reduce-scatter.3.cloned.1.call-update
  22.1 0.0 reduce-scatter.5.cloned.1.call-start
  22.1 0.6 copy-done.5
  22.7 0.1 copy.23
  22.8 0.1 eq.95
  22.9 0.1 eq.91
  23.0 1.2 reduce-window.6
  24.2 0.2 slice_reduce_fusion
  24.5 0.0 copy-done.6
  24.5 0.1 select_reduce_fusion.1
  24.6 0.1 add.73
  24.7 0.5 convert_reduce_fusion
  25.2 0.0 copy-done.4
  25.2 0.1 fusion.32
  25.3 0.3 convolution_convert_fusion
  25.6 0.3 convolution_convert_fusion.1
  25.9 0.1 pad_maximum_fusion
  26.0 0.0 copy-start.1
  26.0 0.0 copy-start.2
  26.0 0.0 copy-start.3
  26.0 27.8 %all_to_all.25 = bf16[64,24,256]{2,1,0:T(8,128)(2,1)S(1)} all-to-all(bf16[64,24,256]{2,1,0:T(8,128)(2,1)S(1)} %bitcast.61), channel_id=1, replica_groups=mesh['rep'=8,'ep'=64] {'ep'}, dimensions={0} | all-to-all | bytes 1572864 | tf_op jit(solution)/shard_map/all_to_all | solution.py:26
  53.8 0.9 copy.30
  54.8 14.1 %reduce-scatter.3.cloned.1.call-done = bf16[256,768]{1,0:T(8,128)(2,1)} async-done(((bf16[2048,768]{1,0:T(8,128)(2,1)}), bf16[256,768]{1,0:T(8,128)(2,1)}) %reduce-scatter.3.cloned.1.call-update) | async-done | bytes 393232 | tf_op jit(solution)/shard_map/reduce_scatter | solution.py:110
  68.9 0.0 copy-done.1
  68.9 0.0 copy-done.2
  68.9 0.0 copy-done.3
  68.9 2.4 %fusion.4.weight_ref = bf16[256,768]{1,0:T(8,128)(2,1)} fusion(bf16[256,768]{1,0:T(8,128)(2,1)S(1)} %bitcast.68, bf16[256,768]{1,0:T(8,128)(2,1)} %reduce-scatter.3.cloned.1.call-done, f32[1,1,256,768]{3,2,1,0:T(8,128)S(1)} %copy-done.1, f32[1,1,256,768]{3,2,1,0:T(8,128)S(1)} %copy-done.2), kind=kLoop, calls=%fused_computation.17 | loop fusion | flops 3538944 | bytes 2752512 | tf_op jit(solution)/shard_map/convert_element_type | solution.py:140
  71.3 4.4 %shard_map.113 = bf16[16,768,96]{2,1,0:T(8,128)(2,1)} custom-call(bf16[256,768]{1,0:T(8,128)(2,1)} %fusion.4.weight_ref, bf16[2,768,256]{2,1,0:T(8,128)(2,1)} %bitcast.63), custom_call_target="tpu_custom_call" | custom-call | flops 603979776 | bytes 3538944 | tf_op jit(solution)/shard_map/pallas_call | solution.py:51
  75.7 0.0 reduce-scatter.5.cloned.1.call-update
  75.7 9.2 %all-to-all-start.1 = ((bf16[32,8,768]{2,1,0:T(8,128)(2,1)}), bf16[32,8,768]{2,1,0:T(8,128)(2,1)S(1)}, u32[]{:S(2)}, u32[]{:S(2)}) async-start(bf16[32,8,768]{2,1,0:T(8,128)(2,1)} %bitcast.17), calls=%async_computation.2 | async-start | bytes 786432 | tf_op jit(solution)/shard_map/all_to_all | solution.py:32
  85.0 0.0 copy-done.8
  85.0 0.1 select_reduce_fusion.2
  85.1 0.1 convert_reduce_fusion.1
  85.2 0.1 reshape.213
  85.3 0.1 rev.3
  85.4 0.1 reshape.214
  85.5 0.0 copy-start.7
  85.5 10.9 %all-to-all-done.1 = bf16[32,8,768]{2,1,0:T(8,128)(2,1)S(1)} async-done(((bf16[32,8,768]{2,1,0:T(8,128)(2,1)}), bf16[32,8,768]{2,1,0:T(8,128)(2,1)S(1)}, u32[]{:S(2)}, u32[]{:S(2)}) %all-to-all-start.1) | async-done | bytes 393248 | tf_op jit(solution)/shard_map/all_to_all | solution.py:32
  96.5 1.5 gather_fusion
  97.9 4.4 %all-to-all-start.2 = ((bf16[32,16,768]{2,1,0:T(8,128)(2,1)}), bf16[32,16,768]{2,1,0:T(8,128)(2,1)S(1)}, u32[]{:S(2)}, u32[]{:S(2)}) async-start(bf16[32,16,768]{2,1,0:T(8,128)(2,1)} %bitcast.19), calls=%async_computation.3 | async-start | bytes 1572864 | tf_op jit(solution)/shard_map/all_to_all | solution.py:32
  102.3 0.1 copy.31
  102.4 0.1 reshape.219
  102.5 0.2 select_reduce_fusion
  102.7 0.1 mul.103
  102.8 17.0 %all-to-all-done.2 = bf16[32,16,768]{2,1,0:T(8,128)(2,1)S(1)} async-done(((bf16[32,16,768]{2,1,0:T(8,128)(2,1)}), bf16[32,16,768]{2,1,0:T(8,128)(2,1)S(1)}, u32[]{:S(2)}, u32[]{:S(2)}) %all-to-all-start.2) | async-done | bytes 786464 | tf_op jit(solution)/shard_map/all_to_all | solution.py:32
  119.8 19.5 %reduce-scatter.5.cloned.1.call-done = bf16[1,768,96]{2,1,0:T(8,128)(2,1)} async-done(((bf16[16,768,96]{2,1,0:T(8,128)(2,1)}), bf16[1,768,96]{2,1,0:T(8,128)(2,1)}) %reduce-scatter.5.cloned.1.call-update) | async-done | bytes 147472 | tf_op jit(solution)/shard_map/reduce_scatter | solution.py:148
  139.3 9.1 %all-to-all-start.3 = ((bf16[32,24,96]{2,1,0:T(8,128)(2,1)}), bf16[32,24,96]{2,1,0:T(8,128)(2,1)S(1)}, u32[]{:S(2)}, u32[]{:S(2)}) async-start(bf16[32,24,96]{2,1,0:T(8,128)(2,1)} %bitcast.69), calls=%async_computation.5 | async-start | bytes 393216 | tf_op jit(solution)/shard_map/all_to_all | solution.py:32
  148.3 9.8 %all-to-all-done.3 = bf16[32,24,96]{2,1,0:T(8,128)(2,1)S(1)} async-done(((bf16[32,24,96]{2,1,0:T(8,128)(2,1)}), bf16[32,24,96]{2,1,0:T(8,128)(2,1)S(1)}, u32[]{:S(2)}, u32[]{:S(2)}) %all-to-all-start.3) | async-done | bytes 147488 | tf_op jit(solution)/shard_map/all_to_all | solution.py:32
  158.2 0.2 fusion.22
  158.4 1.4 gather_fusion.1
  159.8 9.1 %all-to-all-start.4 = ((bf16[64,24,96]{2,1,0:T(8,128)(2,1)}), bf16[64,24,96]{2,1,0:T(8,128)(2,1)S(1)}, u32[]{:S(2)}, u32[]{:S(2)}) async-start(bf16[64,24,96]{2,1,0:T(8,128)(2,1)} %gather_fusion.1), calls=%async_computation.6 | async-start | bytes 786432 | tf_op jit(solution)/shard_map/all_to_all | solution.py:26
  168.9 0.1 slice_bitcast_fusion.1
  168.9 2.5 %collective-permute-start.1 = (bf16[256,768]{1,0:T(8,128)(2,1)S(1)}, bf16[256,768]{1,0:T(8,128)(2,1)S(1)}, u32[]{:S(2)}, u32[]{:S(2)}) collective-permute-start(bf16[256,768]{1,0:T(8,128)(2,1)S(1)} %get-tuple-element.18), channel_id=1, source_target_pairs={{0,1},{1,0},{2,3},{3,2},{4,5},{5,4},{6,7},{7,6},{8,9},{9,8},{10,11... | collective-permute-start | bytes 1179656 | tf_op jit(solution)/shard_map/ppermute | solution.py:22
  171.4 1.3 collective-permute-done.1
  172.7 1.0 maximum_select_fusion
  173.8 10.3 %all-to-all-done.4 = bf16[64,24,96]{2,1,0:T(8,128)(2,1)S(1)} async-done(((bf16[64,24,96]{2,1,0:T(8,128)(2,1)}), bf16[64,24,96]{2,1,0:T(8,128)(2,1)S(1)}, u32[]{:S(2)}, u32[]{:S(2)}) %all-to-all-start.4) | async-done | bytes 294944 | tf_op jit(solution)/shard_map/all_to_all | solution.py:26
  184.1 0.1 reshape.218
  184.2 0.9 copy.32
  (15 shorter events, 0.1 us)
Async XLA Ops:
  7.2 10.3 %copy-start = (bf16[1,1,320,2048]{3,2,1,0:T(8,128)(2,1)S(1)}, bf16[1,1,320,2048]{3,2,1,0:T(8,128)(2,1)}, u32[]{:S(2)}) copy-start(bf16[1,1,320,2048]{3,2,1,0:T(8,128)(2,1)} %param.10) | copy-start | bytes 3932164
  7.2 61.7 %reduce-scatter.3.cloned.1.call-start = ((), (), s32[]{:S(2)}) async-start(), calls=%async_computation.7 | async-start | bytes 3538944 | tf_op jit(solution)/shard_map/reduce_scatter | solution.py:110
  7.2 10.3 %collective-permute-start = (bf16[320,384]{1,0:T(8,128)(2,1)}, bf16[320,384]{1,0:T(8,128)(2,1)S(1)}, u32[]{:S(2)}, u32[]{:S(2)}) collective-permute-start(bf16[320,384]{1,0:T(8,128)(2,1)} %bitcast.70), channel_id=1, source_target_pairs={{0,1},{1,0},{2,3},{3,2},{4,5},{5,4},{6,7},{7,6},{8,9},{9,8},{10,11... | collective-permute-start | bytes 737288 | tf_op jit(solution)/shard_map/ppermute | solution.py:22
  22.1 0.7 copy-start.5
  22.1 2.4 %copy-start.6 = (s32[32]{0:T(128)S(1)}, s32[32]{0:T(128)}, u32[]{:S(2)}) copy-start(s32[32]{0:T(128)} %param.18) | copy-start | bytes 388
  22.1 3.2 %copy-start.4 = (bf16[64,2,256]{2,1,0:T(2,128)(2,1)S(1)}, bf16[64,2,256]{2,1,0:T(2,128)(2,1)}, u32[]{:S(2)}) copy-start(bf16[64,2,256]{2,1,0:T(2,128)(2,1)} %param.15) | copy-start | bytes 196612
  22.1 117.2 %reduce-scatter.5.cloned.1.call-start = ((), (), s32[]{:S(2)}) async-start(), calls=%async_computation.8 | async-start | bytes 3342336 | tf_op jit(solution)/shard_map/reduce_scatter | solution.py:148
  26.0 42.9 %copy-start.1 = (f32[1,1,256,768]{3,2,1,0:T(8,128)S(1)}, f32[1,1,256,768]{3,2,1,0:T(8,128)}, u32[]{:S(2)}) copy-start(f32[1,1,256,768]{3,2,1,0:T(8,128)} %param.14) | copy-start | bytes 2359300
  26.0 42.8 %copy-start.2 = (f32[1,1,256,768]{3,2,1,0:T(8,128)S(1)}, f32[1,1,256,768]{3,2,1,0:T(8,128)}, u32[]{:S(2)}) copy-start(f32[1,1,256,768]{3,2,1,0:T(8,128)} %param.13) | copy-start | bytes 2359300
  26.0 42.8 %copy-start.3 = (bf16[1,1,256,768]{3,2,1,0:T(8,128)(2,1)S(1)}, bf16[1,1,256,768]{3,2,1,0:T(8,128)(2,1)}, u32[]{:S(2)}) copy-start(bf16[1,1,256,768]{3,2,1,0:T(8,128)(2,1)} %param.12) | copy-start | bytes 1179652
  75.7 9.3 %copy-start.8 = (s32[64]{0:T(128)S(1)}, s32[64]{0:T(128)}, u32[]{:S(2)}) copy-start(s32[64]{0:T(128)} %param.19) | copy-start | bytes 772
  75.7 20.7 %all-to-all-start.1 = ((bf16[32,8,768]{2,1,0:T(8,128)(2,1)}), bf16[32,8,768]{2,1,0:T(8,128)(2,1)S(1)}, u32[]{:S(2)}, u32[]{:S(2)}) async-start(bf16[32,8,768]{2,1,0:T(8,128)(2,1)} %bitcast.17), calls=%async_computation.2 | async-start | bytes 786432 | tf_op jit(solution)/shard_map/all_to_all | solution.py:32
  85.5 16.8 %copy-start.7 = (bf16[64,8]{0,1:T(8,128)(2,1)S(1)}, bf16[64,8]{0,1:T(8,128)(2,1)}, u32[]{:S(2)}) copy-start(bf16[64,8]{0,1:T(8,128)(2,1)} %param.17) | copy-start | bytes 3076
  97.9 21.9 %all-to-all-start.2 = ((bf16[32,16,768]{2,1,0:T(8,128)(2,1)}), bf16[32,16,768]{2,1,0:T(8,128)(2,1)S(1)}, u32[]{:S(2)}, u32[]{:S(2)}) async-start(bf16[32,16,768]{2,1,0:T(8,128)(2,1)} %bitcast.19), calls=%async_computation.3 | async-start | bytes 1572864 | tf_op jit(solution)/shard_map/all_to_all | solution.py:32
  139.3 18.9 %all-to-all-start.3 = ((bf16[32,24,96]{2,1,0:T(8,128)(2,1)}), bf16[32,24,96]{2,1,0:T(8,128)(2,1)S(1)}, u32[]{:S(2)}, u32[]{:S(2)}) async-start(bf16[32,24,96]{2,1,0:T(8,128)(2,1)} %bitcast.69), calls=%async_computation.5 | async-start | bytes 393216 | tf_op jit(solution)/shard_map/all_to_all | solution.py:32
  159.8 24.3 %all-to-all-start.4 = ((bf16[64,24,96]{2,1,0:T(8,128)(2,1)}), bf16[64,24,96]{2,1,0:T(8,128)(2,1)S(1)}, u32[]{:S(2)}, u32[]{:S(2)}) async-start(bf16[64,24,96]{2,1,0:T(8,128)(2,1)} %gather_fusion.1), calls=%async_computation.6 | async-start | bytes 786432 | tf_op jit(solution)/shard_map/all_to_all | solution.py:26
  168.9 3.8 %collective-permute-start.1 = (bf16[256,768]{1,0:T(8,128)(2,1)S(1)}, bf16[256,768]{1,0:T(8,128)(2,1)S(1)}, u32[]{:S(2)}, u32[]{:S(2)}) collective-permute-start(bf16[256,768]{1,0:T(8,128)(2,1)S(1)} %get-tuple-element.18), channel_id=1, source_target_pairs={{0,1},{1,0},{2,3},{3,2},{4,5},{5,4},{6,7},{7,6},{8,9},{9,8},{10,11... | collective-permute-start | bytes 1179656 | tf_op jit(solution)/shard_map/ppermute | solution.py:22
Sparse Core Ops, SparseCore 0:
  22.2 46.5 reduce-scatter.2
  75.9 63.3 reduce-scatter.4

commit v5 on v1

--- a/solution.py
+++ b/solution.py
@@ -93,7 +93,9 @@
     send_tokens = jnp.stack(halves, axis=1).reshape(ep_count, capacity, -1)
     gate_row = gate_weights.reshape(1, pair_count).astype(jnp.float32)
     slot_gates = jnp.sum(jnp.where(placing, gate_row, 0.0), axis=1)
-    recv_tokens = exchanged(send_tokens).reshape(ep_count * capacity, -1)
+    recv_tokens = jnp.transpose(
+        exchanged(send_tokens).reshape(chip_count, 2, capacity, piece_rows), (1, 0, 2, 3)
+    ).reshape(2 * slot_count, piece_rows)
 
     weight_local, recv_tokens = lax.optimization_barrier((weight[0, 0], recv_tokens))
     gradient = summed.astype(jnp.float32)
@@ -109,7 +111,13 @@
         )
         * width_scale
     ).astype(jnp.bfloat16)
-    preact_share = lax.psum_scatter(terms, "rep", scatter_dimension=0, tiled=True)
+    half_share = lax.psum_scatter(terms, "rep", scatter_dimension=0, tiled=True)
+    even_rows, odd_rows = half_share[:, :slot_count], half_share[:, slot_count:]
+    partner_share = swapped(jnp.where(is_upper, even_rows, odd_rows))
+    own_share = jnp.where(is_upper, odd_rows, even_rows)
+    preact_share = (
+        own_share.astype(jnp.float32) + partner_share.astype(jnp.float32)
+    ).astype(jnp.bfloat16)
 
     group_rows = piece_rows // chip_count
     spread = exchanged_chips(new_weight.reshape(chip_count, group_rows, hidden_width))
@@ -118,8 +126,10 @@
     )
     from_pairs = served_from.reshape(chip_count, 2)
     from_order = jnp.where(is_upper, from_pairs[:, ::-1], from_pairs).reshape(ep_count)
-    payload = jnp.take(spread, from_order, axis=0).reshape(
-        chip_count, 2 * group_rows, hidden_width
+    payload = (
+        spread.at[from_order]
+        .get(mode="promise_in_bounds")
+        .reshape(chip_count, 2 * group_rows, hidden_width)
     )
     arrived = exchanged_chips(payload)
     own_half = arrived[:, :group_rows].reshape(piece_rows, hidden_width)
@@ -128,15 +138,11 @@
         is_upper, jnp.stack([other_half, own_half]), jnp.stack([own_half, other_half])
     )
 
-    preact_share, arrived = lax.optimization_barrier((preact_share, arrived))
-    back = exchanged(
-        jnp.transpose(preact_share.reshape(share_width, ep_count, capacity), (1, 2, 0))
-    )
-    preact = jnp.sum(
-        back.reshape(chip_count, 2, capacity, share_width).astype(jnp.float32), axis=1
+    back = exchanged_chips(
+        jnp.transpose(preact_share.reshape(share_width, chip_count, capacity), (1, 2, 0))
     )
     activation = (
-        slot_gates.reshape(chip_count, capacity, 1) * jax.nn.silu(preact)
+        slot_gates.reshape(chip_count, capacity, 1) * jax.nn.silu(back.astype(jnp.float32))
     ).astype(jnp.bfloat16)
     first_device = jnp.min(
         jnp.where(serve_place[None, :] == expert_ids[:, None], device_ids[None, :], ep_count),
@@ -145,18 +151,11 @@
     is_first = (
         jnp.sum((first_device[None, :] == device_ids[:, None]).astype(jnp.int32), axis=1) > 0
     )
-    choosing = (
-        (served_from[:, None] == jnp.arange(chip_count, dtype=jnp.int32)[None, :])
-        & is_first[:, None]
-    ).astype(jnp.bfloat16)
-    send_acts = (
-        jnp.dot(
-            choosing,
-            activation.reshape(chip_count, capacity * share_width),
-            preferred_element_type=jnp.float32,
-        )
-        .astype(jnp.bfloat16)
-        .reshape(ep_count, capacity, share_width)
+    padded = jnp.concatenate(
+        [activation, jnp.zeros((1, capacity, share_width), jnp.bfloat16)], axis=0
+    )
+    send_acts = padded.at[jnp.where(is_first, served_from, chip_count)].get(
+        mode="promise_in_bounds"
     )
     out_acts = exchanged(send_acts)
     return (

time: 179 us -> 177 us (0.989)
  waiting for transfers between devices: 87.5 us -> 78.5 us
  starting transfers between devices: 47.4 us -> 52.5 us
    reduce_scatter x1, waiting for transfers between devices: 0.01 us -> 14.4 us  [body(): half_share = lax.psum_scatter(terms, 'rep', scatter_dimension=0, tiled=True)]
    all_to_all x3 -> x2, waiting for transfers between devices: 44.2 us -> 32.2 us  [exchanged(): return lax.all_to_all(x, 'ep', split_axis=0, concat_axis=0, tiled=True)]
    all_to_all x3 -> x2, starting transfers between devices: 22.4 us -> 11.1 us  [exchanged(): return lax.all_to_all(x, 'ep', split_axis=0, concat_axis=0, tiled=True)]
    all_to_all x2 -> x3, starting transfers between devices: 13.7 us -> 23.3 us  [exchanged_chips(): lax.all_to_all(x, 'ep', split_axis=0, concat_axis=0, tiled=True, axis_ind...]
    all_to_all x2 -> x3, waiting for transfers between devices: 28.1 us -> 18.9 us  [exchanged_chips(): lax.all_to_all(x, 'ep', split_axis=0, concat_axis=0, tiled=True, axis_ind...]
    ppermute x2 -> x3, starting transfers between devices: 11.3 us -> 18 us  [swapped(): lax.ppermute(x, 'ep', [(i, i ^ 1) for i in range(lax.axis_size('ep'))])]
    reduce_scatter x1, waiting for transfers between devices: 13.9 us -> 11 us  [body(): lax.psum_scatter((product * width_scale).astype(jnp.bfloat16), 'rep', sca...]
    gather x1 -> x2, local copies, waits for them, and re-layouts: 0.6 us -> 2.84 us  [the longest x1 1.48 us: body(): payload = spread.at[from_order].get(mode='promise_in_bounds').reshape(chi...]
  transfers between devices with their start and end apart: 9 -> 10, of which waited for: 7 -> 8; matrix products, arithmetic and copies ran while one was open for 9% -> 12% of each run, Pallas kernels for 0% -> 0%
where the time goes in v5:
time: 177 us; the launch traced here: 176 us
  waiting for transfers between devices  78.5 us (44%)
  starting transfers between devices  52.5 us (30%)
  local copies, waits for them, and re-layouts  16.5 us (9%)
  between operations  14.4 us (8%)
  other arithmetic  7.36 us (4%)
  matrix products  7.14 us (4%)
    all_to_all x2, waiting for transfers between devices, exchanged(): return lax.all_to_all(x, 'ep', split_axis=0, concat_axis=0, tiled=True)  32.2 us
    all_to_all x3, starting transfers between devices, exchanged_chips(): lax.all_to_all(x, 'ep', split_axis=0, concat_axis=0, tiled=True, axis_ind...  23.3 us
    all_to_all x3, waiting for transfers between devices, exchanged_chips(): lax.all_to_all(x, 'ep', split_axis=0, concat_axis=0, tiled=True, axis_ind...  18.9 us
    ppermute x3, starting transfers between devices, swapped(): lax.ppermute(x, 'ep', [(i, i ^ 1) for i in range(lax.axis_size('ep'))])  18 us
    reduce_scatter x1, waiting for transfers between devices, body(): half_share = lax.psum_scatter(terms, 'rep', scatter_dimension=0, tiled=True)  14.4 us
    all_to_all x2, starting transfers between devices, exchanged(): return lax.all_to_all(x, 'ep', split_axis=0, concat_axis=0, tiled=True)  11.1 us
    reduce_scatter x1, waiting for transfers between devices, body(): lax.psum_scatter((product * width_scale).astype(jnp.bfloat16), 'rep', sca...  11 us
    unnamed x23, local copies, waits for them, and re-layouts  6.31 us
  transfers between devices with their start and end apart: 10, of which 8 were waited for; matrix products, arithmetic and copies ran while one was open for 12% of the time, Pallas kernels for 0%

profile of v5, /device:TPU:1, one launch (start us, length us, event | category | flops | bytes accessed | tf_op | source)
XLA Modules:
  0.0 176.3 jit_solution(16149313002975679699)
XLA Ops:
  7.2 0.0 reduce-scatter.3.cloned.1.call-start
  7.2 8.9 %collective-permute-start = (bf16[320,384]{1,0:T(8,128)(2,1)}, bf16[320,384]{1,0:T(8,128)(2,1)S(1)}, u32[]{:S(2)}, u32[]{:S(2)}) collective-permute-start(bf16[320,384]{1,0:T(8,128)(2,1)} %bitcast.61), channel_id=1, source_target_pairs={{0,1},{1,0},{2,3},{3,2},{4,5},{5,4},{6,7},{7,6},{8,9},{9,8},{10,11... | collective-permute-start | bytes 737288 | tf_op jit(solution)/shard_map/ppermute | solution.py:18
  16.2 1.3 collective-permute-done
  17.5 4.6 %fusion.1 = bf16[2048,768]{0,1:T(8,128)(2,1)} fusion(bf16[1,1,320,2048]{3,2,1,0:T(8,128)(2,1)S(1)} %copy-done, bf16[320,384]{1,0:T(8,128)(2,1)} %bitcast.62, bf16[320,384]{1,0:T(8,128)(2,1)S(1)} %collective-permute-done, pred[]{:T(512)S(6)} %eq.89), kind=kOutput, calls=%fused_computation.5 | convolution fusion | flops 1011990528 | bytes 4947969 | tf_op jit(solution)/shard_map/dot_general | solution.py:71
  22.1 0.0 reduce-scatter.3.cloned.1.call-update
  22.1 0.7 copy-done.5
  22.7 0.1 copy.46
  22.8 0.1 eq.95
  22.9 0.1 eq.91
  23.0 1.2 reduce-window.6
  24.2 0.2 slice_reduce_fusion
  24.4 0.1 select_reduce_fusion.1
  24.6 0.1 add.76
  24.7 0.4 convert_reduce_fusion
  25.1 0.1 fusion.33
  25.2 0.3 convolution_convert_fusion.1
  25.5 0.1 stack_reshape.8
  25.6 0.3 convolution_convert_fusion
  25.9 0.1 stack_reshape.9
  26.0 0.1 pad_maximum_fusion
  26.1 0.9 copy.60
  27.0 5.1 %all-to-all-start = ((bf16[64,20,256]{2,1,0:T(8,128)(2,1)}), bf16[64,20,256]{2,1,0:T(8,128)(2,1)S(1)}, u32[]{:S(2)}, u32[]{:S(2)}) async-start(bf16[64,20,256]{2,1,0:T(8,128)(2,1)} %bitcast.4), calls=%async_computation | async-start | bytes 1572864 | tf_op jit(solution)/shard_map/all_to_all | solution.py:22
  32.1 0.0 reduce-scatter.5.cloned.1.call-start
  32.2 0.9 copy.45
  33.1 1.4 copy.54
  34.5 2.3 %copy.55 = f32[1,1,256,768]{2,3,1,0:T(8,128)} copy(f32[1,1,256,768]{3,2,1,0:T(8,128)} %param.14) | data formatting | bytes 1572864 | tf_op args[4]
  36.9 18.0 %all-to-all-done = bf16[64,20,256]{2,1,0:T(8,128)(2,1)S(1)} async-done(((bf16[64,20,256]{2,1,0:T(8,128)(2,1)}), bf16[64,20,256]{2,1,0:T(8,128)(2,1)S(1)}, u32[]{:S(2)}, u32[]{:S(2)}) %all-to-all-start) | async-done | bytes 655392 | tf_op jit(solution)/shard_map/all_to_all | solution.py:22
  54.9 0.9 copy.71
  55.8 2.1 %reshape.211 = bf16[1280,256]{1,0:T(8,128)(2,1)} reshape(bf16[2,32,20,256]{3,2,1,0:T(8,128)(2,1)} %bitcast.58) | data formatting | bytes 1310720 | tf_op jit(solution)/shard_map/reshape | solution.py:98
  57.9 11.0 %reduce-scatter.3.cloned.1.call-done = bf16[256,768]{0,1:T(8,128)(2,1)} async-done(((bf16[2048,768]{0,1:T(8,128)(2,1)}), bf16[256,768]{0,1:T(8,128)(2,1)}) %reduce-scatter.3.cloned.1.call-update) | async-done | bytes 393232 | tf_op jit(solution)/shard_map/reduce_scatter | solution.py:74
  69.0 1.9 %fusion.5 = bf16[256,768]{0,1:T(8,128)(2,1)S(1)} fusion(bf16[256,768]{0,1:T(8,128)(2,1)} %bitcast.59, bf16[256,768]{0,1:T(8,128)(2,1)} %reduce-scatter.3.cloned.1.call-done, f32[1,1,256,768]{2,3,1,0:T(8,128)S(1)} %copy-done.1, f32[1,1,256,768]{2,3,1,0:T(8,128)S(1)} %copy.54), kind=kLoop, calls=%fused_computation.19 | loop fusion | flops 3538944 | bytes 2752512 | tf_op jit(solution)/shard_map/convert_element_type | solution.py:106
  70.9 2.0 %fusion = bf16[768,1280]{1,0:T(8,128)(2,1)} fusion(bf16[256,768]{0,1:T(8,128)(2,1)S(1)} %fusion.5, bf16[1280,256]{1,0:T(8,128)(2,1)S(1)} %copy-done.2), kind=kOutput, calls=%fused_computation.4 | convolution fusion | flops 505282560 | bytes 3014656 | tf_op jit(solution)/shard_map/dot_general | solution.py:109
  72.9 0.9 copy.56
  73.8 9.3 %all-to-all-start.1 = ((bf16[32,8,768]{2,1,0:T(8,128)(2,1)}), bf16[32,8,768]{2,1,0:T(8,128)(2,1)S(1)}, u32[]{:S(2)}, u32[]{:S(2)}) async-start(bf16[32,8,768]{2,1,0:T(8,128)(2,1)} %bitcast.12), calls=%async_computation.2 | async-start | bytes 786432 | tf_op jit(solution)/shard_map/all_to_all | solution.py:28
  83.1 0.1 select_reduce_fusion.2
  83.2 0.1 convert_reduce_fusion.1
  83.3 0.1 reshape.213
  83.4 0.1 rev.3
  83.5 0.1 reshape.214
  83.6 10.9 %all-to-all-done.1 = bf16[32,8,768]{2,1,0:T(8,128)(2,1)S(1)} async-done(((bf16[32,8,768]{2,1,0:T(8,128)(2,1)}), bf16[32,8,768]{2,1,0:T(8,128)(2,1)S(1)}, u32[]{:S(2)}, u32[]{:S(2)}) %all-to-all-start.1) | async-done | bytes 393248 | tf_op jit(solution)/shard_map/all_to_all | solution.py:28
  94.5 1.5 gather_fusion
  96.0 4.6 %all-to-all-start.2 = ((bf16[32,16,768]{2,1,0:T(8,128)(2,1)}), bf16[32,16,768]{2,1,0:T(8,128)(2,1)S(1)}, u32[]{:S(2)}, u32[]{:S(2)}) async-start(bf16[32,16,768]{2,1,0:T(8,128)(2,1)} %bitcast.14), calls=%async_computation.3 | async-start | bytes 1572864 | tf_op jit(solution)/shard_map/all_to_all | solution.py:28
  100.7 0.1 copy.57
  100.8 0.1 reshape.219
  100.9 14.4 %reduce-scatter.5.cloned.1.call-done = bf16[96,1280]{1,0:T(8,128)(2,1)} async-done(((bf16[768,1280]{1,0:T(8,128)(2,1)}), bf16[96,1280]{1,0:T(8,128)(2,1)}) %reduce-scatter.5.cloned.1.call-update) | async-done | bytes 245776 | tf_op jit(solution)/shard_map/reduce_scatter | solution.py:114
  115.3 1.0 broadcast_select_fusion
  116.3 6.5 %collective-permute-start.2 = (bf16[96,640]{1,0:T(8,128)(2,1)S(1)}, bf16[96,640]{1,0:T(8,128)(2,1)S(1)}, u32[]{:S(2)}, u32[]{:S(2)}) collective-permute-start(bf16[96,640]{1,0:T(8,128)(2,1)S(1)} %broadcast_select_fusion), channel_id=1, source_target_pairs={{0,1},{1,0},{2,3},{3,2},{4,5},{5,4},{6,7},{7,6},{8,9},{9,8},{10,11... | collective-permute-start | bytes 368648 | tf_op jit(solution)/shard_map/ppermute | solution.py:18
  122.8 0.2 select_reduce_fusion
  123.0 0.1 mul.109
  123.1 0.6 collective-permute-done.2
  123.8 1.0 add_convert_fusion
  124.8 0.2 copy.58
  124.9 0.7 reshape.217
  125.7 9.4 %all-to-all-start.3 = ((bf16[32,20,96]{2,1,0:T(8,128)(2,1)}), bf16[32,20,96]{2,1,0:T(8,128)(2,1)S(1)}, u32[]{:S(2)}, u32[]{:S(2)}) async-start(bf16[32,20,96]{2,1,0:T(8,128)(2,1)} %bitcast.18), calls=%async_computation.5 | async-start | bytes 393216 | tf_op jit(solution)/shard_map/all_to_all | solution.py:28
  135.1 0.1 slice_bitcast_fusion.1
  135.1 2.5 %collective-permute-start.1 = (bf16[256,768]{1,0:T(8,128)(2,1)S(1)}, bf16[256,768]{1,0:T(8,128)(2,1)S(1)}, u32[]{:S(2)}, u32[]{:S(2)}) collective-permute-start(bf16[256,768]{1,0:T(8,128)(2,1)S(1)} %get-tuple-element.14), channel_id=1, source_target_pairs={{0,1},{1,0},{2,3},{3,2},{4,5},{5,4},{6,7},{7,6},{8,9},{9,8},{10,11... | collective-permute-start | bytes 1179656 | tf_op jit(solution)/shard_map/ppermute | solution.py:18
  137.7 8.0 %all-to-all-done.3 = bf16[32,20,96]{2,1,0:T(8,128)(2,1)S(1)} async-done(((bf16[32,20,96]{2,1,0:T(8,128)(2,1)}), bf16[32,20,96]{2,1,0:T(8,128)(2,1)S(1)}, u32[]{:S(2)}, u32[]{:S(2)}) %all-to-all-start.3) | async-done | bytes 122912 | tf_op jit(solution)/shard_map/all_to_all | solution.py:28
  145.6 0.2 fusion.23
  145.9 1.4 gather_fusion.1
  147.2 6.0 %all-to-all-start.4 = ((bf16[64,20,96]{2,1,0:T(8,128)(2,1)}), bf16[64,20,96]{2,1,0:T(8,128)(2,1)S(1)}, u32[]{:S(2)}, u32[]{:S(2)}) async-start(bf16[64,20,96]{2,1,0:T(8,128)(2,1)} %gather_fusion.1), calls=%async_computation.6 | async-start | bytes 786432 | tf_op jit(solution)/shard_map/all_to_all | solution.py:22
  153.3 1.0 maximum_select_fusion
  154.3 14.2 %all-to-all-done.4 = bf16[64,20,96]{2,1,0:T(8,128)(2,1)S(1)} async-done(((bf16[64,20,96]{2,1,0:T(8,128)(2,1)}), bf16[64,20,96]{2,1,0:T(8,128)(2,1)S(1)}, u32[]{:S(2)}, u32[]{:S(2)}) %all-to-all-start.4) | async-done | bytes 245792 | tf_op jit(solution)/shard_map/all_to_all | solution.py:22
  168.4 0.1 reshape.218
  168.6 0.9 copy.59
  (30 shorter events, 0.2 us)
Async XLA Ops:
  7.2 10.3 %copy-start = (bf16[1,1,320,2048]{3,2,1,0:T(8,128)(2,1)S(1)}, bf16[1,1,320,2048]{3,2,1,0:T(8,128)(2,1)}, u32[]{:S(2)}) copy-start(bf16[1,1,320,2048]{3,2,1,0:T(8,128)(2,1)} %param.10) | copy-start | bytes 3932164
  7.2 61.8 %reduce-scatter.3.cloned.1.call-start = ((), (), s32[]{:S(2)}) async-start(), calls=%async_computation.7 | async-start | bytes 3538944 | tf_op jit(solution)/shard_map/reduce_scatter | solution.py:74
  7.2 10.3 %collective-permute-start = (bf16[320,384]{1,0:T(8,128)(2,1)}, bf16[320,384]{1,0:T(8,128)(2,1)S(1)}, u32[]{:S(2)}, u32[]{:S(2)}) collective-permute-start(bf16[320,384]{1,0:T(8,128)(2,1)} %bitcast.61), channel_id=1, source_target_pairs={{0,1},{1,0},{2,3},{3,2},{4,5},{5,4},{6,7},{7,6},{8,9},{9,8},{10,11... | collective-permute-start | bytes 737288 | tf_op jit(solution)/shard_map/ppermute | solution.py:18
  22.0 0.7 copy-start.5
  22.0 2.4 %copy-start.6 = (s32[32]{0:T(128)S(1)}, s32[32]{0:T(128)}, u32[]{:S(2)}) copy-start(s32[32]{0:T(128)} %param.18) | copy-start | bytes 388
  22.1 3.1 %copy-start.4 = (bf16[64,2,256]{2,1,0:T(2,128)(2,1)S(1)}, bf16[64,2,256]{2,1,0:T(2,128)(2,1)}, u32[]{:S(2)}) copy-start(bf16[64,2,256]{2,1,0:T(2,128)(2,1)} %param.15) | copy-start | bytes 196612
  26.1 6.1 %copy-start.3 = (bf16[1,1,256,768]{3,2,1,0:T(8,128)(2,1)S(1)}, bf16[1,1,256,768]{3,2,1,0:T(8,128)(2,1)}, u32[]{:S(2)}) copy-start(bf16[1,1,256,768]{3,2,1,0:T(8,128)(2,1)} %param.12) | copy-start | bytes 1179652
  27.0 27.9 %all-to-all-start = ((bf16[64,20,256]{2,1,0:T(8,128)(2,1)}), bf16[64,20,256]{2,1,0:T(8,128)(2,1)S(1)}, u32[]{:S(2)}, u32[]{:S(2)}) async-start(bf16[64,20,256]{2,1,0:T(8,128)(2,1)} %bitcast.4), calls=%async_computation | async-start | bytes 1572864 | tf_op jit(solution)/shard_map/all_to_all | solution.py:22
  32.1 83.2 %reduce-scatter.5.cloned.1.call-start = ((), (), s32[]{:S(2)}) async-start(), calls=%async_computation.8 | async-start | bytes 2211840 | tf_op jit(solution)/shard_map/reduce_scatter | solution.py:114
  55.8 13.1 %copy-start.1 = (f32[1,1,256,768]{2,3,1,0:T(8,128)S(1)}, f32[1,1,256,768]{2,3,1,0:T(8,128)}, u32[]{:S(2)}) copy-start(f32[1,1,256,768]{2,3,1,0:T(8,128)} %copy.55) | copy-start | bytes 2359300
  69.0 1.9 %copy-start.2 = (bf16[1280,256]{1,0:T(8,128)(2,1)S(1)}, bf16[1280,256]{1,0:T(8,128)(2,1)}, u32[]{:S(2)}) copy-start(bf16[1280,256]{1,0:T(8,128)(2,1)} %reshape.211) | copy-start | bytes 1966084
  72.9 10.2 %copy-start.8 = (s32[64]{0:T(128)S(1)}, s32[64]{0:T(128)}, u32[]{:S(2)}) copy-start(s32[64]{0:T(128)} %param.19) | copy-start | bytes 772
  73.8 20.7 %all-to-all-start.1 = ((bf16[32,8,768]{2,1,0:T(8,128)(2,1)}), bf16[32,8,768]{2,1,0:T(8,128)(2,1)S(1)}, u32[]{:S(2)}, u32[]{:S(2)}) async-start(bf16[32,8,768]{2,1,0:T(8,128)(2,1)} %bitcast.12), calls=%async_computation.2 | async-start | bytes 786432 | tf_op jit(solution)/shard_map/all_to_all | solution.py:28
  83.6 17.0 %copy-start.7 = (bf16[64,8]{0,1:T(8,128)(2,1)S(1)}, bf16[64,8]{0,1:T(8,128)(2,1)}, u32[]{:S(2)}) copy-start(bf16[64,8]{0,1:T(8,128)(2,1)} %param.17) | copy-start | bytes 3076
  96.0 29.7 %all-to-all-start.2 = ((bf16[32,16,768]{2,1,0:T(8,128)(2,1)}), bf16[32,16,768]{2,1,0:T(8,128)(2,1)S(1)}, u32[]{:S(2)}, u32[]{:S(2)}) async-start(bf16[32,16,768]{2,1,0:T(8,128)(2,1)} %bitcast.14), calls=%async_computation.3 | async-start | bytes 1572864 | tf_op jit(solution)/shard_map/all_to_all | solution.py:28
  116.3 7.5 %collective-permute-start.2 = (bf16[96,640]{1,0:T(8,128)(2,1)S(1)}, bf16[96,640]{1,0:T(8,128)(2,1)S(1)}, u32[]{:S(2)}, u32[]{:S(2)}) collective-permute-start(bf16[96,640]{1,0:T(8,128)(2,1)S(1)} %broadcast_select_fusion), channel_id=1, source_target_pairs={{0,1},{1,0},{2,3},{3,2},{4,5},{5,4},{6,7},{7,6},{8,9},{9,8},{10,11... | collective-permute-start | bytes 368648 | tf_op jit(solution)/shard_map/ppermute | solution.py:18
  125.7 19.9 %all-to-all-start.3 = ((bf16[32,20,96]{2,1,0:T(8,128)(2,1)}), bf16[32,20,96]{2,1,0:T(8,128)(2,1)S(1)}, u32[]{:S(2)}, u32[]{:S(2)}) async-start(bf16[32,20,96]{2,1,0:T(8,128)(2,1)} %bitcast.18), calls=%async_computation.5 | async-start | bytes 393216 | tf_op jit(solution)/shard_map/all_to_all | solution.py:28
  135.1 18.1 %collective-permute-start.1 = (bf16[256,768]{1,0:T(8,128)(2,1)S(1)}, bf16[256,768]{1,0:T(8,128)(2,1)S(1)}, u32[]{:S(2)}, u32[]{:S(2)}) collective-permute-start(bf16[256,768]{1,0:T(8,128)(2,1)S(1)} %get-tuple-element.14), channel_id=1, source_target_pairs={{0,1},{1,0},{2,3},{3,2},{4,5},{5,4},{6,7},{7,6},{8,9},{9,8},{10,11... | collective-permute-start | bytes 1179656 | tf_op jit(solution)/shard_map/ppermute | solution.py:18
  147.2 21.2 %all-to-all-start.4 = ((bf16[64,20,96]{2,1,0:T(8,128)(2,1)}), bf16[64,20,96]{2,1,0:T(8,128)(2,1)S(1)}, u32[]{:S(2)}, u32[]{:S(2)}) async-start(bf16[64,20,96]{2,1,0:T(8,128)(2,1)} %gather_fusion.1), calls=%async_computation.6 | async-start | bytes 786432 | tf_op jit(solution)/shard_map/all_to_all | solution.py:22
Sparse Core Ops, SparseCore 0:
  22.2 46.7 reduce-scatter.2
  73.0 42.2 reduce-scatter.4

commit v6 on v5

--- a/solution.py
+++ b/solution.py
@@ -93,9 +93,14 @@
     send_tokens = jnp.stack(halves, axis=1).reshape(ep_count, capacity, -1)
     gate_row = gate_weights.reshape(1, pair_count).astype(jnp.float32)
     slot_gates = jnp.sum(jnp.where(placing, gate_row, 0.0), axis=1)
-    recv_tokens = jnp.transpose(
-        exchanged(send_tokens).reshape(chip_count, 2, capacity, piece_rows), (1, 0, 2, 3)
-    ).reshape(2 * slot_count, piece_rows)
+    recv_tokens = exchanged(send_tokens).reshape(chip_count, 2, capacity, piece_rows)
+    even_tokens = recv_tokens[:, 0].reshape(slot_count, piece_rows)
+    odd_tokens = recv_tokens[:, 1].reshape(slot_count, piece_rows)
+    recv_tokens = jnp.where(
+        is_upper,
+        jnp.concatenate([odd_tokens, even_tokens]),
+        jnp.concatenate([even_tokens, odd_tokens]),
+    )
 
     weight_local, recv_tokens = lax.optimization_barrier((weight[0, 0], recv_tokens))
     gradient = summed.astype(jnp.float32)
@@ -112,9 +117,8 @@
         * width_scale
     ).astype(jnp.bfloat16)
     half_share = lax.psum_scatter(terms, "rep", scatter_dimension=0, tiled=True)
-    even_rows, odd_rows = half_share[:, :slot_count], half_share[:, slot_count:]
-    partner_share = swapped(jnp.where(is_upper, even_rows, odd_rows))
-    own_share = jnp.where(is_upper, odd_rows, even_rows)
+    own_share = half_share[:, :slot_count]
+    partner_share = swapped(half_share[:, slot_count:])
     preact_share = (
         own_share.astype(jnp.float32) + partner_share.astype(jnp.float32)
     ).astype(jnp.bfloat16)

time: 177 us -> 177 us (level)
  waiting for transfers between devices: 78.5 us -> 75.5 us
    reshape x2 -> x0, local copies, waits for them, and re-layouts: 3.02 us -> none  [the longest x1 2.09 us: body(): recv_tokens = jnp.transpose(exchanged(send_tokens).reshape(chip_count, 2,...]
    reduce_scatter x1, waiting for transfers between devices: 11 us -> 8.1 us  [body(): lax.psum_scatter((product * width_scale).astype(jnp.bfloat16), 'rep', sca...]
    another operation x1 -> x3, local copies, waits for them, and re-layouts: 0.01 us -> 2.95 us  [the longest x1 1.8 us: body(): even_tokens = recv_tokens[:, 0].reshape(slot_count, piece_rows)]
    slice x1 -> x3, local copies, waits for them, and re-layouts: 0.22 us -> 2.08 us  [the longest x1 0.94 us: body(): odd_tokens = recv_tokens[:, 1].reshape(slot_count, piece_rows)]
  transfers between devices with their start and end apart: 10 -> 10, of which waited for: 8 -> 8; matrix products, arithmetic and copies ran while one was open for 12% -> 13% of each run, Pallas kernels for 0% -> 0%
where the time goes in v6:
time: 177 us; the launch traced here: 176 us
  waiting for transfers between devices  75.5 us (43%)
  starting transfers between devices  52.4 us (30%)
  local copies, waits for them, and re-layouts  18.2 us (10%)
  between operations  14.4 us (8%)
  other arithmetic  8.39 us (5%)
  matrix products  7.14 us (4%)
    all_to_all x2, waiting for transfers between devices, exchanged(): return lax.all_to_all(x, 'ep', split_axis=0, concat_axis=0, tiled=True)  32.2 us
    all_to_all x3, starting transfers between devices, exchanged_chips(): lax.all_to_all(x, 'ep', split_axis=0, concat_axis=0, tiled=True, axis_ind...  23.2 us
    all_to_all x3, waiting for transfers between devices, exchanged_chips(): lax.all_to_all(x, 'ep', split_axis=0, concat_axis=0, tiled=True, axis_ind...  18.9 us
    ppermute x3, starting transfers between devices, swapped(): lax.ppermute(x, 'ep', [(i, i ^ 1) for i in range(lax.axis_size('ep'))])  18 us
    reduce_scatter x1, waiting for transfers between devices, body(): half_share = lax.psum_scatter(terms, 'rep', scatter_dimension=0, tiled=True)  14.4 us
    all_to_all x2, starting transfers between devices, exchanged(): return lax.all_to_all(x, 'ep', split_axis=0, concat_axis=0, tiled=True)  11.1 us
    reduce_scatter x1, waiting for transfers between devices, body(): lax.psum_scatter((product * width_scale).astype(jnp.bfloat16), 'rep', sca...  8.1 us
    unnamed x23, local copies, waits for them, and re-layouts  6.29 us
  transfers between devices with their start and end apart: 10, of which 8 were waited for; matrix products, arithmetic and copies ran while one was open for 13% of the time, Pallas kernels for 0%

profile of v6, /device:TPU:1, one launch (start us, length us, event | category | flops | bytes accessed | tf_op | source)
XLA Modules:
  0.0 176.1 jit_solution(6661684162581903609)
XLA Ops:
  7.2 8.9 %collective-permute-start = (bf16[320,384]{1,0:T(8,128)(2,1)}, bf16[320,384]{1,0:T(8,128)(2,1)S(1)}, u32[]{:S(2)}, u32[]{:S(2)}) collective-permute-start(bf16[320,384]{1,0:T(8,128)(2,1)} %bitcast.57), channel_id=1, source_target_pairs={{0,1},{1,0},{2,3},{3,2},{4,5},{5,4},{6,7},{7,6},{8,9},{9,8},{10,11... | collective-permute-start | bytes 737288 | tf_op jit(solution)/shard_map/ppermute | solution.py:18
  16.2 1.3 collective-permute-done
  17.5 4.6 %fusion.1 = bf16[2048,768]{0,1:T(8,128)(2,1)} fusion(bf16[1,1,320,2048]{3,2,1,0:T(8,128)(2,1)S(1)} %copy-done, bf16[320,384]{1,0:T(8,128)(2,1)} %bitcast.58, bf16[320,384]{1,0:T(8,128)(2,1)S(1)} %collective-permute-done, pred[]{:T(512)S(6)} %eq.89), kind=kOutput, calls=%fused_computation.5 | convolution fusion | flops 1011990528 | bytes 4947969 | tf_op jit(solution)/shard_map/dot_general | solution.py:71
  22.1 0.7 copy-done.5
  22.7 0.1 copy.49
  22.8 0.1 eq.95
  22.9 0.1 eq.91
  23.0 1.2 reduce-window.6
  24.2 0.2 slice_reduce_fusion
  24.4 0.1 select_reduce_fusion.1
  24.6 0.1 add.76
  24.7 0.4 convert_reduce_fusion
  25.1 0.1 fusion.34
  25.2 0.3 convolution_convert_fusion.1
  25.5 0.1 stack_reshape.8
  25.6 0.3 convolution_convert_fusion
  25.9 0.1 stack_reshape.9
  26.0 0.1 pad_maximum_fusion
  26.1 0.9 copy.65
  27.0 5.1 %all-to-all-start = ((bf16[64,20,256]{2,1,0:T(8,128)(2,1)}), bf16[64,20,256]{2,1,0:T(8,128)(2,1)S(1)}, u32[]{:S(2)}, u32[]{:S(2)}) async-start(bf16[64,20,256]{2,1,0:T(8,128)(2,1)} %bitcast.4), calls=%async_computation | async-start | bytes 1572864 | tf_op jit(solution)/shard_map/all_to_all | solution.py:22
  32.1 0.0 reduce-scatter.5.cloned.1.call-start
  32.2 0.9 copy.48
  33.1 1.4 copy.59
  34.5 2.3 %copy.60 = f32[1,1,256,768]{2,3,1,0:T(8,128)} copy(f32[1,1,256,768]{3,2,1,0:T(8,128)} %param.14) | data formatting | bytes 1572864 | tf_op args[4]
  36.8 18.0 %all-to-all-done = bf16[64,20,256]{2,1,0:T(8,128)(2,1)S(1)} async-done(((bf16[64,20,256]{2,1,0:T(8,128)(2,1)}), bf16[64,20,256]{2,1,0:T(8,128)(2,1)S(1)}, u32[]{:S(2)}, u32[]{:S(2)}) %all-to-all-start) | async-done | bytes 655392 | tf_op jit(solution)/shard_map/all_to_all | solution.py:22
  54.9 0.9 fusion.33
  55.8 1.1 reshape_squeeze.6
  57.0 1.8 %reshape_squeeze.7 = bf16[640,256]{1,0:T(8,128)(2,1)} reshape(bf16[32,1,20,256]{3,2,1,0:T(8,128)(2,1)} %get-tuple-element.17) | data formatting | bytes 655360 | tf_op jit(solution)/shard_map/reshape;squeeze | solution.py:97
  58.8 2.1 %maximum_select_fusion.1 = bf16[1280,256]{1,0:T(8,128)(2,1)} fusion(bf16[640,256]{1,0:T(8,128)(2,1)} %reshape_squeeze.7, bf16[640,256]{1,0:T(8,128)(2,1)S(1)} %reshape_squeeze.6, pred[]{:T(512)S(6)} %eq.89), kind=kLoop, calls=%fused_computation.29 | loop fusion | flops 2949120 | bytes 1310721 | tf_op jit(solution)/shard_map/jit(_where)/select_n | solution.py:99
  60.9 8.1 %reduce-scatter.3.cloned.1.call-done = bf16[256,768]{0,1:T(8,128)(2,1)} async-done(((bf16[2048,768]{0,1:T(8,128)(2,1)}), bf16[256,768]{0,1:T(8,128)(2,1)}) %reduce-scatter.3.cloned.1.call-update) | async-done | bytes 393232 | tf_op jit(solution)/shard_map/reduce_scatter | solution.py:74
  69.0 1.9 %fusion.5 = bf16[256,768]{0,1:T(8,128)(2,1)S(1)} fusion(bf16[256,768]{0,1:T(8,128)(2,1)} %bitcast.55, bf16[256,768]{0,1:T(8,128)(2,1)} %reduce-scatter.3.cloned.1.call-done, f32[1,1,256,768]{2,3,1,0:T(8,128)S(1)} %copy-done.1, f32[1,1,256,768]{2,3,1,0:T(8,128)S(1)} %copy.59), kind=kLoop, calls=%fused_computation.19 | loop fusion | flops 3538944 | bytes 2752512 | tf_op jit(solution)/shard_map/convert_element_type | solution.py:111
  70.9 2.0 %fusion = bf16[768,1280]{1,0:T(8,128)(2,1)} fusion(bf16[256,768]{0,1:T(8,128)(2,1)S(1)} %fusion.5, bf16[1280,256]{1,0:T(8,128)(2,1)S(1)} %copy-done.2), kind=kOutput, calls=%fused_computation.4 | convolution fusion | flops 505282560 | bytes 3014656 | tf_op jit(solution)/shard_map/dot_general | solution.py:114
  72.9 0.9 copy.61
  73.8 9.3 %all-to-all-start.1 = ((bf16[32,8,768]{2,1,0:T(8,128)(2,1)}), bf16[32,8,768]{2,1,0:T(8,128)(2,1)S(1)}, u32[]{:S(2)}, u32[]{:S(2)}) async-start(bf16[32,8,768]{2,1,0:T(8,128)(2,1)} %bitcast.11), calls=%async_computation.2 | async-start | bytes 786432 | tf_op jit(solution)/shard_map/all_to_all | solution.py:28
  83.1 0.1 select_reduce_fusion.2
  83.2 0.1 convert_reduce_fusion.1
  83.3 0.1 reshape.209
  83.4 0.1 rev.3
  83.5 0.1 reshape.210
  83.6 10.9 %all-to-all-done.1 = bf16[32,8,768]{2,1,0:T(8,128)(2,1)S(1)} async-done(((bf16[32,8,768]{2,1,0:T(8,128)(2,1)}), bf16[32,8,768]{2,1,0:T(8,128)(2,1)S(1)}, u32[]{:S(2)}, u32[]{:S(2)}) %all-to-all-start.1) | async-done | bytes 393248 | tf_op jit(solution)/shard_map/all_to_all | solution.py:28
  94.5 1.5 gather_fusion
  96.0 4.6 %all-to-all-start.2 = ((bf16[32,16,768]{2,1,0:T(8,128)(2,1)}), bf16[32,16,768]{2,1,0:T(8,128)(2,1)S(1)}, u32[]{:S(2)}, u32[]{:S(2)}) async-start(bf16[32,16,768]{2,1,0:T(8,128)(2,1)} %bitcast.13), calls=%async_computation.3 | async-start | bytes 1572864 | tf_op jit(solution)/shard_map/all_to_all | solution.py:28
  100.7 0.1 copy.62
  100.8 0.1 reshape.215
  100.9 14.4 %reduce-scatter.5.cloned.1.call-done = bf16[96,1280]{1,0:T(8,128)(2,1)} async-done(((bf16[768,1280]{1,0:T(8,128)(2,1)}), bf16[96,1280]{1,0:T(8,128)(2,1)}) %reduce-scatter.5.cloned.1.call-update) | async-done | bytes 245776 | tf_op jit(solution)/shard_map/reduce_scatter | solution.py:119
  115.3 0.9 slice.50
  116.2 6.5 %collective-permute-start.2 = (bf16[96,640]{1,0:T(8,128)(2,1)S(1)}, bf16[96,640]{1,0:T(8,128)(2,1)S(1)}, u32[]{:S(2)}, u32[]{:S(2)}) collective-permute-start(bf16[96,640]{1,0:T(8,128)(2,1)S(1)} %slice.50), channel_id=1, source_target_pairs={{0,1},{1,0},{2,3},{3,2},{4,5},{5,4},{6,7},{7,6},{8,9},{9,8},{10,11... | collective-permute-start | bytes 368648 | tf_op jit(solution)/shard_map/ppermute | solution.py:18
  122.7 0.2 select_reduce_fusion
  123.0 0.1 mul.109
  123.1 0.6 collective-permute-done.2
  123.7 0.9 add_convert_fusion
  124.6 0.2 copy.63
  124.8 0.7 reshape.213
  125.5 9.3 %all-to-all-start.3 = ((bf16[32,20,96]{2,1,0:T(8,128)(2,1)}), bf16[32,20,96]{2,1,0:T(8,128)(2,1)S(1)}, u32[]{:S(2)}, u32[]{:S(2)}) async-start(bf16[32,20,96]{2,1,0:T(8,128)(2,1)} %bitcast.17), calls=%async_computation.5 | async-start | bytes 393216 | tf_op jit(solution)/shard_map/all_to_all | solution.py:28
  134.8 0.1 slice_bitcast_fusion.1
  134.9 2.5 %collective-permute-start.1 = (bf16[256,768]{1,0:T(8,128)(2,1)S(1)}, bf16[256,768]{1,0:T(8,128)(2,1)S(1)}, u32[]{:S(2)}, u32[]{:S(2)}) collective-permute-start(bf16[256,768]{1,0:T(8,128)(2,1)S(1)} %get-tuple-element.14), channel_id=1, source_target_pairs={{0,1},{1,0},{2,3},{3,2},{4,5},{5,4},{6,7},{7,6},{8,9},{9,8},{10,11... | collective-permute-start | bytes 1179656 | tf_op jit(solution)/shard_map/ppermute | solution.py:18
  137.4 8.0 %all-to-all-done.3 = bf16[32,20,96]{2,1,0:T(8,128)(2,1)S(1)} async-done(((bf16[32,20,96]{2,1,0:T(8,128)(2,1)}), bf16[32,20,96]{2,1,0:T(8,128)(2,1)S(1)}, u32[]{:S(2)}, u32[]{:S(2)}) %all-to-all-start.3) | async-done | bytes 122912 | tf_op jit(solution)/shard_map/all_to_all | solution.py:28
  145.4 0.2 fusion.23
  145.6 1.4 gather_fusion.1
  147.0 6.0 %all-to-all-start.4 = ((bf16[64,20,96]{2,1,0:T(8,128)(2,1)}), bf16[64,20,96]{2,1,0:T(8,128)(2,1)S(1)}, u32[]{:S(2)}, u32[]{:S(2)}) async-start(bf16[64,20,96]{2,1,0:T(8,128)(2,1)} %gather_fusion.1), calls=%async_computation.6 | async-start | bytes 786432 | tf_op jit(solution)/shard_map/all_to_all | solution.py:22
  153.0 1.0 maximum_select_fusion
  154.0 14.2 %all-to-all-done.4 = bf16[64,20,96]{2,1,0:T(8,128)(2,1)S(1)} async-done(((bf16[64,20,96]{2,1,0:T(8,128)(2,1)}), bf16[64,20,96]{2,1,0:T(8,128)(2,1)S(1)}, u32[]{:S(2)}, u32[]{:S(2)}) %all-to-all-start.4) | async-done | bytes 245792 | tf_op jit(solution)/shard_map/all_to_all | solution.py:22
  168.2 0.1 reshape.214
  168.3 0.9 copy.64
  (32 shorter events, 0.2 us)
Async XLA Ops:
  7.2 10.3 %copy-start = (bf16[1,1,320,2048]{3,2,1,0:T(8,128)(2,1)S(1)}, bf16[1,1,320,2048]{3,2,1,0:T(8,128)(2,1)}, u32[]{:S(2)}) copy-start(bf16[1,1,320,2048]{3,2,1,0:T(8,128)(2,1)} %param.10) | copy-start | bytes 3932164
  7.2 61.8 %reduce-scatter.3.cloned.1.call-start = ((), (), s32[]{:S(2)}) async-start(), calls=%async_computation.7 | async-start | bytes 3538944 | tf_op jit(solution)/shard_map/reduce_scatter | solution.py:74
  7.2 10.3 %collective-permute-start = (bf16[320,384]{1,0:T(8,128)(2,1)}, bf16[320,384]{1,0:T(8,128)(2,1)S(1)}, u32[]{:S(2)}, u32[]{:S(2)}) collective-permute-start(bf16[320,384]{1,0:T(8,128)(2,1)} %bitcast.57), channel_id=1, source_target_pairs={{0,1},{1,0},{2,3},{3,2},{4,5},{5,4},{6,7},{7,6},{8,9},{9,8},{10,11... | collective-permute-start | bytes 737288 | tf_op jit(solution)/shard_map/ppermute | solution.py:18
  22.0 0.7 copy-start.5
  22.0 2.4 %copy-start.6 = (s32[32]{0:T(128)S(1)}, s32[32]{0:T(128)}, u32[]{:S(2)}) copy-start(s32[32]{0:T(128)} %param.18) | copy-start | bytes 388
  22.1 3.1 %copy-start.4 = (bf16[64,2,256]{2,1,0:T(2,128)(2,1)S(1)}, bf16[64,2,256]{2,1,0:T(2,128)(2,1)}, u32[]{:S(2)}) copy-start(bf16[64,2,256]{2,1,0:T(2,128)(2,1)} %param.15) | copy-start | bytes 196612
  26.1 6.1 %copy-start.3 = (bf16[1,1,256,768]{3,2,1,0:T(8,128)(2,1)S(1)}, bf16[1,1,256,768]{3,2,1,0:T(8,128)(2,1)}, u32[]{:S(2)}) copy-start(bf16[1,1,256,768]{3,2,1,0:T(8,128)(2,1)} %param.12) | copy-start | bytes 1179652
  27.0 27.9 %all-to-all-start = ((bf16[64,20,256]{2,1,0:T(8,128)(2,1)}), bf16[64,20,256]{2,1,0:T(8,128)(2,1)S(1)}, u32[]{:S(2)}, u32[]{:S(2)}) async-start(bf16[64,20,256]{2,1,0:T(8,128)(2,1)} %bitcast.4), calls=%async_computation | async-start | bytes 1572864 | tf_op jit(solution)/shard_map/all_to_all | solution.py:22
  32.1 83.2 %reduce-scatter.5.cloned.1.call-start = ((), (), s32[]{:S(2)}) async-start(), calls=%async_computation.8 | async-start | bytes 2211840 | tf_op jit(solution)/shard_map/reduce_scatter | solution.py:119
  55.8 13.1 %copy-start.1 = (f32[1,1,256,768]{2,3,1,0:T(8,128)S(1)}, f32[1,1,256,768]{2,3,1,0:T(8,128)}, u32[]{:S(2)}) copy-start(f32[1,1,256,768]{2,3,1,0:T(8,128)} %copy.60) | copy-start | bytes 2359300
  69.0 1.9 %copy-start.2 = (bf16[1280,256]{1,0:T(8,128)(2,1)S(1)}, bf16[1280,256]{1,0:T(8,128)(2,1)}, u32[]{:S(2)}) copy-start(bf16[1280,256]{1,0:T(8,128)(2,1)} %maximum_select_fusion.1) | copy-start | bytes 1966084
  72.9 10.2 %copy-start.8 = (s32[64]{0:T(128)S(1)}, s32[64]{0:T(128)}, u32[]{:S(2)}) copy-start(s32[64]{0:T(128)} %param.19) | copy-start | bytes 772
  73.8 20.7 %all-to-all-start.1 = ((bf16[32,8,768]{2,1,0:T(8,128)(2,1)}), bf16[32,8,768]{2,1,0:T(8,128)(2,1)S(1)}, u32[]{:S(2)}, u32[]{:S(2)}) async-start(bf16[32,8,768]{2,1,0:T(8,128)(2,1)} %bitcast.11), calls=%async_computation.2 | async-start | bytes 786432 | tf_op jit(solution)/shard_map/all_to_all | solution.py:28
  83.6 17.0 %copy-start.7 = (bf16[64,8]{0,1:T(8,128)(2,1)S(1)}, bf16[64,8]{0,1:T(8,128)(2,1)}, u32[]{:S(2)}) copy-start(bf16[64,8]{0,1:T(8,128)(2,1)} %param.17) | copy-start | bytes 3076
  96.0 29.5 %all-to-all-start.2 = ((bf16[32,16,768]{2,1,0:T(8,128)(2,1)}), bf16[32,16,768]{2,1,0:T(8,128)(2,1)S(1)}, u32[]{:S(2)}, u32[]{:S(2)}) async-start(bf16[32,16,768]{2,1,0:T(8,128)(2,1)} %bitcast.13), calls=%async_computation.3 | async-start | bytes 1572864 | tf_op jit(solution)/shard_map/all_to_all | solution.py:28
  116.2 7.5 %collective-permute-start.2 = (bf16[96,640]{1,0:T(8,128)(2,1)S(1)}, bf16[96,640]{1,0:T(8,128)(2,1)S(1)}, u32[]{:S(2)}, u32[]{:S(2)}) collective-permute-start(bf16[96,640]{1,0:T(8,128)(2,1)S(1)} %slice.50), channel_id=1, source_target_pairs={{0,1},{1,0},{2,3},{3,2},{4,5},{5,4},{6,7},{7,6},{8,9},{9,8},{10,11... | collective-permute-start | bytes 368648 | tf_op jit(solution)/shard_map/ppermute | solution.py:18
  125.5 19.9 %all-to-all-start.3 = ((bf16[32,20,96]{2,1,0:T(8,128)(2,1)}), bf16[32,20,96]{2,1,0:T(8,128)(2,1)S(1)}, u32[]{:S(2)}, u32[]{:S(2)}) async-start(bf16[32,20,96]{2,1,0:T(8,128)(2,1)} %bitcast.17), calls=%async_computation.5 | async-start | bytes 393216 | tf_op jit(solution)/shard_map/all_to_all | solution.py:28
  134.9 18.1 %collective-permute-start.1 = (bf16[256,768]{1,0:T(8,128)(2,1)S(1)}, bf16[256,768]{1,0:T(8,128)(2,1)S(1)}, u32[]{:S(2)}, u32[]{:S(2)}) collective-permute-start(bf16[256,768]{1,0:T(8,128)(2,1)S(1)} %get-tuple-element.14), channel_id=1, source_target_pairs={{0,1},{1,0},{2,3},{3,2},{4,5},{5,4},{6,7},{7,6},{8,9},{9,8},{10,11... | collective-permute-start | bytes 1179656 | tf_op jit(solution)/shard_map/ppermute | solution.py:18
  147.0 21.2 %all-to-all-start.4 = ((bf16[64,20,96]{2,1,0:T(8,128)(2,1)}), bf16[64,20,96]{2,1,0:T(8,128)(2,1)S(1)}, u32[]{:S(2)}, u32[]{:S(2)}) async-start(bf16[64,20,96]{2,1,0:T(8,128)(2,1)} %gather_fusion.1), calls=%async_computation.6 | async-start | bytes 786432 | tf_op jit(solution)/shard_map/all_to_all | solution.py:22
Sparse Core Ops, SparseCore 0:
  22.2 46.7 reduce-scatter.2
  73.0 42.2 reduce-scatter.4

commit v7 on v5

--- a/solution.py
+++ b/solution.py
@@ -68,6 +68,7 @@
         jnp.concatenate([partner_cotan, own_cotan], axis=1),
         jnp.concatenate([own_cotan, partner_cotan], axis=1),
     )
+    full_cotan = lax.optimization_barrier(full_cotan)
     product = lax.dot_general(
         acts_local, full_cotan, (((0,), (0,)), ((), ())), preferred_element_type=jnp.float32
     )
@@ -93,9 +94,7 @@
     send_tokens = jnp.stack(halves, axis=1).reshape(ep_count, capacity, -1)
     gate_row = gate_weights.reshape(1, pair_count).astype(jnp.float32)
     slot_gates = jnp.sum(jnp.where(placing, gate_row, 0.0), axis=1)
-    recv_tokens = jnp.transpose(
-        exchanged(send_tokens).reshape(chip_count, 2, capacity, piece_rows), (1, 0, 2, 3)
-    ).reshape(2 * slot_count, piece_rows)
+    recv_tokens = exchanged(send_tokens).reshape(ep_count * capacity, piece_rows)
 
     weight_local, recv_tokens = lax.optimization_barrier((weight[0, 0], recv_tokens))
     gradient = summed.astype(jnp.float32)
@@ -112,12 +111,6 @@
         * width_scale
     ).astype(jnp.bfloat16)
     half_share = lax.psum_scatter(terms, "rep", scatter_dimension=0, tiled=True)
-    even_rows, odd_rows = half_share[:, :slot_count], half_share[:, slot_count:]
-    partner_share = swapped(jnp.where(is_upper, even_rows, odd_rows))
-    own_share = jnp.where(is_upper, odd_rows, even_rows)
-    preact_share = (
-        own_share.astype(jnp.float32) + partner_share.astype(jnp.float32)
-    ).astype(jnp.bfloat16)
 
     group_rows = piece_rows // chip_count
     spread = exchanged_chips(new_weight.reshape(chip_count, group_rows, hidden_width))
@@ -138,11 +131,14 @@
         is_upper, jnp.stack([other_half, own_half]), jnp.stack([own_half, other_half])
     )
 
-    back = exchanged_chips(
-        jnp.transpose(preact_share.reshape(share_width, chip_count, capacity), (1, 2, 0))
+    back = exchanged(
+        jnp.transpose(half_share.reshape(share_width, ep_count, capacity), (1, 2, 0))
+    )
+    preact = jnp.sum(
+        back.reshape(chip_count, 2, capacity, share_width).astype(jnp.float32), axis=1
     )
     activation = (
-        slot_gates.reshape(chip_count, capacity, 1) * jax.nn.silu(back.astype(jnp.float32))
+        slot_gates.reshape(chip_count, capacity, 1) * jax.nn.silu(preact)
     ).astype(jnp.bfloat16)
     first_device = jnp.min(
         jnp.where(serve_place[None, :] == expert_ids[:, None], device_ids[None, :], ep_count),

time: 177 us -> 178 us (level)
  waiting for transfers between devices: 78.5 us -> 85 us
  starting transfers between devices: 52.5 us -> 49.6 us
    all_to_all x2 -> x3, starting transfers between devices: 11.1 us -> 24.2 us  [exchanged(): return lax.all_to_all(x, 'ep', split_axis=0, concat_axis=0, tiled=True)]
    all_to_all x2 -> x3, waiting for transfers between devices: 32.2 us -> 44 us  [exchanged(): return lax.all_to_all(x, 'ep', split_axis=0, concat_axis=0, tiled=True)]
    all_to_all x3 -> x2, starting transfers between devices: 23.3 us -> 14.1 us  [exchanged_chips(): lax.all_to_all(x, 'ep', split_axis=0, concat_axis=0, tiled=True, axis_ind...]
    all_to_all x3 -> x2, waiting for transfers between devices: 18.9 us -> 11.8 us  [exchanged_chips(): lax.all_to_all(x, 'ep', split_axis=0, concat_axis=0, tiled=True, axis_ind...]
    ppermute x3 -> x2, starting transfers between devices: 18 us -> 11.3 us  [swapped(): lax.ppermute(x, 'ep', [(i, i ^ 1) for i in range(lax.axis_size('ep'))])]
    reshape x3 -> x2, local copies, waits for them, and re-layouts: 3.76 us -> 0.98 us  [the longest x1 0.84 us: body(): half_share.reshape(share_width, ep_count, capacity)]
    reduce_scatter x1, waiting for transfers between devices: 11 us -> 13.8 us  [body(): lax.psum_scatter((product * width_scale).astype(jnp.bfloat16), 'rep', sca...]
    unnamed x23 -> x19, local copies, waits for them, and re-layouts: 6.31 us -> 6.29 us
  transfers between devices with their start and end apart: 10 -> 9, of which waited for: 8 -> 8; matrix products, arithmetic and copies ran while one was open for 12% -> 10% of each run, Pallas kernels for 0% -> 0%
where the time goes in v7:
time: 178 us; the launch traced here: 177 us
  waiting for transfers between devices  85 us (48%)
  starting transfers between devices  49.6 us (28%)
  local copies, waits for them, and re-layouts  15.4 us (9%)
  between operations  14.4 us (8%)
  other arithmetic  6.83 us (4%)
  matrix products  6.09 us (3%)
    all_to_all x3, waiting for transfers between devices, exchanged(): return lax.all_to_all(x, 'ep', split_axis=0, concat_axis=0, tiled=True)  44 us
    all_to_all x3, starting transfers between devices, exchanged(): return lax.all_to_all(x, 'ep', split_axis=0, concat_axis=0, tiled=True)  24.2 us
    all_to_all x2, starting transfers between devices, exchanged_chips(): lax.all_to_all(x, 'ep', split_axis=0, concat_axis=0, tiled=True, axis_ind...  14.1 us
    reduce_scatter x1, waiting for transfers between devices, body(): half_share = lax.psum_scatter(terms, 'rep', scatter_dimension=0, tiled=True)  14.1 us
    reduce_scatter x1, waiting for transfers between devices, body(): lax.psum_scatter((product * width_scale).astype(jnp.bfloat16), 'rep', sca...  13.8 us
    all_to_all x2, waiting for transfers between devices, exchanged_chips(): lax.all_to_all(x, 'ep', split_axis=0, concat_axis=0, tiled=True, axis_ind...  11.8 us
    ppermute x2, starting transfers between devices, swapped(): lax.ppermute(x, 'ep', [(i, i ^ 1) for i in range(lax.axis_size('ep'))])  11.3 us
    unnamed x19, local copies, waits for them, and re-layouts  6.29 us
  transfers between devices with their start and end apart: 9, of which 8 were waited for; matrix products, arithmetic and copies ran while one was open for 10% of the time, Pallas kernels for 0%

profile of v7, /device:TPU:1, one launch (start us, length us, event | category | flops | bytes accessed | tf_op | source)
XLA Modules:
  0.0 177.3 jit_solution(4924696380682167283)
XLA Ops:
  7.2 0.0 copy-start
  7.2 0.0 reduce-scatter.3.cloned.1.call-start
  7.2 8.9 %collective-permute-start = (bf16[320,384]{1,0:T(8,128)(2,1)}, bf16[320,384]{1,0:T(8,128)(2,1)S(1)}, u32[]{:S(2)}, u32[]{:S(2)}) collective-permute-start(bf16[320,384]{1,0:T(8,128)(2,1)} %bitcast.59), channel_id=1, source_target_pairs={{0,1},{1,0},{2,3},{3,2},{4,5},{5,4},{6,7},{7,6},{8,9},{9,8},{10,11... | collective-permute-start | bytes 737288 | tf_op jit(solution)/shard_map/ppermute | solution.py:18
  16.2 1.3 collective-permute-done
  17.5 1.2 maximum_select_fusion.1
  18.7 3.5 %fusion.1 = bf16[2048,768]{0,1:T(8,128)(2,1)} fusion(bf16[320,768]{1,0:T(8,128)(2,1)S(1)} %maximum_select_fusion.1, bf16[1,1,320,2048]{3,2,1,0:T(8,128)(2,1)S(1)} %copy-done), kind=kOutput, calls=%fused_computation.5 | convolution fusion | flops 1009778688 | bytes 4947968 | tf_op jit(solution)/shard_map/dot_general | solution.py:72
  22.2 0.0 reduce-scatter.3.cloned.1.call-update
  22.2 0.7 copy-done.3
  22.9 0.1 copy.45
  23.0 0.1 eq.95
  23.0 0.1 eq.91
  23.2 1.2 reduce-window.6
  24.3 0.2 slice_reduce_fusion
  24.6 0.1 select_reduce_fusion.1
  24.7 0.1 add.73
  24.8 0.4 convert_reduce_fusion
  25.3 0.1 fusion.21
  25.4 0.3 convolution_convert_fusion.1
  25.7 0.1 stack_reshape.8
  25.7 0.3 convolution_convert_fusion
  26.0 0.1 stack_reshape.9
  26.1 0.1 pad_maximum_fusion
  26.2 0.9 copy.58
  27.1 5.1 %all-to-all-start = ((bf16[64,20,256]{2,1,0:T(8,128)(2,1)}), bf16[64,20,256]{2,1,0:T(8,128)(2,1)S(1)}, u32[]{:S(2)}, u32[]{:S(2)}) async-start(bf16[64,20,256]{2,1,0:T(8,128)(2,1)} %bitcast.4), calls=%async_computation | async-start | bytes 1572864 | tf_op jit(solution)/shard_map/all_to_all | solution.py:22
  32.3 0.0 reduce-scatter.5.cloned.1.call-start
  32.3 0.9 copy.44
  33.2 1.4 copy.52
  34.6 2.3 %copy.53 = f32[1,1,256,768]{2,3,1,0:T(8,128)} copy(f32[1,1,256,768]{3,2,1,0:T(8,128)} %param.14) | data formatting | bytes 1572864 | tf_op args[4]
  37.0 18.0 %all-to-all-done = bf16[64,20,256]{2,1,0:T(8,128)(2,1)S(1)} async-done(((bf16[64,20,256]{2,1,0:T(8,128)(2,1)}), bf16[64,20,256]{2,1,0:T(8,128)(2,1)S(1)}, u32[]{:S(2)}, u32[]{:S(2)}) %all-to-all-start) | async-done | bytes 655392 | tf_op jit(solution)/shard_map/all_to_all | solution.py:22
  55.0 0.1 reshape.210
  55.2 13.8 %reduce-scatter.3.cloned.1.call-done = bf16[256,768]{0,1:T(8,128)(2,1)} async-done(((bf16[2048,768]{0,1:T(8,128)(2,1)}), bf16[256,768]{0,1:T(8,128)(2,1)}) %reduce-scatter.3.cloned.1.call-update) | async-done | bytes 393232 | tf_op jit(solution)/shard_map/reduce_scatter | solution.py:75
  68.9 2.1 %fusion.5 = bf16[256,768]{0,1:T(8,128)(2,1)S(1)} fusion(bf16[256,768]{0,1:T(8,128)(2,1)} %bitcast.57, bf16[256,768]{0,1:T(8,128)(2,1)} %reduce-scatter.3.cloned.1.call-done, f32[1,1,256,768]{2,3,1,0:T(8,128)} %copy.53, f32[1,1,256,768]{2,3,1,0:T(8,128)S(1)} %copy.52), kind=kLoop, calls=%fused_computation.19 | loop fusion | flops 3538944 | bytes 2752512 | tf_op jit(solution)/shard_map/convert_element_type | solution.py:105
  71.0 2.0 %fusion = bf16[768,1280]{1,0:T(8,128)(2,1)} fusion(bf16[256,768]{0,1:T(8,128)(2,1)S(1)} %fusion.5, bf16[1280,256]{1,0:T(8,128)(2,1)S(1)} %reshape.210), kind=kOutput, calls=%fused_computation.4 | convolution fusion | flops 505282560 | bytes 3014656 | tf_op jit(solution)/shard_map/dot_general | solution.py:108
  73.0 0.0 reduce-scatter.5.cloned.1.call-update
  73.0 0.9 copy.54
  74.0 9.4 %all-to-all-start.1 = ((bf16[32,8,768]{2,1,0:T(8,128)(2,1)}), bf16[32,8,768]{2,1,0:T(8,128)(2,1)S(1)}, u32[]{:S(2)}, u32[]{:S(2)}) async-start(bf16[32,8,768]{2,1,0:T(8,128)(2,1)} %bitcast.10), calls=%async_computation.2 | async-start | bytes 786432 | tf_op jit(solution)/shard_map/all_to_all | solution.py:28
  83.4 0.1 select_reduce_fusion.2
  83.5 0.1 convert_reduce_fusion.2
  83.6 0.1 reshape.212
  83.7 0.1 rev.3
  83.8 0.1 reshape.213
  83.9 10.9 %all-to-all-done.1 = bf16[32,8,768]{2,1,0:T(8,128)(2,1)S(1)} async-done(((bf16[32,8,768]{2,1,0:T(8,128)(2,1)}), bf16[32,8,768]{2,1,0:T(8,128)(2,1)S(1)}, u32[]{:S(2)}, u32[]{:S(2)}) %all-to-all-start.1) | async-done | bytes 393248 | tf_op jit(solution)/shard_map/all_to_all | solution.py:28
  94.8 1.5 gather_fusion
  96.3 4.7 %all-to-all-start.2 = ((bf16[32,16,768]{2,1,0:T(8,128)(2,1)}), bf16[32,16,768]{2,1,0:T(8,128)(2,1)S(1)}, u32[]{:S(2)}, u32[]{:S(2)}) async-start(bf16[32,16,768]{2,1,0:T(8,128)(2,1)} %bitcast.12), calls=%async_computation.3 | async-start | bytes 1572864 | tf_op jit(solution)/shard_map/all_to_all | solution.py:28
  101.0 0.1 copy.55
  101.1 0.1 reshape.218
  101.2 0.2 select_reduce_fusion
  101.4 0.1 mul.109
  101.5 14.1 %reduce-scatter.5.cloned.1.call-done = bf16[96,1280]{1,0:T(8,128)(2,1)} async-done(((bf16[768,1280]{1,0:T(8,128)(2,1)}), bf16[96,1280]{1,0:T(8,128)(2,1)}) %reduce-scatter.5.cloned.1.call-update) | async-done | bytes 245776 | tf_op jit(solution)/shard_map/reduce_scatter | solution.py:113
  115.5 1.2 copy.56
  116.7 0.8 reshape.216
  117.6 0.9 all-to-all-done.2
  118.5 13.5 %all-to-all-start.3 = ((bf16[64,20,96]{2,1,0:T(8,128)(2,1)}), bf16[64,20,96]{2,1,0:T(8,128)(2,1)S(1)}, u32[]{:S(2)}, u32[]{:S(2)}) async-start(bf16[64,20,96]{2,1,0:T(8,128)(2,1)} %bitcast.16), calls=%async_computation.5 | async-start | bytes 786432 | tf_op jit(solution)/shard_map/all_to_all | solution.py:22
  132.1 0.8 slice_bitcast_fusion.1
  132.9 2.4 %collective-permute-start.1 = (bf16[256,768]{1,0:T(8,128)(2,1)}, bf16[256,768]{1,0:T(8,128)(2,1)S(1)}, u32[]{:S(2)}, u32[]{:S(2)}) collective-permute-start(bf16[256,768]{1,0:T(8,128)(2,1)} %get-tuple-element.14), channel_id=1, source_target_pairs={{0,1},{1,0},{2,3},{3,2},{4,5},{5,4},{6,7},{7,6},{8,9},{9,8},{10,11... | collective-permute-start | bytes 1179656 | tf_op jit(solution)/shard_map/ppermute | solution.py:18
  135.2 11.9 %all-to-all-done.3 = bf16[64,20,96]{2,1,0:T(8,128)(2,1)S(1)} async-done(((bf16[64,20,96]{2,1,0:T(8,128)(2,1)}), bf16[64,20,96]{2,1,0:T(8,128)(2,1)S(1)}, u32[]{:S(2)}, u32[]{:S(2)}) %all-to-all-start.3) | async-done | bytes 245792 | tf_op jit(solution)/shard_map/all_to_all | solution.py:22
  147.1 0.1 convert_reduce_fusion.1
  147.2 0.2 multiply_convert_fusion.1
  147.4 1.4 gather_fusion.1
  148.8 5.6 %all-to-all-start.4 = ((bf16[64,20,96]{2,1,0:T(8,128)(2,1)}), bf16[64,20,96]{2,1,0:T(8,128)(2,1)S(1)}, u32[]{:S(2)}, u32[]{:S(2)}) async-start(bf16[64,20,96]{2,1,0:T(8,128)(2,1)} %gather_fusion.1), calls=%async_computation.6 | async-start | bytes 786432 | tf_op jit(solution)/shard_map/all_to_all | solution.py:22
  154.4 1.0 maximum_select_fusion
  155.4 14.0 %all-to-all-done.4 = bf16[64,20,96]{2,1,0:T(8,128)(2,1)S(1)} async-done(((bf16[64,20,96]{2,1,0:T(8,128)(2,1)}), bf16[64,20,96]{2,1,0:T(8,128)(2,1)S(1)}, u32[]{:S(2)}, u32[]{:S(2)}) %all-to-all-start.4) | async-done | bytes 245792 | tf_op jit(solution)/shard_map/all_to_all | solution.py:22
  169.4 0.1 reshape.217
  169.6 0.9 copy.57
  (23 shorter events, 0.2 us)
Async XLA Ops:
  7.2 11.5 %copy-start = (bf16[1,1,320,2048]{3,2,1,0:T(8,128)(2,1)S(1)}, bf16[1,1,320,2048]{3,2,1,0:T(8,128)(2,1)}, u32[]{:S(2)}) copy-start(bf16[1,1,320,2048]{3,2,1,0:T(8,128)(2,1)} %param.10) | copy-start | bytes 3932164
  7.2 61.7 %reduce-scatter.3.cloned.1.call-start = ((), (), s32[]{:S(2)}) async-start(), calls=%async_computation.7 | async-start | bytes 3538944 | tf_op jit(solution)/shard_map/reduce_scatter | solution.py:75
  7.2 10.3 %collective-permute-start = (bf16[320,384]{1,0:T(8,128)(2,1)}, bf16[320,384]{1,0:T(8,128)(2,1)S(1)}, u32[]{:S(2)}, u32[]{:S(2)}) collective-permute-start(bf16[320,384]{1,0:T(8,128)(2,1)} %bitcast.59), channel_id=1, source_target_pairs={{0,1},{1,0},{2,3},{3,2},{4,5},{5,4},{6,7},{7,6},{8,9},{9,8},{10,11... | collective-permute-start | bytes 737288 | tf_op jit(solution)/shard_map/ppermute | solution.py:18
  22.2 0.7 copy-start.3
  22.2 2.4 %copy-start.4 = (s32[32]{0:T(128)S(1)}, s32[32]{0:T(128)}, u32[]{:S(2)}) copy-start(s32[32]{0:T(128)} %param.18) | copy-start | bytes 388
  22.2 3.1 %copy-start.2 = (bf16[64,2,256]{2,1,0:T(2,128)(2,1)S(1)}, bf16[64,2,256]{2,1,0:T(2,128)(2,1)}, u32[]{:S(2)}) copy-start(bf16[64,2,256]{2,1,0:T(2,128)(2,1)} %param.15) | copy-start | bytes 196612
  26.2 6.1 %copy-start.1 = (bf16[1,1,256,768]{3,2,1,0:T(8,128)(2,1)S(1)}, bf16[1,1,256,768]{3,2,1,0:T(8,128)(2,1)}, u32[]{:S(2)}) copy-start(bf16[1,1,256,768]{3,2,1,0:T(8,128)(2,1)} %param.12) | copy-start | bytes 1179652
  27.1 27.9 %all-to-all-start = ((bf16[64,20,256]{2,1,0:T(8,128)(2,1)}), bf16[64,20,256]{2,1,0:T(8,128)(2,1)S(1)}, u32[]{:S(2)}, u32[]{:S(2)}) async-start(bf16[64,20,256]{2,1,0:T(8,128)(2,1)} %bitcast.4), calls=%async_computation | async-start | bytes 1572864 | tf_op jit(solution)/shard_map/all_to_all | solution.py:22
  32.3 83.3 %reduce-scatter.5.cloned.1.call-start = ((), (), s32[]{:S(2)}) async-start(), calls=%async_computation.8 | async-start | bytes 2211840 | tf_op jit(solution)/shard_map/reduce_scatter | solution.py:113
  73.0 10.4 %copy-start.6 = (s32[64]{0:T(128)S(1)}, s32[64]{0:T(128)}, u32[]{:S(2)}) copy-start(s32[64]{0:T(128)} %param.19) | copy-start | bytes 772
  74.0 20.9 %all-to-all-start.1 = ((bf16[32,8,768]{2,1,0:T(8,128)(2,1)}), bf16[32,8,768]{2,1,0:T(8,128)(2,1)S(1)}, u32[]{:S(2)}, u32[]{:S(2)}) async-start(bf16[32,8,768]{2,1,0:T(8,128)(2,1)} %bitcast.10), calls=%async_computation.2 | async-start | bytes 786432 | tf_op jit(solution)/shard_map/all_to_all | solution.py:28
  83.9 17.0 %copy-start.5 = (bf16[64,8]{0,1:T(8,128)(2,1)S(1)}, bf16[64,8]{0,1:T(8,128)(2,1)}, u32[]{:S(2)}) copy-start(bf16[64,8]{0,1:T(8,128)(2,1)} %param.17) | copy-start | bytes 3076
  96.3 22.2 %all-to-all-start.2 = ((bf16[32,16,768]{2,1,0:T(8,128)(2,1)}), bf16[32,16,768]{2,1,0:T(8,128)(2,1)S(1)}, u32[]{:S(2)}, u32[]{:S(2)}) async-start(bf16[32,16,768]{2,1,0:T(8,128)(2,1)} %bitcast.12), calls=%async_computation.3 | async-start | bytes 1572864 | tf_op jit(solution)/shard_map/all_to_all | solution.py:28
  118.5 28.6 %all-to-all-start.3 = ((bf16[64,20,96]{2,1,0:T(8,128)(2,1)}), bf16[64,20,96]{2,1,0:T(8,128)(2,1)S(1)}, u32[]{:S(2)}, u32[]{:S(2)}) async-start(bf16[64,20,96]{2,1,0:T(8,128)(2,1)} %bitcast.16), calls=%async_computation.5 | async-start | bytes 786432 | tf_op jit(solution)/shard_map/all_to_all | solution.py:22
  132.9 21.5 %collective-permute-start.1 = (bf16[256,768]{1,0:T(8,128)(2,1)}, bf16[256,768]{1,0:T(8,128)(2,1)S(1)}, u32[]{:S(2)}, u32[]{:S(2)}) collective-permute-start(bf16[256,768]{1,0:T(8,128)(2,1)} %get-tuple-element.14), channel_id=1, source_target_pairs={{0,1},{1,0},{2,3},{3,2},{4,5},{5,4},{6,7},{7,6},{8,9},{9,8},{10,11... | collective-permute-start | bytes 1179656 | tf_op jit(solution)/shard_map/ppermute | solution.py:18
  148.8 20.7 %all-to-all-start.4 = ((bf16[64,20,96]{2,1,0:T(8,128)(2,1)}), bf16[64,20,96]{2,1,0:T(8,128)(2,1)S(1)}, u32[]{:S(2)}, u32[]{:S(2)}) async-start(bf16[64,20,96]{2,1,0:T(8,128)(2,1)} %gather_fusion.1), calls=%async_computation.6 | async-start | bytes 786432 | tf_op jit(solution)/shard_map/all_to_all | solution.py:22
Sparse Core Ops, SparseCore 0:
  22.3 46.5 reduce-scatter.2
  73.2 42.3 reduce-scatter.4

commit v8 on v6

--- a/solution.py
+++ b/solution.py
@@ -62,11 +62,16 @@
     device_ids = jnp.arange(ep_count, dtype=jnp.int32)
 
     own_cotan = train_cotan[0, 0]
+    half_hidden = own_cotan.shape[1]
+    own_twice = lax.optimization_barrier(jnp.concatenate([own_cotan, own_cotan], axis=1))
     partner_cotan = swapped(own_cotan)
-    full_cotan = jnp.where(
-        is_upper,
-        jnp.concatenate([partner_cotan, own_cotan], axis=1),
-        jnp.concatenate([own_cotan, partner_cotan], axis=1),
+    upper_columns = jnp.arange(2 * half_hidden, dtype=jnp.int32)[None, :] >= half_hidden
+    full_cotan = lax.optimization_barrier(
+        jnp.where(
+            upper_columns != is_upper,
+            jnp.concatenate([partner_cotan, partner_cotan], axis=1),
+            own_twice,
+        )
     )
     product = lax.dot_general(
         acts_local, full_cotan, (((0,), (0,)), ((), ())), preferred_element_type=jnp.float32
@@ -118,7 +123,7 @@
     ).astype(jnp.bfloat16)
     half_share = lax.psum_scatter(terms, "rep", scatter_dimension=0, tiled=True)
     own_share = half_share[:, :slot_count]
-    partner_share = swapped(half_share[:, slot_count:])
+    partner_share = swapped(half_share)[:, slot_count:]
     preact_share = (
         own_share.astype(jnp.float32) + partner_share.astype(jnp.float32)
     ).astype(jnp.bfloat16)

time: 177 us -> 175 us (0.989)
  transfers between devices with their start and end apart: 10 -> 10, of which waited for: 8 -> 8; matrix products, arithmetic and copies ran while one was open for 13% -> 14% of each run, Pallas kernels for 0% -> 0%
where the time goes in v8:
time: 175 us
  waiting for transfers between devices  74.6 us (43%)
  starting transfers between devices  52.6 us (30%)
  local copies, waits for them, and re-layouts  17.3 us (10%)
  between operations  14.4 us (8%)
  other arithmetic  9.62 us (5%)
  matrix products  6.09 us (3%)
    all_to_all x2, waiting for transfers between devices, exchanged(): return lax.all_to_all(x, 'ep', split_axis=0, concat_axis=0, tiled=True)  32.2 us
    all_to_all x3, starting transfers between devices, exchanged_chips(): lax.all_to_all(x, 'ep', split_axis=0, concat_axis=0, tiled=True, axis_ind...  22.9 us
    all_to_all x3, waiting for transfers between devices, exchanged_chips(): lax.all_to_all(x, 'ep', split_axis=0, concat_axis=0, tiled=True, axis_ind...  18.9 us
    ppermute x3, starting transfers between devices, swapped(): lax.ppermute(x, 'ep', [(i, i ^ 1) for i in range(lax.axis_size('ep'))])  18.4 us
    reduce_scatter x1, waiting for transfers between devices, body(): half_share = lax.psum_scatter(terms, 'rep', scatter_dimension=0, tiled=True)  14.1 us
    all_to_all x2, starting transfers between devices, exchanged(): return lax.all_to_all(x, 'ep', split_axis=0, concat_axis=0, tiled=True)  11.1 us
    reduce_scatter x1, waiting for transfers between devices, body(): lax.psum_scatter((product * width_scale).astype(jnp.bfloat16), 'rep', sca...  7.93 us
    unnamed x23, local copies, waits for them, and re-layouts  6.29 us
  transfers between devices with their start and end apart: 10, of which 8 were waited for; matrix products, arithmetic and copies ran while one was open for 14% of the time, Pallas kernels for 0%

profile of v8, /device:TPU:1, one launch (start us, length us, event | category | flops | bytes accessed | tf_op | source)
XLA Modules:
  0.0 174.6 jit_solution(14879476981643259044)
XLA Ops:
  7.2 8.9 %collective-permute-start = (bf16[320,384]{1,0:T(8,128)(2,1)}, bf16[320,384]{1,0:T(8,128)(2,1)S(1)}, u32[]{:S(2)}, u32[]{:S(2)}) collective-permute-start(bf16[320,384]{1,0:T(8,128)(2,1)} %bitcast.58), channel_id=1, source_target_pairs={{0,1},{1,0},{2,3},{3,2},{4,5},{5,4},{6,7},{7,6},{8,9},{9,8},{10,11... | collective-permute-start | bytes 737288 | tf_op jit(solution)/shard_map/ppermute | solution.py:18
  16.2 1.1 pad_maximum_fusion.1
  17.3 0.2 collective-permute-done
  17.5 0.1 maximum_select_fusion.2
  17.6 3.5 %fusion.1 = bf16[2048,768]{0,1:T(8,128)(2,1)} fusion(bf16[320,768]{1,0:T(8,128)(2,1)S(1)} %maximum_select_fusion.2, bf16[1,1,320,2048]{3,2,1,0:T(8,128)(2,1)S(1)} %copy-done), kind=kOutput, calls=%fused_computation.5 | convolution fusion | flops 1009778688 | bytes 4947968 | tf_op jit(solution)/shard_map/dot_general | solution.py:76
  21.2 0.7 copy-done.5
  21.8 0.1 copy.49
  21.9 0.1 eq.95
  22.0 0.1 eq.91
  22.1 1.2 reduce-window.6
  23.3 0.2 slice_reduce_fusion
  23.5 0.1 select_reduce_fusion.1
  23.7 0.1 add.76
  23.7 0.4 convert_reduce_fusion
  24.2 0.1 fusion.28
  24.3 0.3 convolution_convert_fusion.1
  24.6 0.1 stack_reshape.8
  24.7 0.3 convolution_convert_fusion
  25.0 0.1 stack_reshape.9
  25.0 0.1 pad_maximum_fusion
  25.1 0.9 copy.65
  26.1 5.1 %all-to-all-start = ((bf16[64,20,256]{2,1,0:T(8,128)(2,1)}), bf16[64,20,256]{2,1,0:T(8,128)(2,1)S(1)}, u32[]{:S(2)}, u32[]{:S(2)}) async-start(bf16[64,20,256]{2,1,0:T(8,128)(2,1)} %bitcast.4), calls=%async_computation | async-start | bytes 1572864 | tf_op jit(solution)/shard_map/all_to_all | solution.py:22
  31.3 0.9 copy.48
  32.2 1.4 copy.59
  33.6 2.3 %copy.60 = f32[1,1,256,768]{2,3,1,0:T(8,128)} copy(f32[1,1,256,768]{3,2,1,0:T(8,128)} %param.14) | data formatting | bytes 1572864 | tf_op args[4]
  35.9 18.0 %all-to-all-done = bf16[64,20,256]{2,1,0:T(8,128)(2,1)S(1)} async-done(((bf16[64,20,256]{2,1,0:T(8,128)(2,1)}), bf16[64,20,256]{2,1,0:T(8,128)(2,1)S(1)}, u32[]{:S(2)}, u32[]{:S(2)}) %all-to-all-start) | async-done | bytes 655392 | tf_op jit(solution)/shard_map/all_to_all | solution.py:22
  54.0 0.9 fusion.27
  54.9 1.1 reshape_squeeze.6
  56.0 1.8 %reshape_squeeze.7 = bf16[640,256]{1,0:T(8,128)(2,1)} reshape(bf16[32,1,20,256]{3,2,1,0:T(8,128)(2,1)} %get-tuple-element.17) | data formatting | bytes 655360 | tf_op jit(solution)/shard_map/reshape;squeeze | solution.py:102
  57.8 2.1 %maximum_select_fusion.1 = bf16[1280,256]{1,0:T(8,128)(2,1)} fusion(bf16[640,256]{1,0:T(8,128)(2,1)} %reshape_squeeze.7, bf16[640,256]{1,0:T(8,128)(2,1)S(1)} %reshape_squeeze.6, pred[]{:T(512)S(6)} %eq.89), kind=kLoop, calls=%fused_computation.29 | loop fusion | flops 2949120 | bytes 1310721 | tf_op jit(solution)/shard_map/jit(_where)/select_n | solution.py:104
  59.9 7.9 %reduce-scatter.3.cloned.1.call-done = bf16[256,768]{0,1:T(8,128)(2,1)} async-done(((bf16[2048,768]{0,1:T(8,128)(2,1)}), bf16[256,768]{0,1:T(8,128)(2,1)}) %reduce-scatter.3.cloned.1.call-update) | async-done | bytes 393232 | tf_op jit(solution)/shard_map/reduce_scatter | solution.py:79
  67.9 1.9 %fusion.5 = bf16[256,768]{0,1:T(8,128)(2,1)S(1)} fusion(bf16[256,768]{0,1:T(8,128)(2,1)} %bitcast.56, bf16[256,768]{0,1:T(8,128)(2,1)} %reduce-scatter.3.cloned.1.call-done, f32[1,1,256,768]{2,3,1,0:T(8,128)S(1)} %copy-done.1, f32[1,1,256,768]{2,3,1,0:T(8,128)S(1)} %copy.59), kind=kLoop, calls=%fused_computation.19 | loop fusion | flops 3538944 | bytes 2752512 | tf_op jit(solution)/shard_map/convert_element_type | solution.py:116
  69.8 2.0 %fusion = bf16[768,1280]{1,0:T(8,128)(2,1)} fusion(bf16[256,768]{0,1:T(8,128)(2,1)S(1)} %fusion.5, bf16[1280,256]{1,0:T(8,128)(2,1)S(1)} %copy-done.2), kind=kOutput, calls=%fused_computation.4 | convolution fusion | flops 505282560 | bytes 3014656 | tf_op jit(solution)/shard_map/dot_general | solution.py:119
  71.8 0.9 copy.61
  72.7 9.4 %all-to-all-start.1 = ((bf16[32,8,768]{2,1,0:T(8,128)(2,1)}), bf16[32,8,768]{2,1,0:T(8,128)(2,1)S(1)}, u32[]{:S(2)}, u32[]{:S(2)}) async-start(bf16[32,8,768]{2,1,0:T(8,128)(2,1)} %bitcast.11), calls=%async_computation.2 | async-start | bytes 786432 | tf_op jit(solution)/shard_map/all_to_all | solution.py:28
  82.1 0.1 select_reduce_fusion.2
  82.2 0.1 convert_reduce_fusion.1
  82.3 0.1 reshape.216
  82.5 0.1 rev.3
  82.5 0.1 reshape.217
  82.7 10.9 %all-to-all-done.1 = bf16[32,8,768]{2,1,0:T(8,128)(2,1)S(1)} async-done(((bf16[32,8,768]{2,1,0:T(8,128)(2,1)}), bf16[32,8,768]{2,1,0:T(8,128)(2,1)S(1)}, u32[]{:S(2)}, u32[]{:S(2)}) %all-to-all-start.1) | async-done | bytes 393248 | tf_op jit(solution)/shard_map/all_to_all | solution.py:28
  93.6 1.5 gather_fusion
  95.1 4.6 %all-to-all-start.2 = ((bf16[32,16,768]{2,1,0:T(8,128)(2,1)}), bf16[32,16,768]{2,1,0:T(8,128)(2,1)S(1)}, u32[]{:S(2)}, u32[]{:S(2)}) async-start(bf16[32,16,768]{2,1,0:T(8,128)(2,1)} %bitcast.13), calls=%async_computation.3 | async-start | bytes 1572864 | tf_op jit(solution)/shard_map/all_to_all | solution.py:28
  99.7 0.1 copy.62
  99.8 0.1 reshape.222
  99.9 0.2 select_reduce_fusion
  100.1 0.1 mul.109
  100.2 14.1 %reduce-scatter.5.cloned.1.call-done = bf16[96,1280]{1,0:T(8,128)(2,1)} async-done(((bf16[768,1280]{1,0:T(8,128)(2,1)}), bf16[96,1280]{1,0:T(8,128)(2,1)}) %reduce-scatter.5.cloned.1.call-update) | async-done | bytes 245776 | tf_op jit(solution)/shard_map/reduce_scatter | solution.py:124
  114.3 7.0 %collective-permute-start.2 = (bf16[96,1280]{1,0:T(8,128)(2,1)}, bf16[96,1280]{1,0:T(8,128)(2,1)S(1)}, u32[]{:S(2)}, u32[]{:S(2)}) collective-permute-start(bf16[96,1280]{1,0:T(8,128)(2,1)} %reduce-scatter.5.cloned.1.call-done), channel_id=1, source_target_pairs={{0,1},{1,0},{2,3},{3,2},{4,5},{5,4},{6,7},{7,6},{8,9},{9,8},{10,11... | collective-permute-start | bytes 737288 | tf_op jit(solution)/shard_map/ppermute | solution.py:18
  121.3 1.3 collective-permute-done.2
  122.6 0.9 add_convert_fusion
  123.6 0.2 copy.63
  123.7 0.7 reshape.220
  124.5 8.9 %all-to-all-start.3 = ((bf16[32,20,96]{2,1,0:T(8,128)(2,1)}), bf16[32,20,96]{2,1,0:T(8,128)(2,1)S(1)}, u32[]{:S(2)}, u32[]{:S(2)}) async-start(bf16[32,20,96]{2,1,0:T(8,128)(2,1)} %bitcast.17), calls=%async_computation.5 | async-start | bytes 393216 | tf_op jit(solution)/shard_map/all_to_all | solution.py:28
  133.4 0.1 slice_bitcast_fusion.1
  133.5 2.6 %collective-permute-start.1 = (bf16[256,768]{1,0:T(8,128)(2,1)S(1)}, bf16[256,768]{1,0:T(8,128)(2,1)S(1)}, u32[]{:S(2)}, u32[]{:S(2)}) collective-permute-start(bf16[256,768]{1,0:T(8,128)(2,1)S(1)} %get-tuple-element.14), channel_id=1, source_target_pairs={{0,1},{1,0},{2,3},{3,2},{4,5},{5,4},{6,7},{7,6},{8,9},{9,8},{10,11... | collective-permute-start | bytes 1179656 | tf_op jit(solution)/shard_map/ppermute | solution.py:18
  136.0 8.0 %all-to-all-done.3 = bf16[32,20,96]{2,1,0:T(8,128)(2,1)S(1)} async-done(((bf16[32,20,96]{2,1,0:T(8,128)(2,1)}), bf16[32,20,96]{2,1,0:T(8,128)(2,1)S(1)}, u32[]{:S(2)}, u32[]{:S(2)}) %all-to-all-start.3) | async-done | bytes 122912 | tf_op jit(solution)/shard_map/all_to_all | solution.py:28
  144.0 0.2 fusion.17
  144.2 1.4 gather_fusion.1
  145.6 6.0 %all-to-all-start.4 = ((bf16[64,20,96]{2,1,0:T(8,128)(2,1)}), bf16[64,20,96]{2,1,0:T(8,128)(2,1)S(1)}, u32[]{:S(2)}, u32[]{:S(2)}) async-start(bf16[64,20,96]{2,1,0:T(8,128)(2,1)} %gather_fusion.1), calls=%async_computation.6 | async-start | bytes 786432 | tf_op jit(solution)/shard_map/all_to_all | solution.py:22
  151.6 1.0 maximum_select_fusion
  152.6 14.2 %all-to-all-done.4 = bf16[64,20,96]{2,1,0:T(8,128)(2,1)S(1)} async-done(((bf16[64,20,96]{2,1,0:T(8,128)(2,1)}), bf16[64,20,96]{2,1,0:T(8,128)(2,1)S(1)}, u32[]{:S(2)}, u32[]{:S(2)}) %all-to-all-start.4) | async-done | bytes 245792 | tf_op jit(solution)/shard_map/all_to_all | solution.py:22
  166.8 0.1 reshape.221
  166.9 0.9 copy.64
  (34 shorter events, 0.3 us)
Async XLA Ops:
  7.2 10.4 %copy-start = (bf16[1,1,320,2048]{3,2,1,0:T(8,128)(2,1)S(1)}, bf16[1,1,320,2048]{3,2,1,0:T(8,128)(2,1)}, u32[]{:S(2)}) copy-start(bf16[1,1,320,2048]{3,2,1,0:T(8,128)(2,1)} %param.10) | copy-start | bytes 3932164
  7.2 60.7 %reduce-scatter.3.cloned.1.call-start = ((), (), s32[]{:S(2)}) async-start(), calls=%async_computation.7 | async-start | bytes 3538944 | tf_op jit(solution)/shard_map/reduce_scatter | solution.py:79
  7.2 10.3 %collective-permute-start = (bf16[320,384]{1,0:T(8,128)(2,1)}, bf16[320,384]{1,0:T(8,128)(2,1)S(1)}, u32[]{:S(2)}, u32[]{:S(2)}) collective-permute-start(bf16[320,384]{1,0:T(8,128)(2,1)} %bitcast.58), channel_id=1, source_target_pairs={{0,1},{1,0},{2,3},{3,2},{4,5},{5,4},{6,7},{7,6},{8,9},{9,8},{10,11... | collective-permute-start | bytes 737288 | tf_op jit(solution)/shard_map/ppermute | solution.py:18
  21.1 0.7 copy-start.5
  21.1 2.4 %copy-start.6 = (s32[32]{0:T(128)S(1)}, s32[32]{0:T(128)}, u32[]{:S(2)}) copy-start(s32[32]{0:T(128)} %param.18) | copy-start | bytes 388
  21.1 3.1 %copy-start.4 = (bf16[64,2,256]{2,1,0:T(2,128)(2,1)S(1)}, bf16[64,2,256]{2,1,0:T(2,128)(2,1)}, u32[]{:S(2)}) copy-start(bf16[64,2,256]{2,1,0:T(2,128)(2,1)} %param.15) | copy-start | bytes 196612
  25.1 6.1 %copy-start.3 = (bf16[1,1,256,768]{3,2,1,0:T(8,128)(2,1)S(1)}, bf16[1,1,256,768]{3,2,1,0:T(8,128)(2,1)}, u32[]{:S(2)}) copy-start(bf16[1,1,256,768]{3,2,1,0:T(8,128)(2,1)} %param.12) | copy-start | bytes 1179652
  26.1 27.9 %all-to-all-start = ((bf16[64,20,256]{2,1,0:T(8,128)(2,1)}), bf16[64,20,256]{2,1,0:T(8,128)(2,1)S(1)}, u32[]{:S(2)}, u32[]{:S(2)}) async-start(bf16[64,20,256]{2,1,0:T(8,128)(2,1)} %bitcast.4), calls=%async_computation | async-start | bytes 1572864 | tf_op jit(solution)/shard_map/all_to_all | solution.py:22
  31.2 83.1 %reduce-scatter.5.cloned.1.call-start = ((), (), s32[]{:S(2)}) async-start(), calls=%async_computation.8 | async-start | bytes 2211840 | tf_op jit(solution)/shard_map/reduce_scatter | solution.py:124
  54.9 13.0 %copy-start.1 = (f32[1,1,256,768]{2,3,1,0:T(8,128)S(1)}, f32[1,1,256,768]{2,3,1,0:T(8,128)}, u32[]{:S(2)}) copy-start(f32[1,1,256,768]{2,3,1,0:T(8,128)} %copy.60) | copy-start | bytes 2359300
  67.9 1.9 %copy-start.2 = (bf16[1280,256]{1,0:T(8,128)(2,1)S(1)}, bf16[1280,256]{1,0:T(8,128)(2,1)}, u32[]{:S(2)}) copy-start(bf16[1280,256]{1,0:T(8,128)(2,1)} %maximum_select_fusion.1) | copy-start | bytes 1966084
  71.8 10.3 %copy-start.8 = (s32[64]{0:T(128)S(1)}, s32[64]{0:T(128)}, u32[]{:S(2)}) copy-start(s32[64]{0:T(128)} %param.19) | copy-start | bytes 772
  72.7 20.9 %all-to-all-start.1 = ((bf16[32,8,768]{2,1,0:T(8,128)(2,1)}), bf16[32,8,768]{2,1,0:T(8,128)(2,1)S(1)}, u32[]{:S(2)}, u32[]{:S(2)}) async-start(bf16[32,8,768]{2,1,0:T(8,128)(2,1)} %bitcast.11), calls=%async_computation.2 | async-start | bytes 786432 | tf_op jit(solution)/shard_map/all_to_all | solution.py:28
  82.7 17.0 %copy-start.7 = (bf16[64,8]{0,1:T(8,128)(2,1)S(1)}, bf16[64,8]{0,1:T(8,128)(2,1)}, u32[]{:S(2)}) copy-start(bf16[64,8]{0,1:T(8,128)(2,1)} %param.17) | copy-start | bytes 3076
  95.1 29.4 %all-to-all-start.2 = ((bf16[32,16,768]{2,1,0:T(8,128)(2,1)}), bf16[32,16,768]{2,1,0:T(8,128)(2,1)S(1)}, u32[]{:S(2)}, u32[]{:S(2)}) async-start(bf16[32,16,768]{2,1,0:T(8,128)(2,1)} %bitcast.13), calls=%async_computation.3 | async-start | bytes 1572864 | tf_op jit(solution)/shard_map/all_to_all | solution.py:28
  114.3 8.3 %collective-permute-start.2 = (bf16[96,1280]{1,0:T(8,128)(2,1)}, bf16[96,1280]{1,0:T(8,128)(2,1)S(1)}, u32[]{:S(2)}, u32[]{:S(2)}) collective-permute-start(bf16[96,1280]{1,0:T(8,128)(2,1)} %reduce-scatter.5.cloned.1.call-done), channel_id=1, source_target_pairs={{0,1},{1,0},{2,3},{3,2},{4,5},{5,4},{6,7},{7,6},{8,9},{9,8},{10,11... | collective-permute-start | bytes 737288 | tf_op jit(solution)/shard_map/ppermute | solution.py:18
  124.5 19.5 %all-to-all-start.3 = ((bf16[32,20,96]{2,1,0:T(8,128)(2,1)}), bf16[32,20,96]{2,1,0:T(8,128)(2,1)S(1)}, u32[]{:S(2)}, u32[]{:S(2)}) async-start(bf16[32,20,96]{2,1,0:T(8,128)(2,1)} %bitcast.17), calls=%async_computation.5 | async-start | bytes 393216 | tf_op jit(solution)/shard_map/all_to_all | solution.py:28
  133.5 18.1 %collective-permute-start.1 = (bf16[256,768]{1,0:T(8,128)(2,1)S(1)}, bf16[256,768]{1,0:T(8,128)(2,1)S(1)}, u32[]{:S(2)}, u32[]{:S(2)}) collective-permute-start(bf16[256,768]{1,0:T(8,128)(2,1)S(1)} %get-tuple-element.14), channel_id=1, source_target_pairs={{0,1},{1,0},{2,3},{3,2},{4,5},{5,4},{6,7},{7,6},{8,9},{9,8},{10,11... | collective-permute-start | bytes 1179656 | tf_op jit(solution)/shard_map/ppermute | solution.py:18
  145.6 21.2 %all-to-all-start.4 = ((bf16[64,20,96]{2,1,0:T(8,128)(2,1)}), bf16[64,20,96]{2,1,0:T(8,128)(2,1)S(1)}, u32[]{:S(2)}, u32[]{:S(2)}) async-start(bf16[64,20,96]{2,1,0:T(8,128)(2,1)} %gather_fusion.1), calls=%async_computation.6 | async-start | bytes 786432 | tf_op jit(solution)/shard_map/all_to_all | solution.py:22
Sparse Core Ops, SparseCore 0:
  21.3 46.5 reduce-scatter.2
  71.9 42.3 reduce-scatter.4

commit v9 on v8

--- a/solution.py
+++ b/solution.py
@@ -122,7 +122,7 @@
         * width_scale
     ).astype(jnp.bfloat16)
     half_share = lax.psum_scatter(terms, "rep", scatter_dimension=0, tiled=True)
-    own_share = half_share[:, :slot_count]
+    own_share = lax.optimization_barrier(half_share[:, :slot_count])
     partner_share = swapped(half_share)[:, slot_count:]
     preact_share = (
         own_share.astype(jnp.float32) + partner_share.astype(jnp.float32)

time: 175 us -> 175 us (level)
  no operation moved by 1% of the time
where the time goes in v9:
time: 175 us; the launch traced here: 174 us
  waiting for transfers between devices  73.7 us (42%)
  starting transfers between devices  52.6 us (30%)
  local copies, waits for them, and re-layouts  18.2 us (10%)
  between operations  14.4 us (8%)
  other arithmetic  8.72 us (5%)
  matrix products  6.09 us (3%)
    all_to_all x2, waiting for transfers between devices, exchanged(): return lax.all_to_all(x, 'ep', split_axis=0, concat_axis=0, tiled=True)  32.2 us
    all_to_all x3, starting transfers between devices, exchanged_chips(): lax.all_to_all(x, 'ep', split_axis=0, concat_axis=0, tiled=True, axis_ind...  22.9 us
    all_to_all x3, waiting for transfers between devices, exchanged_chips(): lax.all_to_all(x, 'ep', split_axis=0, concat_axis=0, tiled=True, axis_ind...  18.9 us
    ppermute x3, starting transfers between devices, swapped(): lax.ppermute(x, 'ep', [(i, i ^ 1) for i in range(lax.axis_size('ep'))])  18.4 us
    reduce_scatter x1, waiting for transfers between devices, body(): half_share = lax.psum_scatter(terms, 'rep', scatter_dimension=0, tiled=True)  14.1 us
    all_to_all x2, starting transfers between devices, exchanged(): return lax.all_to_all(x, 'ep', split_axis=0, concat_axis=0, tiled=True)  11.1 us
    reduce_scatter x1, waiting for transfers between devices, body(): lax.psum_scatter((product * width_scale).astype(jnp.bfloat16), 'rep', sca...  7.93 us
    unnamed x23, local copies, waits for them, and re-layouts  6.29 us
  transfers between devices with their start and end apart: 10, of which 8 were waited for; matrix products, arithmetic and copies ran while one was open for 14% of the time, Pallas kernels for 0%

profile of v9, /device:TPU:1, one launch (start us, length us, event | category | flops | bytes accessed | tf_op | source)
XLA Modules:
  0.0 173.7 jit_solution(2970023109984071908)
XLA Ops:
  7.2 8.9 %collective-permute-start = (bf16[320,384]{1,0:T(8,128)(2,1)}, bf16[320,384]{1,0:T(8,128)(2,1)S(1)}, u32[]{:S(2)}, u32[]{:S(2)}) collective-permute-start(bf16[320,384]{1,0:T(8,128)(2,1)} %bitcast.58), channel_id=1, source_target_pairs={{0,1},{1,0},{2,3},{3,2},{4,5},{5,4},{6,7},{7,6},{8,9},{9,8},{10,11... | collective-permute-start | bytes 737288 | tf_op jit(solution)/shard_map/ppermute | solution.py:18
  16.2 1.1 pad_maximum_fusion.1
  17.3 0.2 collective-permute-done
  17.5 0.1 maximum_select_fusion.2
  17.6 3.5 %fusion.1 = bf16[2048,768]{0,1:T(8,128)(2,1)} fusion(bf16[320,768]{1,0:T(8,128)(2,1)S(1)} %maximum_select_fusion.2, bf16[1,1,320,2048]{3,2,1,0:T(8,128)(2,1)S(1)} %copy-done), kind=kOutput, calls=%fused_computation.5 | convolution fusion | flops 1009778688 | bytes 4947968 | tf_op jit(solution)/shard_map/dot_general | solution.py:76
  21.2 0.7 copy-done.5
  21.8 0.1 copy.49
  21.9 0.1 eq.95
  22.0 0.1 eq.91
  22.1 1.2 reduce-window.6
  23.3 0.2 slice_reduce_fusion
  23.5 0.1 select_reduce_fusion.1
  23.7 0.1 add.76
  23.7 0.4 convert_reduce_fusion
  24.2 0.1 fusion.28
  24.3 0.3 convolution_convert_fusion.1
  24.6 0.1 stack_reshape.8
  24.7 0.3 convolution_convert_fusion
  25.0 0.1 stack_reshape.9
  25.0 0.1 pad_maximum_fusion
  25.1 0.9 copy.65
  26.1 5.1 %all-to-all-start = ((bf16[64,20,256]{2,1,0:T(8,128)(2,1)}), bf16[64,20,256]{2,1,0:T(8,128)(2,1)S(1)}, u32[]{:S(2)}, u32[]{:S(2)}) async-start(bf16[64,20,256]{2,1,0:T(8,128)(2,1)} %bitcast.4), calls=%async_computation | async-start | bytes 1572864 | tf_op jit(solution)/shard_map/all_to_all | solution.py:22
  31.3 0.9 copy.48
  32.2 1.4 copy.59
  33.6 2.3 %copy.60 = f32[1,1,256,768]{2,3,1,0:T(8,128)} copy(f32[1,1,256,768]{3,2,1,0:T(8,128)} %param.14) | data formatting | bytes 1572864 | tf_op args[4]
  35.9 18.0 %all-to-all-done = bf16[64,20,256]{2,1,0:T(8,128)(2,1)S(1)} async-done(((bf16[64,20,256]{2,1,0:T(8,128)(2,1)}), bf16[64,20,256]{2,1,0:T(8,128)(2,1)S(1)}, u32[]{:S(2)}, u32[]{:S(2)}) %all-to-all-start) | async-done | bytes 655392 | tf_op jit(solution)/shard_map/all_to_all | solution.py:22
  54.0 0.9 fusion.27
  54.9 1.1 reshape_squeeze.6
  56.0 1.8 %reshape_squeeze.7 = bf16[640,256]{1,0:T(8,128)(2,1)} reshape(bf16[32,1,20,256]{3,2,1,0:T(8,128)(2,1)} %get-tuple-element.17) | data formatting | bytes 655360 | tf_op jit(solution)/shard_map/reshape;squeeze | solution.py:102
  57.8 2.1 %maximum_select_fusion.1 = bf16[1280,256]{1,0:T(8,128)(2,1)} fusion(bf16[640,256]{1,0:T(8,128)(2,1)} %reshape_squeeze.7, bf16[640,256]{1,0:T(8,128)(2,1)S(1)} %reshape_squeeze.6, pred[]{:T(512)S(6)} %eq.89), kind=kLoop, calls=%fused_computation.29 | loop fusion | flops 2949120 | bytes 1310721 | tf_op jit(solution)/shard_map/jit(_where)/select_n | solution.py:104
  59.9 7.9 %reduce-scatter.3.cloned.1.call-done = bf16[256,768]{0,1:T(8,128)(2,1)} async-done(((bf16[2048,768]{0,1:T(8,128)(2,1)}), bf16[256,768]{0,1:T(8,128)(2,1)}) %reduce-scatter.3.cloned.1.call-update) | async-done | bytes 393232 | tf_op jit(solution)/shard_map/reduce_scatter | solution.py:79
  67.9 1.9 %fusion.5 = bf16[256,768]{0,1:T(8,128)(2,1)S(1)} fusion(bf16[256,768]{0,1:T(8,128)(2,1)} %bitcast.56, bf16[256,768]{0,1:T(8,128)(2,1)} %reduce-scatter.3.cloned.1.call-done, f32[1,1,256,768]{2,3,1,0:T(8,128)S(1)} %copy-done.1, f32[1,1,256,768]{2,3,1,0:T(8,128)S(1)} %copy.59), kind=kLoop, calls=%fused_computation.19 | loop fusion | flops 3538944 | bytes 2752512 | tf_op jit(solution)/shard_map/convert_element_type | solution.py:116
  69.8 2.0 %fusion = bf16[768,1280]{1,0:T(8,128)(2,1)} fusion(bf16[256,768]{0,1:T(8,128)(2,1)S(1)} %fusion.5, bf16[1280,256]{1,0:T(8,128)(2,1)S(1)} %copy-done.2), kind=kOutput, calls=%fused_computation.4 | convolution fusion | flops 505282560 | bytes 3014656 | tf_op jit(solution)/shard_map/dot_general | solution.py:119
  71.8 0.9 copy.61
  72.7 9.4 %all-to-all-start.1 = ((bf16[32,8,768]{2,1,0:T(8,128)(2,1)}), bf16[32,8,768]{2,1,0:T(8,128)(2,1)S(1)}, u32[]{:S(2)}, u32[]{:S(2)}) async-start(bf16[32,8,768]{2,1,0:T(8,128)(2,1)} %bitcast.11), calls=%async_computation.2 | async-start | bytes 786432 | tf_op jit(solution)/shard_map/all_to_all | solution.py:28
  82.1 0.1 select_reduce_fusion.2
  82.2 0.1 convert_reduce_fusion.1
  82.3 0.1 reshape.216
  82.5 0.1 rev.3
  82.5 0.1 reshape.217
  82.7 10.9 %all-to-all-done.1 = bf16[32,8,768]{2,1,0:T(8,128)(2,1)S(1)} async-done(((bf16[32,8,768]{2,1,0:T(8,128)(2,1)}), bf16[32,8,768]{2,1,0:T(8,128)(2,1)S(1)}, u32[]{:S(2)}, u32[]{:S(2)}) %all-to-all-start.1) | async-done | bytes 393248 | tf_op jit(solution)/shard_map/all_to_all | solution.py:28
  93.6 1.5 gather_fusion
  95.1 4.6 %all-to-all-start.2 = ((bf16[32,16,768]{2,1,0:T(8,128)(2,1)}), bf16[32,16,768]{2,1,0:T(8,128)(2,1)S(1)}, u32[]{:S(2)}, u32[]{:S(2)}) async-start(bf16[32,16,768]{2,1,0:T(8,128)(2,1)} %bitcast.13), calls=%async_computation.3 | async-start | bytes 1572864 | tf_op jit(solution)/shard_map/all_to_all | solution.py:28
  99.7 0.1 copy.62
  99.8 0.1 reshape.222
  99.9 0.2 select_reduce_fusion
  100.1 0.1 mul.109
  100.2 14.1 %reduce-scatter.5.cloned.1.call-done = bf16[96,1280]{1,0:T(8,128)(2,1)} async-done(((bf16[768,1280]{1,0:T(8,128)(2,1)}), bf16[96,1280]{1,0:T(8,128)(2,1)}) %reduce-scatter.5.cloned.1.call-update) | async-done | bytes 245776 | tf_op jit(solution)/shard_map/reduce_scatter | solution.py:124
  114.3 7.0 %collective-permute-start.2 = (bf16[96,1280]{1,0:T(8,128)(2,1)}, bf16[96,1280]{1,0:T(8,128)(2,1)S(1)}, u32[]{:S(2)}, u32[]{:S(2)}) collective-permute-start(bf16[96,1280]{1,0:T(8,128)(2,1)} %reduce-scatter.5.cloned.1.call-done), channel_id=1, source_target_pairs={{0,1},{1,0},{2,3},{3,2},{4,5},{5,4},{6,7},{7,6},{8,9},{9,8},{10,11... | collective-permute-start | bytes 737288 | tf_op jit(solution)/shard_map/ppermute | solution.py:18
  121.3 0.9 slice.49
  122.3 0.4 collective-permute-done.2
  122.7 0.2 copy.63
  122.8 0.7 reshape.220
  123.6 8.9 %all-to-all-start.3 = ((bf16[32,20,96]{2,1,0:T(8,128)(2,1)}), bf16[32,20,96]{2,1,0:T(8,128)(2,1)S(1)}, u32[]{:S(2)}, u32[]{:S(2)}) async-start(bf16[32,20,96]{2,1,0:T(8,128)(2,1)} %bitcast.17), calls=%async_computation.5 | async-start | bytes 393216 | tf_op jit(solution)/shard_map/all_to_all | solution.py:28
  132.5 0.1 slice_bitcast_fusion.1
  132.6 2.6 %collective-permute-start.1 = (bf16[256,768]{1,0:T(8,128)(2,1)S(1)}, bf16[256,768]{1,0:T(8,128)(2,1)S(1)}, u32[]{:S(2)}, u32[]{:S(2)}) collective-permute-start(bf16[256,768]{1,0:T(8,128)(2,1)S(1)} %get-tuple-element.14), channel_id=1, source_target_pairs={{0,1},{1,0},{2,3},{3,2},{4,5},{5,4},{6,7},{7,6},{8,9},{9,8},{10,11... | collective-permute-start | bytes 1179656 | tf_op jit(solution)/shard_map/ppermute | solution.py:18
  135.1 8.0 %all-to-all-done.3 = bf16[32,20,96]{2,1,0:T(8,128)(2,1)S(1)} async-done(((bf16[32,20,96]{2,1,0:T(8,128)(2,1)}), bf16[32,20,96]{2,1,0:T(8,128)(2,1)S(1)}, u32[]{:S(2)}, u32[]{:S(2)}) %all-to-all-start.3) | async-done | bytes 122912 | tf_op jit(solution)/shard_map/all_to_all | solution.py:28
  143.1 0.2 fusion.17
  143.3 1.4 gather_fusion.1
  144.7 6.0 %all-to-all-start.4 = ((bf16[64,20,96]{2,1,0:T(8,128)(2,1)}), bf16[64,20,96]{2,1,0:T(8,128)(2,1)S(1)}, u32[]{:S(2)}, u32[]{:S(2)}) async-start(bf16[64,20,96]{2,1,0:T(8,128)(2,1)} %gather_fusion.1), calls=%async_computation.6 | async-start | bytes 786432 | tf_op jit(solution)/shard_map/all_to_all | solution.py:22
  150.7 1.0 maximum_select_fusion
  151.7 14.2 %all-to-all-done.4 = bf16[64,20,96]{2,1,0:T(8,128)(2,1)S(1)} async-done(((bf16[64,20,96]{2,1,0:T(8,128)(2,1)}), bf16[64,20,96]{2,1,0:T(8,128)(2,1)S(1)}, u32[]{:S(2)}, u32[]{:S(2)}) %all-to-all-start.4) | async-done | bytes 245792 | tf_op jit(solution)/shard_map/all_to_all | solution.py:22
  165.9 0.1 reshape.221
  166.0 0.9 copy.64
  (35 shorter events, 0.3 us)
Async XLA Ops:
  7.2 10.4 %copy-start = (bf16[1,1,320,2048]{3,2,1,0:T(8,128)(2,1)S(1)}, bf16[1,1,320,2048]{3,2,1,0:T(8,128)(2,1)}, u32[]{:S(2)}) copy-start(bf16[1,1,320,2048]{3,2,1,0:T(8,128)(2,1)} %param.10) | copy-start | bytes 3932164
  7.2 60.7 %reduce-scatter.3.cloned.1.call-start = ((), (), s32[]{:S(2)}) async-start(), calls=%async_computation.7 | async-start | bytes 3538944 | tf_op jit(solution)/shard_map/reduce_scatter | solution.py:79
  7.2 10.3 %collective-permute-start = (bf16[320,384]{1,0:T(8,128)(2,1)}, bf16[320,384]{1,0:T(8,128)(2,1)S(1)}, u32[]{:S(2)}, u32[]{:S(2)}) collective-permute-start(bf16[320,384]{1,0:T(8,128)(2,1)} %bitcast.58), channel_id=1, source_target_pairs={{0,1},{1,0},{2,3},{3,2},{4,5},{5,4},{6,7},{7,6},{8,9},{9,8},{10,11... | collective-permute-start | bytes 737288 | tf_op jit(solution)/shard_map/ppermute | solution.py:18
  21.1 0.7 copy-start.5
  21.1 2.4 %copy-start.6 = (s32[32]{0:T(128)S(1)}, s32[32]{0:T(128)}, u32[]{:S(2)}) copy-start(s32[32]{0:T(128)} %param.18) | copy-start | bytes 388
  21.1 3.1 %copy-start.4 = (bf16[64,2,256]{2,1,0:T(2,128)(2,1)S(1)}, bf16[64,2,256]{2,1,0:T(2,128)(2,1)}, u32[]{:S(2)}) copy-start(bf16[64,2,256]{2,1,0:T(2,128)(2,1)} %param.15) | copy-start | bytes 196612
  25.1 6.1 %copy-start.3 = (bf16[1,1,256,768]{3,2,1,0:T(8,128)(2,1)S(1)}, bf16[1,1,256,768]{3,2,1,0:T(8,128)(2,1)}, u32[]{:S(2)}) copy-start(bf16[1,1,256,768]{3,2,1,0:T(8,128)(2,1)} %param.12) | copy-start | bytes 1179652
  26.1 27.9 %all-to-all-start = ((bf16[64,20,256]{2,1,0:T(8,128)(2,1)}), bf16[64,20,256]{2,1,0:T(8,128)(2,1)S(1)}, u32[]{:S(2)}, u32[]{:S(2)}) async-start(bf16[64,20,256]{2,1,0:T(8,128)(2,1)} %bitcast.4), calls=%async_computation | async-start | bytes 1572864 | tf_op jit(solution)/shard_map/all_to_all | solution.py:22
  31.2 83.1 %reduce-scatter.5.cloned.1.call-start = ((), (), s32[]{:S(2)}) async-start(), calls=%async_computation.8 | async-start | bytes 2211840 | tf_op jit(solution)/shard_map/reduce_scatter | solution.py:124
  54.9 13.0 %copy-start.1 = (f32[1,1,256,768]{2,3,1,0:T(8,128)S(1)}, f32[1,1,256,768]{2,3,1,0:T(8,128)}, u32[]{:S(2)}) copy-start(f32[1,1,256,768]{2,3,1,0:T(8,128)} %copy.60) | copy-start | bytes 2359300
  67.9 1.9 %copy-start.2 = (bf16[1280,256]{1,0:T(8,128)(2,1)S(1)}, bf16[1280,256]{1,0:T(8,128)(2,1)}, u32[]{:S(2)}) copy-start(bf16[1280,256]{1,0:T(8,128)(2,1)} %maximum_select_fusion.1) | copy-start | bytes 1966084
  71.8 10.3 %copy-start.8 = (s32[64]{0:T(128)S(1)}, s32[64]{0:T(128)}, u32[]{:S(2)}) copy-start(s32[64]{0:T(128)} %param.19) | copy-start | bytes 772
  72.7 20.9 %all-to-all-start.1 = ((bf16[32,8,768]{2,1,0:T(8,128)(2,1)}), bf16[32,8,768]{2,1,0:T(8,128)(2,1)S(1)}, u32[]{:S(2)}, u32[]{:S(2)}) async-start(bf16[32,8,768]{2,1,0:T(8,128)(2,1)} %bitcast.11), calls=%async_computation.2 | async-start | bytes 786432 | tf_op jit(solution)/shard_map/all_to_all | solution.py:28
  82.7 17.1 %copy-start.7 = (bf16[64,8]{0,1:T(8,128)(2,1)S(1)}, bf16[64,8]{0,1:T(8,128)(2,1)}, u32[]{:S(2)}) copy-start(bf16[64,8]{0,1:T(8,128)(2,1)} %param.17) | copy-start | bytes 3076
  95.1 28.5 %all-to-all-start.2 = ((bf16[32,16,768]{2,1,0:T(8,128)(2,1)}), bf16[32,16,768]{2,1,0:T(8,128)(2,1)S(1)}, u32[]{:S(2)}, u32[]{:S(2)}) async-start(bf16[32,16,768]{2,1,0:T(8,128)(2,1)} %bitcast.13), calls=%async_computation.3 | async-start | bytes 1572864 | tf_op jit(solution)/shard_map/all_to_all | solution.py:28
  114.3 8.3 %collective-permute-start.2 = (bf16[96,1280]{1,0:T(8,128)(2,1)}, bf16[96,1280]{1,0:T(8,128)(2,1)S(1)}, u32[]{:S(2)}, u32[]{:S(2)}) collective-permute-start(bf16[96,1280]{1,0:T(8,128)(2,1)} %reduce-scatter.5.cloned.1.call-done), channel_id=1, source_target_pairs={{0,1},{1,0},{2,3},{3,2},{4,5},{5,4},{6,7},{7,6},{8,9},{9,8},{10,11... | collective-permute-start | bytes 737288 | tf_op jit(solution)/shard_map/ppermute | solution.py:18
  123.6 19.5 %all-to-all-start.3 = ((bf16[32,20,96]{2,1,0:T(8,128)(2,1)}), bf16[32,20,96]{2,1,0:T(8,128)(2,1)S(1)}, u32[]{:S(2)}, u32[]{:S(2)}) async-start(bf16[32,20,96]{2,1,0:T(8,128)(2,1)} %bitcast.17), calls=%async_computation.5 | async-start | bytes 393216 | tf_op jit(solution)/shard_map/all_to_all | solution.py:28
  132.6 18.1 %collective-permute-start.1 = (bf16[256,768]{1,0:T(8,128)(2,1)S(1)}, bf16[256,768]{1,0:T(8,128)(2,1)S(1)}, u32[]{:S(2)}, u32[]{:S(2)}) collective-permute-start(bf16[256,768]{1,0:T(8,128)(2,1)S(1)} %get-tuple-element.14), channel_id=1, source_target_pairs={{0,1},{1,0},{2,3},{3,2},{4,5},{5,4},{6,7},{7,6},{8,9},{9,8},{10,11... | collective-permute-start | bytes 1179656 | tf_op jit(solution)/shard_map/ppermute | solution.py:18
  144.7 21.2 %all-to-all-start.4 = ((bf16[64,20,96]{2,1,0:T(8,128)(2,1)}), bf16[64,20,96]{2,1,0:T(8,128)(2,1)S(1)}, u32[]{:S(2)}, u32[]{:S(2)}) async-start(bf16[64,20,96]{2,1,0:T(8,128)(2,1)} %gather_fusion.1), calls=%async_computation.6 | async-start | bytes 786432 | tf_op jit(solution)/shard_map/all_to_all | solution.py:22
Sparse Core Ops, SparseCore 0:
  21.3 46.5 reduce-scatter.2
  71.9 42.3 reduce-scatter.4

commit v10 on v9

--- a/solution.py
+++ b/solution.py
@@ -109,11 +109,15 @@
 
     weight_local, recv_tokens = lax.optimization_barrier((weight[0, 0], recv_tokens))
     gradient = summed.astype(jnp.float32)
-    first = beta_one * moment_one[0, 0] + (1.0 - beta_one) * gradient
-    second = beta_two * moment_two[0, 0] + (1.0 - beta_two) * gradient * gradient
+    step = learn_rate / bias_one
+    step_first = (step * beta_one) * moment_one[0, 0] + (step * (1.0 - beta_one)) * gradient
+    second = (beta_two / bias_two) * moment_two[0, 0] + (
+        (1.0 - beta_two) / bias_two
+    ) * gradient * gradient
     weight_now = weight_local.astype(jnp.float32)
-    update = first / bias_one / (jnp.sqrt(second / bias_two) + adam_eps)
-    new_weight = (weight_now - learn_rate * (update + decay_rate * weight_now)).astype(jnp.bfloat16)
+    new_weight = (
+        (1.0 - learn_rate * decay_rate) * weight_now - step_first / (jnp.sqrt(second) + adam_eps)
+    ).astype(jnp.bfloat16)
 
     terms = (
         lax.dot_general(

time: 175 us -> 174 us (level)
  no operation moved by 1% of the time
where the time goes in v10:
time: 174 us
  waiting for transfers between devices  73.8 us (42%)
  starting transfers between devices  52.4 us (30%)
  local copies, waits for them, and re-layouts  18.2 us (10%)
  between operations  14.4 us (8%)
  other arithmetic  8.57 us (5%)
  matrix products  6.09 us (4%)
    all_to_all x2, waiting for transfers between devices, exchanged(): return lax.all_to_all(x, 'ep', split_axis=0, concat_axis=0, tiled=True)  32.2 us
    all_to_all x3, starting transfers between devices, exchanged_chips(): lax.all_to_all(x, 'ep', split_axis=0, concat_axis=0, tiled=True, axis_ind...  22.9 us
    all_to_all x3, waiting for transfers between devices, exchanged_chips(): lax.all_to_all(x, 'ep', split_axis=0, concat_axis=0, tiled=True, axis_ind...  18.9 us
    ppermute x3, starting transfers between devices, swapped(): lax.ppermute(x, 'ep', [(i, i ^ 1) for i in range(lax.axis_size('ep'))])  18.3 us
    reduce_scatter x1, waiting for transfers between devices, body(): half_share = lax.psum_scatter(terms, 'rep', scatter_dimension=0, tiled=True)  14.2 us
    all_to_all x2, starting transfers between devices, exchanged(): return lax.all_to_all(x, 'ep', split_axis=0, concat_axis=0, tiled=True)  11.1 us
    reduce_scatter x1, waiting for transfers between devices, body(): lax.psum_scatter((product * width_scale).astype(jnp.bfloat16), 'rep', sca...  7.96 us
    unnamed x23, local copies, waits for them, and re-layouts  6.28 us
  transfers between devices with their start and end apart: 10, of which 8 were waited for; matrix products, arithmetic and copies ran while one was open for 14% of the time, Pallas kernels for 0%

profile of v10, /device:TPU:1, one launch (start us, length us, event | category | flops | bytes accessed | tf_op | source)
XLA Modules:
  0.0 173.5 jit_solution(3533883346966551960)
XLA Ops:
  7.2 8.9 %collective-permute-start = (bf16[320,384]{1,0:T(8,128)(2,1)}, bf16[320,384]{1,0:T(8,128)(2,1)S(1)}, u32[]{:S(2)}, u32[]{:S(2)}) collective-permute-start(bf16[320,384]{1,0:T(8,128)(2,1)} %bitcast.62), channel_id=1, source_target_pairs={{0,1},{1,0},{2,3},{3,2},{4,5},{5,4},{6,7},{7,6},{8,9},{9,8},{10,11... | collective-permute-start | bytes 737288 | tf_op jit(solution)/shard_map/ppermute | solution.py:18
  16.2 1.1 pad_maximum_fusion.1
  17.3 0.2 collective-permute-done
  17.5 0.1 maximum_select_fusion.2
  17.6 3.5 %fusion.1 = bf16[2048,768]{0,1:T(8,128)(2,1)} fusion(bf16[320,768]{1,0:T(8,128)(2,1)S(1)} %maximum_select_fusion.2, bf16[1,1,320,2048]{3,2,1,0:T(8,128)(2,1)S(1)} %copy-done), kind=kOutput, calls=%fused_computation.5 | convolution fusion | flops 1009778688 | bytes 4947968 | tf_op jit(solution)/shard_map/dot_general | solution.py:76
  21.2 0.7 copy-done.5
  21.8 0.1 copy.49
  21.9 0.1 eq.91
  22.0 0.1 eq.95
  22.1 1.2 reduce-window.6
  23.3 0.2 slice_reduce_fusion
  23.5 0.1 select_reduce_fusion.1
  23.7 0.1 add.73
  23.7 0.4 convert_reduce_fusion
  24.2 0.1 fusion.25
  24.3 0.3 convolution_convert_fusion
  24.6 0.1 stack_reshape.9
  24.7 0.3 convolution_convert_fusion.1
  25.0 0.1 stack_reshape.8
  25.0 0.1 pad_maximum_fusion
  25.1 0.9 copy.65
  26.1 5.1 %all-to-all-start = ((bf16[64,20,256]{2,1,0:T(8,128)(2,1)}), bf16[64,20,256]{2,1,0:T(8,128)(2,1)S(1)}, u32[]{:S(2)}, u32[]{:S(2)}) async-start(bf16[64,20,256]{2,1,0:T(8,128)(2,1)} %bitcast.4), calls=%async_computation | async-start | bytes 1572864 | tf_op jit(solution)/shard_map/all_to_all | solution.py:22
  31.3 1.4 copy.60
  32.7 2.3 %copy.59 = f32[1,1,256,768]{2,3,1,0:T(8,128)} copy(f32[1,1,256,768]{3,2,1,0:T(8,128)} %param.13) | data formatting | bytes 1572864 | tf_op args[3]
  35.0 0.9 copy.48
  35.9 18.0 %all-to-all-done = bf16[64,20,256]{2,1,0:T(8,128)(2,1)S(1)} async-done(((bf16[64,20,256]{2,1,0:T(8,128)(2,1)}), bf16[64,20,256]{2,1,0:T(8,128)(2,1)S(1)}, u32[]{:S(2)}, u32[]{:S(2)}) %all-to-all-start) | async-done | bytes 655392 | tf_op jit(solution)/shard_map/all_to_all | solution.py:22
  53.9 0.9 fusion.24
  54.9 1.1 reshape_squeeze.7
  56.0 1.8 %reshape_squeeze.6 = bf16[640,256]{1,0:T(8,128)(2,1)} reshape(bf16[32,1,20,256]{3,2,1,0:T(8,128)(2,1)} %get-tuple-element.16) | data formatting | bytes 655360 | tf_op jit(solution)/shard_map/reshape;squeeze | solution.py:103
  57.8 2.1 %maximum_select_fusion.1 = bf16[1280,256]{1,0:T(8,128)(2,1)} fusion(bf16[640,256]{1,0:T(8,128)(2,1)S(1)} %reshape_squeeze.7, bf16[640,256]{1,0:T(8,128)(2,1)} %reshape_squeeze.6, pred[]{:T(512)S(6)} %eq.89), kind=kLoop, calls=%fused_computation.24 | loop fusion | flops 2949120 | bytes 1310721 | tf_op jit(solution)/shard_map/jit(_where)/select_n | solution.py:104
  59.9 8.0 %reduce-scatter.3.cloned.1.call-done = bf16[256,768]{0,1:T(8,128)(2,1)} async-done(((bf16[2048,768]{0,1:T(8,128)(2,1)}), bf16[256,768]{0,1:T(8,128)(2,1)}) %reduce-scatter.3.cloned.1.call-update) | async-done | bytes 393232 | tf_op jit(solution)/shard_map/reduce_scatter | solution.py:79
  67.9 1.7 fusion.9
  69.6 2.0 %fusion = bf16[768,1280]{1,0:T(8,128)(2,1)} fusion(bf16[256,768]{0,1:T(8,128)(2,1)S(1)} %fusion.9, bf16[1280,256]{1,0:T(8,128)(2,1)S(1)} %copy-done.2), kind=kOutput, calls=%fused_computation.4 | convolution fusion | flops 505282560 | bytes 3014656 | tf_op jit(solution)/shard_map/dot_general | solution.py:123
  71.6 0.9 copy.61
  72.6 9.4 %all-to-all-start.1 = ((bf16[32,8,768]{2,1,0:T(8,128)(2,1)}), bf16[32,8,768]{2,1,0:T(8,128)(2,1)S(1)}, u32[]{:S(2)}, u32[]{:S(2)}) async-start(bf16[32,8,768]{2,1,0:T(8,128)(2,1)} %bitcast.11), calls=%async_computation.2 | async-start | bytes 786432 | tf_op jit(solution)/shard_map/all_to_all | solution.py:28
  81.9 0.1 select_reduce_fusion.2
  82.1 0.1 convert_reduce_fusion.1
  82.2 0.1 reshape.216
  82.3 0.1 rev.3
  82.3 0.1 reshape.217
  82.5 10.9 %all-to-all-done.1 = bf16[32,8,768]{2,1,0:T(8,128)(2,1)S(1)} async-done(((bf16[32,8,768]{2,1,0:T(8,128)(2,1)}), bf16[32,8,768]{2,1,0:T(8,128)(2,1)S(1)}, u32[]{:S(2)}, u32[]{:S(2)}) %all-to-all-start.1) | async-done | bytes 393248 | tf_op jit(solution)/shard_map/all_to_all | solution.py:28
  93.4 1.5 gather_fusion
  94.9 4.6 %all-to-all-start.2 = ((bf16[32,16,768]{2,1,0:T(8,128)(2,1)}), bf16[32,16,768]{2,1,0:T(8,128)(2,1)S(1)}, u32[]{:S(2)}, u32[]{:S(2)}) async-start(bf16[32,16,768]{2,1,0:T(8,128)(2,1)} %bitcast.13), calls=%async_computation.3 | async-start | bytes 1572864 | tf_op jit(solution)/shard_map/all_to_all | solution.py:28
  99.5 0.1 copy.62
  99.6 0.1 reshape.222
  99.7 0.2 select_reduce_fusion
  99.9 0.1 mul.109
  100.0 14.2 %reduce-scatter.5.cloned.1.call-done = bf16[96,1280]{1,0:T(8,128)(2,1)} async-done(((bf16[768,1280]{1,0:T(8,128)(2,1)}), bf16[96,1280]{1,0:T(8,128)(2,1)}) %reduce-scatter.5.cloned.1.call-update) | async-done | bytes 245776 | tf_op jit(solution)/shard_map/reduce_scatter | solution.py:128
  114.2 6.8 %collective-permute-start.2 = (bf16[96,1280]{1,0:T(8,128)(2,1)}, bf16[96,1280]{1,0:T(8,128)(2,1)S(1)}, u32[]{:S(2)}, u32[]{:S(2)}) collective-permute-start(bf16[96,1280]{1,0:T(8,128)(2,1)} %reduce-scatter.5.cloned.1.call-done), channel_id=1, source_target_pairs={{0,1},{1,0},{2,3},{3,2},{4,5},{5,4},{6,7},{7,6},{8,9},{9,8},{10,11... | collective-permute-start | bytes 737288 | tf_op jit(solution)/shard_map/ppermute | solution.py:18
  121.1 0.9 slice.49
  122.0 0.4 collective-permute-done.2
  122.4 0.2 copy.63
  122.6 0.7 reshape.220
  123.3 9.0 %all-to-all-start.3 = ((bf16[32,20,96]{2,1,0:T(8,128)(2,1)}), bf16[32,20,96]{2,1,0:T(8,128)(2,1)S(1)}, u32[]{:S(2)}, u32[]{:S(2)}) async-start(bf16[32,20,96]{2,1,0:T(8,128)(2,1)} %bitcast.17), calls=%async_computation.5 | async-start | bytes 393216 | tf_op jit(solution)/shard_map/all_to_all | solution.py:28
  132.3 0.1 slice_bitcast_fusion.1
  132.4 2.6 %collective-permute-start.1 = (bf16[256,768]{1,0:T(8,128)(2,1)S(1)}, bf16[256,768]{1,0:T(8,128)(2,1)S(1)}, u32[]{:S(2)}, u32[]{:S(2)}) collective-permute-start(bf16[256,768]{1,0:T(8,128)(2,1)S(1)} %get-tuple-element.14), channel_id=1, source_target_pairs={{0,1},{1,0},{2,3},{3,2},{4,5},{5,4},{6,7},{7,6},{8,9},{9,8},{10,11... | collective-permute-start | bytes 1179656 | tf_op jit(solution)/shard_map/ppermute | solution.py:18
  134.9 8.0 %all-to-all-done.3 = bf16[32,20,96]{2,1,0:T(8,128)(2,1)S(1)} async-done(((bf16[32,20,96]{2,1,0:T(8,128)(2,1)}), bf16[32,20,96]{2,1,0:T(8,128)(2,1)S(1)}, u32[]{:S(2)}, u32[]{:S(2)}) %all-to-all-start.3) | async-done | bytes 122912 | tf_op jit(solution)/shard_map/all_to_all | solution.py:28
  142.9 0.2 fusion.14
  143.1 1.4 gather_fusion.1
  144.5 6.0 %all-to-all-start.4 = ((bf16[64,20,96]{2,1,0:T(8,128)(2,1)}), bf16[64,20,96]{2,1,0:T(8,128)(2,1)S(1)}, u32[]{:S(2)}, u32[]{:S(2)}) async-start(bf16[64,20,96]{2,1,0:T(8,128)(2,1)} %gather_fusion.1), calls=%async_computation.6 | async-start | bytes 786432 | tf_op jit(solution)/shard_map/all_to_all | solution.py:22
  150.5 1.0 maximum_select_fusion
  151.5 14.2 %all-to-all-done.4 = bf16[64,20,96]{2,1,0:T(8,128)(2,1)S(1)} async-done(((bf16[64,20,96]{2,1,0:T(8,128)(2,1)}), bf16[64,20,96]{2,1,0:T(8,128)(2,1)S(1)}, u32[]{:S(2)}, u32[]{:S(2)}) %all-to-all-start.4) | async-done | bytes 245792 | tf_op jit(solution)/shard_map/all_to_all | solution.py:22
  165.7 0.1 reshape.221
  165.8 0.9 copy.64
  (35 shorter events, 0.3 us)
Async XLA Ops:
  7.2 10.4 %copy-start = (bf16[1,1,320,2048]{3,2,1,0:T(8,128)(2,1)S(1)}, bf16[1,1,320,2048]{3,2,1,0:T(8,128)(2,1)}, u32[]{:S(2)}) copy-start(bf16[1,1,320,2048]{3,2,1,0:T(8,128)(2,1)} %param.10) | copy-start | bytes 3932164
  7.2 60.7 %reduce-scatter.3.cloned.1.call-start = ((), (), s32[]{:S(2)}) async-start(), calls=%async_computation.7 | async-start | bytes 3538944 | tf_op jit(solution)/shard_map/reduce_scatter | solution.py:79
  7.2 10.3 %collective-permute-start = (bf16[320,384]{1,0:T(8,128)(2,1)}, bf16[320,384]{1,0:T(8,128)(2,1)S(1)}, u32[]{:S(2)}, u32[]{:S(2)}) collective-permute-start(bf16[320,384]{1,0:T(8,128)(2,1)} %bitcast.62), channel_id=1, source_target_pairs={{0,1},{1,0},{2,3},{3,2},{4,5},{5,4},{6,7},{7,6},{8,9},{9,8},{10,11... | collective-permute-start | bytes 737288 | tf_op jit(solution)/shard_map/ppermute | solution.py:18
  21.1 0.7 copy-start.5
  21.1 2.4 %copy-start.6 = (s32[32]{0:T(128)S(1)}, s32[32]{0:T(128)}, u32[]{:S(2)}) copy-start(s32[32]{0:T(128)} %param.18) | copy-start | bytes 388
  21.1 3.1 %copy-start.4 = (bf16[64,2,256]{2,1,0:T(2,128)(2,1)S(1)}, bf16[64,2,256]{2,1,0:T(2,128)(2,1)}, u32[]{:S(2)}) copy-start(bf16[64,2,256]{2,1,0:T(2,128)(2,1)} %param.15) | copy-start | bytes 196612
  26.1 27.9 %all-to-all-start = ((bf16[64,20,256]{2,1,0:T(8,128)(2,1)}), bf16[64,20,256]{2,1,0:T(8,128)(2,1)S(1)}, u32[]{:S(2)}, u32[]{:S(2)}) async-start(bf16[64,20,256]{2,1,0:T(8,128)(2,1)} %bitcast.4), calls=%async_computation | async-start | bytes 1572864 | tf_op jit(solution)/shard_map/all_to_all | solution.py:22
  31.2 3.8 %copy-start.3 = (bf16[1,1,256,768]{3,2,1,0:T(8,128)(2,1)S(1)}, bf16[1,1,256,768]{3,2,1,0:T(8,128)(2,1)}, u32[]{:S(2)}) copy-start(bf16[1,1,256,768]{3,2,1,0:T(8,128)(2,1)} %param.12) | copy-start | bytes 1179652
  31.2 83.0 %reduce-scatter.5.cloned.1.call-start = ((), (), s32[]{:S(2)}) async-start(), calls=%async_computation.8 | async-start | bytes 2211840 | tf_op jit(solution)/shard_map/reduce_scatter | solution.py:128
  54.9 13.0 %copy-start.1 = (f32[1,1,256,768]{2,3,1,0:T(8,128)S(1)}, f32[1,1,256,768]{2,3,1,0:T(8,128)}, u32[]{:S(2)}) copy-start(f32[1,1,256,768]{2,3,1,0:T(8,128)} %copy.59) | copy-start | bytes 2359300
  67.9 1.7 %copy-start.2 = (bf16[1280,256]{1,0:T(8,128)(2,1)S(1)}, bf16[1280,256]{1,0:T(8,128)(2,1)}, u32[]{:S(2)}) copy-start(bf16[1280,256]{1,0:T(8,128)(2,1)} %maximum_select_fusion.1) | copy-start | bytes 1966084
  71.6 10.3 %copy-start.8 = (s32[64]{0:T(128)S(1)}, s32[64]{0:T(128)}, u32[]{:S(2)}) copy-start(s32[64]{0:T(128)} %param.19) | copy-start | bytes 772
  72.6 20.8 %all-to-all-start.1 = ((bf16[32,8,768]{2,1,0:T(8,128)(2,1)}), bf16[32,8,768]{2,1,0:T(8,128)(2,1)S(1)}, u32[]{:S(2)}, u32[]{:S(2)}) async-start(bf16[32,8,768]{2,1,0:T(8,128)(2,1)} %bitcast.11), calls=%async_computation.2 | async-start | bytes 786432 | tf_op jit(solution)/shard_map/all_to_all | solution.py:28
  82.5 17.0 %copy-start.7 = (bf16[64,8]{0,1:T(8,128)(2,1)S(1)}, bf16[64,8]{0,1:T(8,128)(2,1)}, u32[]{:S(2)}) copy-start(bf16[64,8]{0,1:T(8,128)(2,1)} %param.17) | copy-start | bytes 3076
  94.9 28.5 %all-to-all-start.2 = ((bf16[32,16,768]{2,1,0:T(8,128)(2,1)}), bf16[32,16,768]{2,1,0:T(8,128)(2,1)S(1)}, u32[]{:S(2)}, u32[]{:S(2)}) async-start(bf16[32,16,768]{2,1,0:T(8,128)(2,1)} %bitcast.13), calls=%async_computation.3 | async-start | bytes 1572864 | tf_op jit(solution)/shard_map/all_to_all | solution.py:28
  114.2 8.1 %collective-permute-start.2 = (bf16[96,1280]{1,0:T(8,128)(2,1)}, bf16[96,1280]{1,0:T(8,128)(2,1)S(1)}, u32[]{:S(2)}, u32[]{:S(2)}) collective-permute-start(bf16[96,1280]{1,0:T(8,128)(2,1)} %reduce-scatter.5.cloned.1.call-done), channel_id=1, source_target_pairs={{0,1},{1,0},{2,3},{3,2},{4,5},{5,4},{6,7},{7,6},{8,9},{9,8},{10,11... | collective-permute-start | bytes 737288 | tf_op jit(solution)/shard_map/ppermute | solution.py:18
  123.3 19.6 %all-to-all-start.3 = ((bf16[32,20,96]{2,1,0:T(8,128)(2,1)}), bf16[32,20,96]{2,1,0:T(8,128)(2,1)S(1)}, u32[]{:S(2)}, u32[]{:S(2)}) async-start(bf16[32,20,96]{2,1,0:T(8,128)(2,1)} %bitcast.17), calls=%async_computation.5 | async-start | bytes 393216 | tf_op jit(solution)/shard_map/all_to_all | solution.py:28
  132.4 18.1 %collective-permute-start.1 = (bf16[256,768]{1,0:T(8,128)(2,1)S(1)}, bf16[256,768]{1,0:T(8,128)(2,1)S(1)}, u32[]{:S(2)}, u32[]{:S(2)}) collective-permute-start(bf16[256,768]{1,0:T(8,128)(2,1)S(1)} %get-tuple-element.14), channel_id=1, source_target_pairs={{0,1},{1,0},{2,3},{3,2},{4,5},{5,4},{6,7},{7,6},{8,9},{9,8},{10,11... | collective-permute-start | bytes 1179656 | tf_op jit(solution)/shard_map/ppermute | solution.py:18
  144.5 21.2 %all-to-all-start.4 = ((bf16[64,20,96]{2,1,0:T(8,128)(2,1)}), bf16[64,20,96]{2,1,0:T(8,128)(2,1)S(1)}, u32[]{:S(2)}, u32[]{:S(2)}) async-start(bf16[64,20,96]{2,1,0:T(8,128)(2,1)} %gather_fusion.1), calls=%async_computation.6 | async-start | bytes 786432 | tf_op jit(solution)/shard_map/all_to_all | solution.py:22
Sparse Core Ops, SparseCore 0:
  21.3 46.5 reduce-scatter.2
  71.8 42.4 reduce-scatter.4
